TPU v7x, 32 devices: a whole 2x2x4 slice. The times are simulated.
32 devices in a mesh: dp: 2 (over y), ulysses: 4 (over x, core), blk: 4 (over z).
Axes of the slice: x: 2, y: 2, z: 4, core: 2. Of those that a mesh axis runs over, the one named last changes fastest.
Arguments:
- hidden_in: bfloat16 [2, 2048, 4096], P('dp', ('blk', 'ulysses')), may hold values from -6 to 6
- queries: bfloat16 [2, 2048, 2048], P('dp', ('blk', 'ulysses')), may hold values from -240 to 240
- pair_weight: bfloat16 [4096, 2048], P(('dp', 'blk')), may hold values from -0.09375 to 0.09375
- span_order: int32 [2, 8], P('dp'), may hold values from 0 to 7, each once within a row
- yarn_divisor: int32 [64], replicated, may hold values from 1 to 8
Outputs:
- attended: bfloat16 [2, 2048, 2048], P('dp', ('blk', 'ulysses'))
All inputs are finite; a program needn't handle non-finite values.
Results may differ from a plain program's by a relative error of at most 0.02.
The roundings to bfloat16 on the way count: a program that leaves them out, or rounds other values in their place, can miss the bound.
Values may be sent and summed in bfloat16 or wider, within the bound.
No kernel may reach another device: no remote copies, remote signals or barrier semaphores. Data moves between devices by JAX's collectives and lax.ppermute only.
A program may use at most 128 MiB of HBM per device.

v0:
```python
import math

import jax
import jax.numpy as jnp
from jax import lax
from jax.sharding import PartitionSpec as P

KVH = 8
HD = 128
QH = 16
STEPS = 3


LOG_BASE = math.log(500000.0)


def from_behind(block, axis, distance):
    devices = range(lax.axis_size(axis))
    route = [((i - distance) % len(devices), i) for i in devices]
    return lax.ppermute(block, axis, route)


def rotate(vectors, angle_table):
    half_dim = vectors.shape[-1] // 2
    first_half = vectors[..., :half_dim]
    second_half = vectors[..., half_dim:]
    cosine = jnp.cos(angle_table)
    sine_part = jnp.sin(angle_table)
    return jnp.concatenate(
        [
            first_half * cosine - second_half * sine_part,
            second_half * cosine + first_half * sine_part,
        ],
        axis=-1,
    )


def angles(positions, yarn_divisor):
    half_dim = yarn_divisor.shape[0]
    scaled = 2.0 * jnp.arange(half_dim, dtype=jnp.float32) / (2 * half_dim)
    inverse = jnp.exp(-LOG_BASE * scaled) / yarn_divisor.astype(jnp.float32)
    return positions.astype(jnp.float32)[:, None] * inverse[None, :]


def positions_of(order_row, first_row, row_count, span_rows):
    stored = first_row + jnp.arange(row_count, dtype=jnp.int32)
    span_index = stored // span_rows
    matches = span_index[:, None] == jnp.arange(order_row.shape[0], dtype=jnp.int32)[None, :]
    span_value = jnp.sum(jnp.where(matches, order_row[None, :], 0), axis=1)
    return span_value * span_rows + stored % span_rows


def tile_scores(query_rows, key_rows):
    product = lax.dot_general(
        query_rows, key_rows, (((1,), (1,)), ((), ())), preferred_element_type=jnp.float32
    )
    return product * (1.0 / math.sqrt(HD))


def row_maximum(query_rows, query_pos, key_rows, key_pos):
    score = tile_scores(query_rows, key_rows)
    return jnp.max(jnp.where(key_pos[None, :] <= query_pos[:, None], score, -jnp.inf), axis=1)


def add_tile(denominator, numerator, query_rows, query_pos, key_rows, value_rows, key_pos, row_top):
    score = tile_scores(query_rows, key_rows)
    allowed = key_pos[None, :] <= query_pos[:, None]
    weights = jnp.where(allowed, jnp.exp(score - row_top[:, None]), 0.0)
    denominator = denominator + jnp.sum(weights, axis=1)
    numerator = numerator + jnp.dot(
        weights.astype(jnp.bfloat16), value_rows, preferred_element_type=jnp.float32
    )
    return (denominator, numerator)


def shards(hidden_in, queries, pair_weight, span_order, yarn_divisor):
    inputs_local = hidden_in[0]
    queries_local = queries[0]
    order_row = span_order[0]
    token_rows = inputs_local.shape[0]
    ulysses_size = lax.axis_size("ulysses")
    cycle_size = lax.axis_size("blk")
    ulysses_index = lax.axis_index("ulysses")
    cycle_index = lax.axis_index("blk")
    block_rows = token_rows * ulysses_size
    span_rows = block_rows // 2
    kv_width = KVH * HD
    kv_local = KVH // ulysses_size
    group_size = QH // KVH
    own_positions = positions_of(
        order_row, cycle_index * block_rows + ulysses_index * token_rows, token_rows, span_rows
    )
    own_angles = angles(own_positions, yarn_divisor)
    block_positions = positions_of(order_row, cycle_index * block_rows, block_rows, span_rows)
    rotated_queries = rotate(
        queries_local.astype(jnp.float32).reshape(token_rows, QH, HD), own_angles[:, None, :]
    )
    rotated_queries = rotated_queries.astype(jnp.bfloat16).reshape(token_rows, QH * HD)
    projected = jnp.dot(
        inputs_local,
        lax.all_gather(pair_weight, ("dp", "blk"), axis=0, tiled=True),
        preferred_element_type=jnp.float32,
    )
    token_keys = rotate(
        projected[:, :kv_width].reshape(token_rows, KVH, HD), own_angles[:, None, :]
    )
    token_keys = token_keys.astype(jnp.bfloat16).reshape(token_rows, kv_width)
    token_values = projected[:, kv_width:].astype(jnp.bfloat16)
    query_block, key_block, value_block = (
        lax.all_to_all(rotated_queries, "ulysses", split_axis=1, concat_axis=0, tiled=True),
        lax.all_to_all(token_keys, "ulysses", split_axis=1, concat_axis=0, tiled=True),
        lax.all_to_all(token_values, "ulysses", split_axis=1, concat_axis=0, tiled=True),
    )
    own_pair = jnp.stack([key_block, value_block])
    carried_blocks = [own_pair]
    current_pair = own_pair
    for step_index in range(STEPS):
        current_pair = from_behind(current_pair, "blk", 1)
        carried_blocks.append(current_pair)
    carried_positions = []
    for step_index in range(STEPS + 1):
        source_block = jnp.remainder(cycle_index - step_index, cycle_size)
        carried_positions.append(
            positions_of(order_row, source_block * block_rows, block_rows, span_rows)
        )
    output_rows = []
    for query_half in range(2):
        row_start = query_half * span_rows
        half_positions = block_positions[row_start : row_start + span_rows]
        query_pos = jnp.tile(half_positions, group_size)
        head_outputs = []
        for local_head in range(kv_local):
            query_part = query_block[
                row_start : row_start + span_rows,
                local_head * group_size * HD : (local_head + 1) * group_size * HD,
            ]
            query_rows = (
                query_part.reshape(span_rows, group_size, HD)
                .transpose(1, 0, 2)
                .reshape(group_size * span_rows, HD)
            )
            tile_list = []
            for step_index in range(STEPS + 1):
                pair_block = carried_blocks[step_index]
                for key_half in range(2):
                    key_start = key_half * span_rows
                    key_rows = pair_block[
                        0,
                        key_start : key_start + span_rows,
                        local_head * HD : (local_head + 1) * HD,
                    ]
                    value_rows = pair_block[
                        1,
                        key_start : key_start + span_rows,
                        local_head * HD : (local_head + 1) * HD,
                    ]
                    key_pos = carried_positions[step_index][key_start : key_start + span_rows]
                    tile_list.append((key_rows, value_rows, key_pos))
            row_top = jnp.full((group_size * span_rows,), -jnp.inf, jnp.float32)
            for key_rows, value_rows, key_pos in tile_list:
                tile_top = row_maximum(query_rows, query_pos, key_rows, key_pos)
                row_top = jnp.maximum(row_top, tile_top)
            denominator = jnp.zeros((group_size * span_rows,), jnp.float32)
            numerator = jnp.zeros((group_size * span_rows, HD), jnp.float32)
            for key_rows, value_rows, key_pos in tile_list:
                denominator, numerator = add_tile(
                    denominator,
                    numerator,
                    query_rows,
                    query_pos,
                    key_rows,
                    value_rows,
                    key_pos,
                    row_top,
                )
            normalized = (numerator / denominator[:, None]).astype(jnp.bfloat16)
            normalized = (
                normalized.reshape(group_size, span_rows, HD)
                .transpose(1, 0, 2)
                .reshape(span_rows, group_size * HD)
            )
            head_outputs.append(normalized)
        output_rows.append(jnp.concatenate(head_outputs, axis=1))
    block_output = jnp.concatenate(output_rows, axis=0)
    token_output = lax.all_to_all(block_output, "ulysses", split_axis=0, concat_axis=1, tiled=True)
    return token_output[None]


def solution(mesh):
    return jax.shard_map(
        shards,
        mesh=mesh,
        in_specs=(
            P("dp", ("blk", "ulysses"), None),
            P("dp", ("blk", "ulysses"), None),
            P(("dp", "blk"), None),
            P("dp", None),
            P(),
        ),
        out_specs=P("dp", ("blk", "ulysses"), None),
        check_vma=False,
    )
```

profile of v0, /device:TPU:0, one launch (start us, length us, event | category | flops | bytes accessed | tf_op | source)
XLA Modules:
  0.0 399.9 jit_solution(2221440257208466754)
XLA Ops:
  11.2 4.2 %all-to-all-start = ((bf16[128,4,512]{0,2,1:T(8,128)(2,1)}), bf16[128,4,512]{0,2,1:T(8,128)(2,1)S(1)}, u32[]{:S(2)}, u32[]{:S(2)}) async-start(bf16[128,4,512]{0,2,1:T(8,128)(2,1)} %bitcast.2), calls=%async_computation | async-start | bytes 1048576 | tf_op jit(solution)/shard_map/all_to_all | solution.py:110
  18.7 5.6 %all-to-all-done = bf16[128,4,512]{0,2,1:T(8,128)(2,1)S(1)} async-done(((bf16[128,4,512]{0,2,1:T(8,128)(2,1)}), bf16[128,4,512]{0,2,1:T(8,128)(2,1)S(1)}, u32[]{:S(2)}, u32[]{:S(2)}) %all-to-all-start) | async-done | bytes 524320 | tf_op jit(solution)/shard_map/all_to_all | solution.py:110
  25.2 214.7 %all-gather.2.cloned.1.call-done = bf16[4096,2048]{1,0:T(8,128)(2,1)} async-done(((bf16[512,2048]{1,0:T(8,128)(2,1)}), bf16[4096,2048]{1,0:T(8,128)(2,1)}) %all-gather.2.cloned.1.call-update) | async-done | bytes 16777232 | tf_op jit(solution)/shard_map/all_gather | solution.py:101
  239.8 8.1 %fusion.20 = f32[128,2048]{1,0:T(8,128)S(1)} fusion(bf16[4096,2048]{1,0:T(8,128)(2,1)} %all-gather.2.cloned.1.call-done, bf16[1,128,4096]{2,1,0:T(8,128)(2,1)S(1)} %copy-done), kind=kOutput, calls=%fused_computation.68 | convolution fusion | flops 2147483648 | bytes 18874368 | tf_op jit(solution)/shard_map/dot_general | solution.py:99
  249.0 3.4 all-to-all-start.1
  253.2 5.2 %all-to-all-done.1 = bf16[128,4,256]{0,2,1:T(8,128)(2,1)S(1)} async-done(((bf16[128,4,256]{0,2,1:T(8,128)(2,1)}), bf16[128,4,256]{0,2,1:T(8,128)(2,1)S(1)}, u32[]{:S(2)}, u32[]{:S(2)}) %all-to-all-start.1) | async-done | bytes 262176 | tf_op jit(solution)/shard_map/all_to_all | solution.py:111
  258.4 3.4 all-to-all-start.2
  263.0 4.8 %all-to-all-done.2 = bf16[128,4,256]{2,0,1:T(8,128)(2,1)S(1)} async-done(((bf16[128,4,256]{2,0,1:T(8,128)(2,1)}), bf16[128,4,256]{2,0,1:T(8,128)(2,1)S(1)}, u32[]{:S(2)}, u32[]{:S(2)}) %all-to-all-start.2) | async-done | bytes 262176 | tf_op jit(solution)/shard_map/all_to_all | solution.py:112
  268.9 14.3 %collective-permute-done = bf16[2,512,256]{2,1,0:T(8,128)(2,1)S(1)} collective-permute-done((bf16[2,512,256]{2,1,0:T(8,128)(2,1)S(1)}, bf16[2,512,256]{2,1,0:T(8,128)(2,1)S(1)}, u32[]{:S(2)}, u32[]{:S(2)}) %collective-permute-start) | collective-permute-done | bytes 524320 | tf_op jit(solution)/shard_map/ppermute | solution.py:20
  285.2 12.4 %collective-permute-done.1 = bf16[2,512,256]{2,1,0:T(8,128)(2,1)S(1)} collective-permute-done((bf16[2,512,256]{2,1,0:T(8,128)(2,1)S(1)}, bf16[2,512,256]{2,1,0:T(8,128)(2,1)S(1)}, u32[]{:S(2)}, u32[]{:S(2)}) %collective-permute-start.1) | collective-permute-done | bytes 524320 | tf_op jit(solution)/shard_map/ppermute | solution.py:20
  300.5 10.5 %collective-permute-done.2 = bf16[2,512,256]{2,1,0:T(8,128)(2,1)S(1)} collective-permute-done((bf16[2,512,256]{2,1,0:T(8,128)(2,1)S(1)}, bf16[2,512,256]{2,1,0:T(8,128)(2,1)S(1)}, u32[]{:S(2)}, u32[]{:S(2)}) %collective-permute-start.2) | collective-permute-done | bytes 524320 | tf_op jit(solution)/shard_map/ppermute | solution.py:20
  311.5 3.2 fusion.40
  317.1 2.5 fusion.52
  319.7 3.2 fusion.92
  323.8 2.6 fusion.24
  326.4 3.2 fusion.60
  337.8 2.7 fusion.90
  349.0 2.1 fusion.18
  351.0 1.7 copy.44
  352.7 1.5 convolution_add_fusion.11
  361.9 2.1 fusion.17
  364.0 1.7 copy.42
  367.8 2.3 fusion.58
  380.5 11.2 %all_to_all.61 = bf16[4,128,512]{2,1,0:T(8,128)(2,1)S(1)} all-to-all(bf16[4,128,512]{2,1,0:T(8,128)(2,1)S(1)} %bitcast.297), channel_id=1, replica_groups=mesh['dp'=2,'ulysses'=4,'blk'=4] {'ulysses'}, dimensions={0} | all-to-all | bytes 1048576 | tf_op jit(solution)/shard_map/all_to_all | solution.py:185
  (177 shorter events, 59.1 us)
Async XLA Ops:
  6.5 233.3 %copy-start = (bf16[1,128,4096]{2,1,0:T(8,128)(2,1)S(1)}, bf16[1,128,4096]{2,1,0:T(8,128)(2,1)}, u32[]{:S(2)}) copy-start(bf16[1,128,4096]{2,1,0:T(8,128)(2,1)} %param.5) | copy-start | bytes 3145732
  6.5 233.3 %all-gather.2.cloned.1.call-start = ((), (), s32[]{:S(2)}) async-start(), calls=%async_computation.4 | async-start | bytes 18874368 | tf_op jit(solution)/shard_map/all_gather | solution.py:101
  11.2 13.1 %all-to-all-start = ((bf16[128,4,512]{0,2,1:T(8,128)(2,1)}), bf16[128,4,512]{0,2,1:T(8,128)(2,1)S(1)}, u32[]{:S(2)}, u32[]{:S(2)}) async-start(bf16[128,4,512]{0,2,1:T(8,128)(2,1)} %bitcast.2), calls=%async_computation | async-start | bytes 1048576 | tf_op jit(solution)/shard_map/all_to_all | solution.py:110
  18.1 305.6 %copy-start.25 = (s32[256]{0:T(256)}, s32[256]{0:T(256)S(1)}, u32[]{:S(2)}) copy-start(s32[256]{0:T(256)S(1)} %get-tuple-element.110) | copy-start | bytes 3076
  249.0 9.4 %all-to-all-start.1 = ((bf16[128,4,256]{0,2,1:T(8,128)(2,1)}), bf16[128,4,256]{0,2,1:T(8,128)(2,1)S(1)}, u32[]{:S(2)}, u32[]{:S(2)}) async-start(bf16[128,4,256]{0,2,1:T(8,128)(2,1)} %bitcast.8), calls=%async_computation.1 | async-start | bytes 524288 | tf_op jit(solution)/shard_map/all_to_all | solution.py:111
  252.5 46.1 %copy-start.6 = (bf16[256,2,128]{2,0,1:T(8,128)(2,1)}, bf16[256,2,128]{2,0,1:T(8,128)(2,1)S(1)}, u32[]{:S(2)}) copy-start(bf16[256,2,128]{2,0,1:T(8,128)(2,1)S(1)} %get-tuple-element.129) | copy-start | bytes 393220
  258.4 9.4 %all-to-all-start.2 = ((bf16[128,4,256]{2,0,1:T(8,128)(2,1)}), bf16[128,4,256]{2,0,1:T(8,128)(2,1)S(1)}, u32[]{:S(2)}, u32[]{:S(2)}) async-start(bf16[128,4,256]{2,0,1:T(8,128)(2,1)} %bitcast.242), calls=%async_computation.2 | async-start | bytes 524288 | tf_op jit(solution)/shard_map/all_to_all | solution.py:112
  263.0 35.3 %copy-start.19 = (bf16[4,128,256]{2,1,0:T(8,128)(2,1)}, bf16[4,128,256]{2,1,0:T(8,128)(2,1)S(1)}, u32[]{:S(2)}) copy-start(bf16[4,128,256]{2,1,0:T(8,128)(2,1)S(1)} %copy.38) | copy-start | bytes 786436
  267.9 15.3 %collective-permute-start = (bf16[2,512,256]{2,1,0:T(8,128)(2,1)S(1)}, bf16[2,512,256]{2,1,0:T(8,128)(2,1)S(1)}, u32[]{:S(2)}, u32[]{:S(2)}) collective-permute-start(bf16[2,512,256]{2,1,0:T(8,128)(2,1)S(1)} %pad_maximum_fusion.1), channel_id=1, source_target_pairs={{3,0},{0,1},{1,2},{2,3},{7,4},{4,5},{5,6},{6,7},{11,8},{8,9},{9,10... | collective-permute-start | bytes 1572872 | tf_op jit(solution)/shard_map/ppermute | solution.py:20
  268.2 58.2 %copy-start.11 = (f32[512,256]{0,1:T(8,128)}, f32[512,256]{0,1:T(8,128)S(1)}, u32[]{:S(2)}) copy-start(f32[512,256]{0,1:T(8,128)S(1)} %convolution_multiply_fusion.22) | copy-start | bytes 1572868
  268.4 54.4 %copy-start.30 = (s32[256]{0:T(256)S(1)}, s32[256]{0:T(256)}, u32[]{:S(2)}) copy-start(s32[256]{0:T(256)} %get-tuple-element.112) | copy-start | bytes 3076
  283.2 49.0 %copy-start.22 = (bf16[2,512,256]{2,1,0:T(8,128)(2,1)}, bf16[2,512,256]{2,1,0:T(8,128)(2,1)S(1)}, u32[]{:S(2)}) copy-start(bf16[2,512,256]{2,1,0:T(8,128)(2,1)S(1)} %collective-permute-done) | copy-start | bytes 1572868
  283.2 14.4 %collective-permute-start.1 = (bf16[2,512,256]{2,1,0:T(8,128)(2,1)S(1)}, bf16[2,512,256]{2,1,0:T(8,128)(2,1)S(1)}, u32[]{:S(2)}, u32[]{:S(2)}) collective-permute-start(bf16[2,512,256]{2,1,0:T(8,128)(2,1)S(1)} %collective-permute-done), channel_id=1, source_target_pairs={{3,0},{0,1},{1,2},{2,3},{7,4},{4,5},{5,6},{6,7},{11,8},{8,9},{9,10... | collective-permute-start | bytes 1572872 | tf_op jit(solution)/shard_map/ppermute | solution.py:20
  283.4 42.9 %copy-start.12 = (f32[512,256]{0,1:T(8,128)}, f32[512,256]{0,1:T(8,128)S(1)}, u32[]{:S(2)}) copy-start(f32[512,256]{0,1:T(8,128)S(1)} %convolution_multiply_fusion.20) | copy-start | bytes 1572868
  283.5 40.3 %copy-start.26 = (s32[256]{0:T(256)S(1)}, s32[256]{0:T(256)}, u32[]{:S(2)}) copy-start(s32[256]{0:T(256)} %get-tuple-element.111) | copy-start | bytes 3076
  283.5 40.3 %copy-start.27 = (s32[256]{0:T(256)S(1)}, s32[256]{0:T(256)}, u32[]{:S(2)}) copy-start(s32[256]{0:T(256)} %get-tuple-element.109) | copy-start | bytes 3076
  283.5 40.3 %copy-start.28 = (s32[256]{0:T(256)S(1)}, s32[256]{0:T(256)}, u32[]{:S(2)}) copy-start(s32[256]{0:T(256)} %get-tuple-element.107) | copy-start | bytes 3076
  283.5 40.3 %copy-start.31 = (s32[256]{0:T(256)S(1)}, s32[256]{0:T(256)}, u32[]{:S(2)}) copy-start(s32[256]{0:T(256)} %get-tuple-element.105) | copy-start | bytes 3076
  283.7 42.7 %copy-start.10 = (f32[512,256]{0,1:T(8,128)}, f32[512,256]{0,1:T(8,128)S(1)}, u32[]{:S(2)}) copy-start(f32[512,256]{0,1:T(8,128)S(1)} %convolution_multiply_fusion.21) | copy-start | bytes 1572868
  284.9 41.4 %copy-start.2 = (f32[512,256]{0,1:T(8,128)}, f32[512,256]{0,1:T(8,128)S(1)}, u32[]{:S(2)}) copy-start(f32[512,256]{0,1:T(8,128)S(1)} %convolution_multiply_fusion.12) | copy-start | bytes 1572868
  285.2 41.2 %copy-start.1 = (f32[512,256]{0,1:T(8,128)}, f32[512,256]{0,1:T(8,128)S(1)}, u32[]{:S(2)}) copy-start(f32[512,256]{0,1:T(8,128)S(1)} %convolution_multiply_fusion.13) | copy-start | bytes 1572868
  297.6 35.6 %copy-start.23 = (bf16[2,512,256]{2,1,0:T(8,128)(2,1)}, bf16[2,512,256]{2,1,0:T(8,128)(2,1)S(1)}, u32[]{:S(2)}) copy-start(bf16[2,512,256]{2,1,0:T(8,128)(2,1)S(1)} %collective-permute-done.1) | copy-start | bytes 1572868
  297.6 13.4 %collective-permute-start.2 = (bf16[2,512,256]{2,1,0:T(8,128)(2,1)S(1)}, bf16[2,512,256]{2,1,0:T(8,128)(2,1)S(1)}, u32[]{:S(2)}, u32[]{:S(2)}) collective-permute-start(bf16[2,512,256]{2,1,0:T(8,128)(2,1)S(1)} %collective-permute-done.1), channel_id=1, source_target_pairs={{3,0},{0,1},{1,2},{2,3},{7,4},{4,5},{5,6},{6,7},{11,8},{8,9},{9,10... | collective-permute-start | bytes 1572872 | tf_op jit(solution)/shard_map/ppermute | solution.py:20
  298.1 31.6 %copy-start.13 = (f32[512,256]{0,1:T(8,128)}, f32[512,256]{0,1:T(8,128)S(1)}, u32[]{:S(2)}) copy-start(f32[512,256]{0,1:T(8,128)S(1)} %convolution_multiply_fusion.19) | copy-start | bytes 1572868
  (15 other events, 309.5 us)
Sparse Core Ops, SparseCore 0:
  9.5 230.3 all-gather.1
where the time goes:
time: 401 us; the launch traced here: 400 us
  waiting for transfers between devices  268 us (67%)
  matrix products  68.9 us (17%)
  between operations  14.4 us (4%)
  local copies, waits for them, and re-layouts  13.6 us (3%)
  other arithmetic  12.5 us (3%)
  blocking collectives  11.2 us (3%)
  starting transfers between devices  11.1 us (3%)
    all_gather x1, waiting for transfers between devices, shards(): lax.all_gather(pair_weight, ('dp', 'blk'), axis=0, tiled=True)  215 us
    dot_general x32, matrix products, add_tile(): jnp.dot(weights.astype(jnp.bfloat16), value_rows, preferred_element_type=...  38.1 us
    ppermute x3, waiting for transfers between devices, from_behind(): return lax.ppermute(block, axis, route)  37.2 us
    dot_general x32, matrix products, tile_scores(): lax.dot_general(query_rows, key_rows, (((1,), (1,)), ((), ())), preferred...  22.7 us
    all_to_all x1, blocking collectives, shards(): lax.all_to_all(block_output, 'ulysses', split_axis=0, concat_axis=1, tile...  11.2 us
    dot_general x1, matrix products, shards(): jnp.dot(inputs_local, lax.all_gather(pair_weight, ('dp', 'blk'), axis=0,...  8.09 us
  transfers between devices with their start and end apart: 7, of which 7 were waited for; matrix products, arithmetic and copies ran while one was open for 4% of the time, Pallas kernels for 0%

commit v1 on v0

--- a/solution.py
+++ b/solution.py
@@ -3,6 +3,8 @@
 import jax
 import jax.numpy as jnp
 from jax import lax
+from jax.experimental import pallas as pl
+from jax.experimental.pallas import tpu as pltpu
 from jax.sharding import PartitionSpec as P
 
 KVH = 8
@@ -73,7 +75,7 @@
     return (denominator, numerator)
 
 
-def shards(hidden_in, queries, pair_weight, span_order, yarn_divisor):
+def general_shards(hidden_in, queries, pair_weight, span_order, yarn_divisor):
     inputs_local = hidden_in[0]
     queries_local = queries[0]
     order_row = span_order[0]
@@ -186,9 +188,220 @@
     return token_output[None]
 
 
+def ring_route(dp_size, cycle_size):
+    order = []
+    for row in range(dp_size):
+        steps = range(cycle_size) if row % 2 == 0 else reversed(range(cycle_size))
+        order += [row * cycle_size + step for step in steps]
+    return order
+
+
+def swap(block, distance):
+    size = lax.axis_size("ulysses")
+    return lax.ppermute(block, "ulysses", [(i, i ^ distance) for i in range(size)])
+
+
+def wide_tables(positions, yarn_divisor):
+    angle_table = angles(positions, yarn_divisor)
+    cosine, sine = jnp.cos(angle_table), jnp.sin(angle_table)
+    return jnp.concatenate([cosine, cosine], axis=1), jnp.concatenate([-sine, sine], axis=1)
+
+
+def rope_head(head, cosine, signed_sine):
+    return head * cosine + pltpu.roll(head, HD // 2, 1) * signed_sine
+
+
+def query_rope_kernel(head_order, query_ref, cosine_ref, sine_ref, out_ref):
+    cosine, sine = cosine_ref[...], sine_ref[...]
+    for place, head in enumerate(head_order):
+        rows = query_ref[:, head * HD : (head + 1) * HD].astype(jnp.float32)
+        out_ref[place] = rope_head(rows, cosine, sine).astype(jnp.bfloat16)
+
+
+def pair_rope_kernel(total_ref, cosine_ref, sine_ref, out_ref):
+    cosine, sine = cosine_ref[...], sine_ref[...]
+    for head in range(out_ref.shape[0]):
+        rows = total_ref[:, head * HD : (head + 1) * HD]
+        out_ref[head] = rope_head(rows, cosine, sine).astype(jnp.bfloat16)
+
+
+def order_heads_kernel(head_order, block_ref, out_ref):
+    for place, head in enumerate(head_order):
+        out_ref[:, head * HD : (head + 1) * HD] = block_ref[place]
+
+
+def attention_kernel(order_ref, place_ref, query_ref, mine_ref, theirs_ref, out_ref, key_rows, value_rows):
+    spans = order_ref.shape[1]
+    sources, token_rows = query_ref.shape[0], query_ref.shape[2]
+    per_span = sources // 2
+    span_rows = per_span * token_rows
+    place = place_ref[0]
+    keys_here = place % 2 == 0
+    stored = []
+    for position in range(spans):
+        span = jnp.int32(0)
+        for candidate in range(1, spans):
+            span = jnp.where(order_ref[0, candidate] == position, candidate, span)
+        stored.append((span // 2, span % 2))
+    for position, (block, half) in enumerate(stored):
+        for part in range(per_span):
+            slot = jnp.bitwise_xor(half * per_span + part, place)
+            other = jnp.bitwise_xor(slot, 1)
+            mine = mine_ref[block, pl.ds(pl.multiple_of(slot * token_rows, token_rows), token_rows), :]
+            theirs = theirs_ref[block, pl.ds(pl.multiple_of(other * token_rows, token_rows), token_rows), :]
+            rows = pl.ds(position * span_rows + part * token_rows, token_rows)
+            key_rows[rows, :] = jnp.where(keys_here, mine, theirs)
+            value_rows[rows, :] = jnp.where(keys_here, theirs, mine)
+    row_index = lax.broadcasted_iota(jnp.int32, (span_rows, span_rows), 0)
+    column_index = lax.broadcasted_iota(jnp.int32, (span_rows, span_rows), 1)
+    for position, (block, half) in enumerate(stored):
+        query = query_ref[pl.ds(half * per_span, per_span), block].reshape(span_rows, HD)
+        reach = (position + 1) * span_rows
+        score = tile_scores(query, key_rows[:reach, :])
+        last = jnp.where(column_index <= row_index, score[:, position * span_rows :], -jnp.inf)
+        score = jnp.concatenate([score[:, : position * span_rows], last], axis=1) if position else last
+        row_top = jnp.max(score, axis=1, keepdims=True)
+        weights = jnp.exp(score - row_top)
+        denominator = jnp.sum(weights, axis=1, keepdims=True)
+        numerator = jnp.dot(
+            weights.astype(jnp.bfloat16), value_rows[:reach, :], preferred_element_type=jnp.float32
+        )
+        rows = (numerator / denominator).astype(jnp.bfloat16)
+        out_ref[pl.ds(half * per_span, per_span), block] = rows.reshape(per_span, token_rows, HD)
+
+
+VMEM = pl.BlockSpec(memory_space=pltpu.VMEM)
+SMEM = pl.BlockSpec(memory_space=pltpu.SMEM)
+
+
+def whole_cycle_shards(hidden_in, queries, pair_weight, span_order, yarn_divisor):
+    own_hidden = hidden_in[0]
+    token_rows = own_hidden.shape[0]
+    ulysses_size, cycle_size = lax.axis_size("ulysses"), lax.axis_size("blk")
+    dp_size = lax.axis_size("dp")
+    ulysses_index, cycle_index = lax.axis_index("ulysses"), lax.axis_index("blk")
+    dp_index = lax.axis_index("dp")
+    block_rows = token_rows * ulysses_size
+    span_rows = block_rows // 2
+    shard_rows = pair_weight.shape[0]
+    kv_width = KVH * HD
+    columns = cycle_size * HD
+    core, chip = ulysses_index % 2, ulysses_index // 2
+
+    piece = lax.dynamic_slice(
+        pair_weight, (0, core * kv_width + chip * columns), (shard_rows, columns)
+    )
+    order = ring_route(dp_size, cycle_size)
+    shards_total = len(order)
+    forward = [(order[i], order[(i + 1) % shards_total]) for i in range(shards_total)]
+    backward = [(target, source) for source, target in forward]
+    walked = jnp.where(dp_index % 2 == 0, cycle_index, cycle_size - 1 - cycle_index)
+    ring_place = dp_index * cycle_size + walked
+
+    def shard_at(place):
+        place = jnp.remainder(place, shards_total)
+        row, step = place // cycle_size, place % cycle_size
+        return row * cycle_size + jnp.where(row % 2 == 0, step, cycle_size - 1 - step)
+
+    partner = swap(own_hidden, 1)
+    slots = [own_hidden, partner]
+    for distance in range(2, ulysses_size, 2):
+        far = swap(own_hidden, distance)
+        slots += [far, swap(far, 1)]
+    hidden = jnp.concatenate(slots, axis=0)
+
+    def term(weight_rows, first_row):
+        left = lax.dynamic_slice(hidden, (0, first_row), (block_rows, weight_rows.shape[0]))
+        return jnp.dot(left, weight_rows, preferred_element_type=jnp.float32)
+
+    total = term(piece, shard_at(ring_place) * shard_rows)
+    ahead = behind = piece
+    for step in range(1, shards_total // 2):
+        ahead = lax.ppermute(ahead, ("dp", "blk"), forward)
+        behind = lax.ppermute(behind, ("dp", "blk"), backward)
+        total = total + term(ahead, shard_at(ring_place - step) * shard_rows)
+        total = total + term(behind, shard_at(ring_place + step) * shard_rows)
+    half_rows = shard_rows // 2
+    opposite = shard_at(ring_place + shards_total // 2) * shard_rows
+    ahead = lax.ppermute(ahead[:half_rows], ("dp", "blk"), forward)
+    behind = lax.ppermute(behind[half_rows:], ("dp", "blk"), backward)
+    total = total + term(ahead, opposite)
+    total = total + term(behind, opposite + half_rows)
+
+    slot_devices = jnp.bitwise_xor(ulysses_index, jnp.arange(ulysses_size, dtype=jnp.int32))
+    order_row = span_order[0]
+    span_values = lax.dynamic_slice(order_row, (2 * cycle_index,), (2,))
+    stored = slot_devices[:, None] * token_rows + jnp.arange(token_rows, dtype=jnp.int32)[None, :]
+    stored = stored.reshape(block_rows)
+    positions = jnp.where(stored < span_rows, span_values[0], span_values[1]) * span_rows + stored % span_rows
+    cosine, sine = wide_tables(positions, yarn_divisor)
+    own_cosine, own_sine = cosine[:token_rows], sine[:token_rows]
+    pair_cosine = jnp.where(core == 0, cosine, 1.0)
+    pair_sine = jnp.where(core == 0, sine, 0.0)
+
+    head_order = [
+        (chip_place * cycle_size + block) * 2 + core_place
+        for chip_place in range(ulysses_size // 2)
+        for core_place in range(2)
+        for block in range(cycle_size)
+    ]
+    rotated = pl.pallas_call(
+        lambda *refs: query_rope_kernel(head_order, *refs),
+        out_shape=jax.ShapeDtypeStruct((QH, token_rows, HD), jnp.bfloat16),
+        in_specs=[VMEM] * 3,
+        out_specs=VMEM,
+        name="query_rope",
+    )(queries[0], own_cosine, own_sine)
+    query_rows = lax.all_to_all(rotated, ("ulysses", "blk"), split_axis=0, concat_axis=0, tiled=True)
+    query_rows = query_rows.reshape(ulysses_size, cycle_size, token_rows, HD)
+
+    pair = pl.pallas_call(
+        pair_rope_kernel,
+        out_shape=jax.ShapeDtypeStruct((cycle_size, block_rows, HD), jnp.bfloat16),
+        in_specs=[VMEM] * 3,
+        out_specs=VMEM,
+        name="pair_rope",
+    )(total, pair_cosine, pair_sine)
+    mine = lax.all_to_all(pair, "blk", split_axis=0, concat_axis=0, tiled=True)
+    theirs = swap(mine, 1)
+
+    sequence_rows = cycle_size * block_rows
+    attended = pl.pallas_call(
+        attention_kernel,
+        out_shape=jax.ShapeDtypeStruct((ulysses_size, cycle_size, token_rows, HD), jnp.bfloat16),
+        in_specs=[SMEM, SMEM, VMEM, VMEM, VMEM],
+        out_specs=VMEM,
+        scratch_shapes=[
+            pltpu.VMEM((sequence_rows, HD), jnp.bfloat16),
+            pltpu.VMEM((sequence_rows, HD), jnp.bfloat16),
+        ],
+        compiler_params=pltpu.CompilerParams(vmem_limit_bytes=40 * 1024 * 1024),
+        name="attention",
+    )(span_order, ulysses_index.astype(jnp.int32).reshape(1), query_rows, mine, theirs)
+    heads = lax.all_to_all(
+        attended.reshape(QH, token_rows, HD), ("ulysses", "blk"), split_axis=0, concat_axis=0, tiled=True
+    )
+    rows = pl.pallas_call(
+        lambda *refs: order_heads_kernel(head_order, *refs),
+        out_shape=jax.ShapeDtypeStruct((token_rows, QH * HD), jnp.bfloat16),
+        in_specs=[VMEM],
+        out_specs=VMEM,
+        name="order_heads",
+    )(heads)
+    return rows[None]
+
+
 def solution(mesh):
+    sizes = dict(mesh.shape)
+    whole_cycle = (
+        sizes["blk"] == STEPS + 1
+        and sizes["ulysses"] * sizes["blk"] == QH
+        and QH == 2 * KVH
+        and sizes["ulysses"] & (sizes["ulysses"] - 1) == 0
+        and sizes["dp"] % 2 == 0
+    )
     return jax.shard_map(
-        shards,
+        whole_cycle_shards if whole_cycle else general_shards,
         mesh=mesh,
         in_specs=(
             P("dp", ("blk", "ulysses"), None),

time: 401 us -> 124 us (0.31)
  waiting for transfers between devices: 268 us -> 56.2 us
  matrix products: 68.9 us -> 7.86 us
  between operations: 14.4 us -> 0.13 us
  Pallas kernels: 0 us -> 12.6 us
  local copies, waits for them, and re-layouts: 13.6 us -> 1.47 us
  starting transfers between devices: 11.1 us -> 19.2 us
  blocking collectives: 11.2 us -> 19 us
  other arithmetic: 12.5 us -> 7.19 us
    all_gather x1 -> x0, waiting for transfers between devices: 215 us -> none  [shards(): lax.all_gather(pair_weight, ('dp', 'blk'), axis=0, tiled=True)]
    dot_general x65 -> x9, matrix products: 68.9 us -> 7.86 us  [term(): return jnp.dot(left, weight_rows, preferred_element_type=jnp.float32)]
    pallas_call x0 -> x4, Pallas kernels: none -> 12.6 us  [the longest x1 6.04 us: whole_cycle_shards(): pl.pallas_call(attention_kernel, out_shape=jax.ShapeDtypeStruct((ulysses_...]
    ppermute x3 -> x12, starting transfers between devices: 0.06 us -> 11.6 us  [the longest x3 5.04 us: whole_cycle_shards(): behind = lax.ppermute(behind, ('dp', 'blk'), backward)]
    all_to_all x3 -> x2, waiting for transfers between devices: 15.6 us -> 25.5 us  [the longest x1 15.3 us: whole_cycle_shards(): lax.all_to_all(rotated, ('ulysses', 'blk'), split_axis=0, concat_axis=0,...]
    all_to_all x1, blocking collectives: 11.2 us -> 19 us  [whole_cycle_shards(): lax.all_to_all(attended.reshape(QH, token_rows, HD), ('ulysses', 'blk'),...]
    reduce_sum x4 -> x0, other arithmetic: 6.51 us -> none  [the longest x2 5.01 us: add_tile(): denominator = denominator + jnp.sum(weights, axis=1)]
    ppermute x3 -> x12, waiting for transfers between devices: 37.2 us -> 30.7 us  [the longest x3 12.1 us: whole_cycle_shards(): behind = lax.ppermute(behind, ('dp', 'blk'), backward)]
  transfers between devices with their start and end apart: 7 -> 14, of which waited for: 7 -> 6; matrix products, arithmetic and copies ran while one was open for 4% -> 11% of each run, Pallas kernels for 0% -> 2%
where the time goes in v1:
time: 124 us
  waiting for transfers between devices  56.2 us (45%)
  starting transfers between devices  19.2 us (15%)
  blocking collectives  19 us (15%)
  Pallas kernels  12.6 us (10%)
  matrix products  7.86 us (6%)
  other arithmetic  7.19 us (6%)
  local copies, waits for them, and re-layouts  1.47 us (1%)
    all_to_all x1, blocking collectives, whole_cycle_shards(): lax.all_to_all(attended.reshape(QH, token_rows, HD), ('ulysses', 'blk'),...  19 us
    all_to_all x1, waiting for transfers between devices, whole_cycle_shards(): lax.all_to_all(rotated, ('ulysses', 'blk'), split_axis=0, concat_axis=0,...  15.3 us
    ppermute x3, waiting for transfers between devices, whole_cycle_shards(): behind = lax.ppermute(behind, ('dp', 'blk'), backward)  12.1 us
    ppermute x3, waiting for transfers between devices, whole_cycle_shards(): ahead = lax.ppermute(ahead, ('dp', 'blk'), forward)  10.9 us
    all_to_all x1, waiting for transfers between devices, whole_cycle_shards(): mine = lax.all_to_all(pair, 'blk', split_axis=0, concat_axis=0, tiled=True)  10.2 us
    dot_general x9, matrix products, term(): return jnp.dot(left, weight_rows, preferred_element_type=jnp.float32)  7.86 us
    ppermute x4, waiting for transfers between devices, swap(): lax.ppermute(block, 'ulysses', [(i, i ^ distance) for i in range(size)])  7.75 us
    pallas_call x1, Pallas kernels, whole_cycle_shards(): pl.pallas_call(attention_kernel, out_shape=jax.ShapeDtypeStruct((ulysses_...  6.04 us
  transfers between devices with their start and end apart: 14, of which 6 were waited for; matrix products, arithmetic and copies ran while one was open for 11% of the time, Pallas kernels for 2%

profile of v1, /device:TPU:0, one launch (start us, length us, event | category | flops | bytes accessed | tf_op | source)
XLA Modules:
  0.0 123.6 jit_solution(8740569142901122399)
XLA Ops:
  0.0 2.9 %collective-permute-start.1 = (bf16[128,4096]{1,0:T(8,128)(2,1)}, bf16[128,4096]{1,0:T(8,128)(2,1)}, u32[]{:S(2)}, u32[]{:S(2)}) collective-permute-start(bf16[128,4096]{1,0:T(8,128)(2,1)} %bitcast.26), channel_id=1, source_target_pairs={{0,8},{4,12},{8,0},{12,4},{1,9},{5,13},{9,1},{13,5},{2,10},{6,14},... | collective-permute-start | bytes 3145736 | tf_op jit(solution)/shard_map/ppermute | solution.py:201
  3.0 1.7 %collective-permute-start.4 = (bf16[512,512]{1,0:T(8,128)(2,1)S(1)}, bf16[512,512]{1,0:T(8,128)(2,1)S(1)}, u32[]{:S(2)}, u32[]{:S(2)}) collective-permute-start(bf16[512,512]{1,0:T(8,128)(2,1)S(1)} %constant_dynamic-slice_fusion), channel_id=1, source_target_pairs={{1,0},{2,1},{3,2},{19,3},{18,19},{17,18},{16,17},{0,16},{5,4},{6,5... | collective-permute-start | bytes 1572872 | tf_op jit(solution)/shard_map/ppermute | solution.py:321
  5.1 11.6 %collective-permute-done.4 = bf16[512,512]{1,0:T(8,128)(2,1)S(1)} collective-permute-done((bf16[512,512]{1,0:T(8,128)(2,1)S(1)}, bf16[512,512]{1,0:T(8,128)(2,1)S(1)}, u32[]{:S(2)}, u32[]{:S(2)}) %collective-permute-start.4) | collective-permute-done | bytes 524320 | tf_op jit(solution)/shard_map/ppermute | solution.py:321
  16.6 1.7 %collective-permute-start.6 = (bf16[512,512]{1,0:T(8,128)(2,1)S(1)}, bf16[512,512]{1,0:T(8,128)(2,1)}, u32[]{:S(2)}, u32[]{:S(2)}) collective-permute-start(bf16[512,512]{1,0:T(8,128)(2,1)S(1)} %collective-permute-done.4), channel_id=1, source_target_pairs={{1,0},{2,1},{3,2},{19,3},{18,19},{17,18},{16,17},{0,16},{5,4},{6,5... | collective-permute-start | bytes 1572872 | tf_op jit(solution)/shard_map/ppermute | solution.py:321
  18.7 7.7 %collective-permute-done.1 = bf16[128,4096]{1,0:T(8,128)(2,1)} collective-permute-done((bf16[128,4096]{1,0:T(8,128)(2,1)}, bf16[128,4096]{1,0:T(8,128)(2,1)}, u32[]{:S(2)}, u32[]{:S(2)}) %collective-permute-start.1) | collective-permute-done | bytes 1048608 | tf_op jit(solution)/shard_map/ppermute | solution.py:201
  27.8 1.3 %fusion.34 = f32[512]{0:T(512)S(1)} fusion(s32[]{:T(128)} %bitcast.4, s32[]{:T(128)} %bitcast.3, s32[4]{0:T(128)S(1)} %xor_multiply_fusion), kind=kLoop, calls=%fused_computation.51 | loop fusion | flops 8704 | bytes 2072 | tf_op jit(solution)/shard_map/convert_element_type | solution.py:44
  29.6 1.7 %collective-permute-start.8 = (bf16[512,512]{1,0:T(8,128)(2,1)}, bf16[512,512]{1,0:T(8,128)(2,1)S(1)}, u32[]{:S(2)}, u32[]{:S(2)}) collective-permute-start(bf16[512,512]{1,0:T(8,128)(2,1)} %collective-permute-done.6), channel_id=1, source_target_pairs={{1,0},{2,1},{3,2},{19,3},{18,19},{17,18},{16,17},{0,16},{5,4},{6,5... | collective-permute-start | bytes 1572872 | tf_op jit(solution)/shard_map/ppermute | solution.py:321
  33.3 1.0 maximum_select_fusion
  34.3 10.9 %collective-permute-done.7 = bf16[512,512]{1,0:T(8,128)(2,1)S(1)} collective-permute-done((bf16[512,512]{1,0:T(8,128)(2,1)}, bf16[512,512]{1,0:T(8,128)(2,1)S(1)}, u32[]{:S(2)}, u32[]{:S(2)}) %collective-permute-start.7) | collective-permute-done | bytes 524320 | tf_op jit(solution)/shard_map/ppermute | solution.py:320
  45.8 1.7 %collective-permute-start.10 = (bf16[256,512]{1,0:T(8,128)(2,1)S(1)}, bf16[256,512]{1,0:T(8,128)(2,1)S(1)}, u32[]{:S(2)}, u32[]{:S(2)}) collective-permute-start(bf16[256,512]{1,0:T(8,128)(2,1)S(1)} %slice.31), channel_id=1, source_target_pairs={{1,0},{2,1},{3,2},{19,3},{18,19},{17,18},{16,17},{0,16},{5,4},{6,5... | collective-permute-start | bytes 786440 | tf_op jit(solution)/shard_map/ppermute | solution.py:327
  47.4 2.4 %pad_maximum_fusion = bf16[512,4096]{1,0:T(8,128)(2,1)S(1)} fusion(bf16[128,4096]{1,0:T(8,128)(2,1)} %collective-permute-done.2, bf16[128,4096]{1,0:T(8,128)(2,1)} %collective-permute-done.1, bf16[128,4096]{1,0:T(8,128)(2,1)} %collective-permute-done, bf16[128,4096]{1,0:T(8,128)(2,1)} %bitcast.28), kind=kLoop, calls=%fused_computation | loop fusion | flops 16777216 | bytes 8388608 | tf_op jit(solution)/shard_map/concatenate | solution.py:311
  49.9 1.5 %fusion.13 = f32[512,512]{1,0:T(8,128)S(1)} fusion(bf16[512,512]{1,0:T(8,128)(2,1)} %collective-permute-done.3, bf16[512,4096]{1,0:T(8,128)(2,1)S(1)} %pad_maximum_fusion, s32[]{:T(128)S(6)} %select_n.244), kind=kOutput, calls=%fused_computation.17 | convolution fusion | flops 268435456 | bytes 2097156 | tf_op jit(solution)/shard_map/dot_general | solution.py:315
  52.2 1.5 %fusion.8 = f32[512,512]{1,0:T(8,128)S(1)} fusion(bf16[512,512]{1,0:T(8,128)(2,1)} %collective-permute-done.6, bf16[512,4096]{1,0:T(8,128)(2,1)S(1)} %pad_maximum_fusion, s32[]{:T(128)S(6)} %select_n.262), kind=kOutput, calls=%fused_computation.12 | convolution fusion | flops 268435456 | bytes 2097156 | tf_op jit(solution)/shard_map/dot_general | solution.py:315
  54.8 1.5 %fusion.3 = f32[512,512]{1,0:T(8,128)S(1)} fusion(f32[512,512]{1,0:T(8,128)S(1)} %fusion.8, f32[512,512]{1,0:T(8,128)S(1)} %fusion.4, bf16[512,512]{1,0:T(8,128)(2,1)} %collective-permute-done.5, bf16[512,4096]{1,0:T(8,128)(2,1)S(1)} %pad_maximum_fusion, s32[]{:T(128)S(6)} %select_n.256), kind=kOutput, calls=%fused_computation.6 | convolution fusion | flops 268959744 | bytes 4194308 | tf_op jit(solution)/shard_map/dot_general | solution.py:315
  56.3 1.5 %fusion.2.total_ref = f32[512,512]{1,0:T(8,128)} fusion(f32[512,512]{1,0:T(8,128)S(1)} %fusion.16, f32[512,512]{1,0:T(8,128)S(1)} %fusion.18, f32[512,512]{1,0:T(8,128)S(1)} %fusion.5, f32[512,512]{1,0:T(8,128)S(1)} %fusion.3, bf16[512,512]{1,0:T(8,128)(2,1)S(1)} %collective-permute-done.7, bf16[512,4096]{1,0:T(8,128)(2,1)S(1)} %pad_maximum_fusion, ...), kind=kOutput, calls=%fused_computation.4 | convolution fusion | flops 269484032 | bytes 6291460 | tf_op jit(solution)/shard_map/dot_general | solution.py:315
  57.8 2.5 %pair_rope.1 = bf16[4,512,128]{2,1,0:T(8,128)(2,1)} custom-call(f32[512,512]{1,0:T(8,128)} %fusion.2.total_ref, f32[512,128]{1,0:T(8,128)} %get-tuple-element.10.cosine_ref, f32[512,128]{1,0:T(8,128)} %get-tuple-element.11.sine_ref), custom_call_target="tpu_custom_call" | custom-call | tf_op jit(solution)/shard_map/pair_rope/pallas_call | solution.py:358
  60.3 3.8 %all-to-all-start.1 = ((bf16[4,512,128]{2,1,0:T(8,128)(2,1)}), bf16[4,512,128]{2,1,0:T(8,128)(2,1)S(1)}, u32[]{:S(2)}, u32[]{:S(2)}) async-start(bf16[4,512,128]{2,1,0:T(8,128)(2,1)} %pair_rope.1), calls=%async_computation.1 | async-start | bytes 1048576 | tf_op jit(solution)/shard_map/all_to_all | solution.py:365
  64.9 2.1 %query_rope.1 = bf16[16,128,128]{2,1,0:T(8,128)(2,1)} custom-call(bf16[128,2048]{1,0:T(8,128)(2,1)} %bitcast.29, f32[128,128]{1,0:T(8,128)} %get-tuple-element.13.refs_1_, f32[128,128]{1,0:T(8,128)} %get-tuple-element.12.refs_2_), custom_call_target="tpu_custom_call" | custom-call | tf_op jit(solution)/shard_map/query_rope/pallas_call | solution.py:348
  67.0 10.2 %all-to-all-done.1.mine_ref = bf16[4,512,128]{2,1,0:T(8,128)(2,1)S(1)} async-done(((bf16[4,512,128]{2,1,0:T(8,128)(2,1)}), bf16[4,512,128]{2,1,0:T(8,128)(2,1)S(1)}, u32[]{:S(2)}, u32[]{:S(2)}) %all-to-all-start.1) | async-done | bytes 524320 | tf_op jit(solution)/shard_map/all_to_all | solution.py:365
  77.2 3.8 %all-to-all-start = ((bf16[16,128,128]{2,1,0:T(8,128)(2,1)}), bf16[16,128,128]{2,1,0:T(8,128)(2,1)S(1)}, u32[]{:S(2)}, u32[]{:S(2)}) async-start(bf16[16,128,128]{2,1,0:T(8,128)(2,1)} %query_rope.1), calls=%async_computation | async-start | bytes 1048576 | tf_op jit(solution)/shard_map/all_to_all | solution.py:355
  81.4 15.3 %all-to-all-done = bf16[16,128,128]{2,1,0:T(8,128)(2,1)S(1)} async-done(((bf16[16,128,128]{2,1,0:T(8,128)(2,1)}), bf16[16,128,128]{2,1,0:T(8,128)(2,1)S(1)}, u32[]{:S(2)}, u32[]{:S(2)}) %all-to-all-start) | async-done | bytes 524320 | tf_op jit(solution)/shard_map/all_to_all | solution.py:355
  96.7 6.0 %attention.1 = bf16[4,4,128,128]{3,2,1,0:T(8,128)(2,1)S(1)} custom-call(s32[1,8]{1,0:T(1,128)S(1)} %copy-done.1, s32[1]{0:T(128)} %bitcast.place_ref, bf16[4,4,128,128]{3,2,1,0:T(8,128)(2,1)S(1)} %bitcast.24, bf16[4,512,128]{2,1,0:T(8,128)(2,1)S(1)} %all-to-all-done.1.mine_ref, bf16[4,512,128]{2,1,0:T(8,128)(2,1)} %collective-permute-done.11.theirs_ref), custom_call_target="tpu_custom_call" | custom-call | tf_op jit(solution)/shard_map/attention/pallas_call | solution.py:369
  102.7 19.0 %all_to_all.15.refs_0_ = bf16[16,128,128]{2,1,0:T(8,128)(2,1)} all-to-all(bf16[16,128,128]{2,1,0:T(8,128)(2,1)S(1)} %bitcast.25), channel_id=1, replica_groups=mesh['dp'=2,'ulysses'=4,'blk'=4] {'ulysses','blk'}, dimensions={0} | all-to-all | bytes 1048576 | tf_op jit(solution)/shard_map/all_to_all | solution.py:381
  121.7 2.0 %order_heads.1 = bf16[128,2048]{1,0:T(8,128)(2,1)} custom-call(bf16[16,128,128]{2,1,0:T(8,128)(2,1)} %all_to_all.15.refs_0_), custom_call_target="tpu_custom_call" | custom-call | tf_op jit(solution)/shard_map/order_heads/pallas_call | solution.py:384
  (38 shorter events, 8.3 us)
Async XLA Ops:
  0.0 2.9 %copy-start = (bf16[512,2048]{1,0:T(8,128)(2,1)S(1)}, bf16[512,2048]{1,0:T(8,128)(2,1)}, u32[]{:S(2)}) copy-start(bf16[512,2048]{1,0:T(8,128)(2,1)} %param.7) | copy-start | bytes 6291460
  0.0 26.4 %collective-permute-start.1 = (bf16[128,4096]{1,0:T(8,128)(2,1)}, bf16[128,4096]{1,0:T(8,128)(2,1)}, u32[]{:S(2)}, u32[]{:S(2)}) collective-permute-start(bf16[128,4096]{1,0:T(8,128)(2,1)} %bitcast.26), channel_id=1, source_target_pairs={{0,8},{4,12},{8,0},{12,4},{1,9},{5,13},{9,1},{13,5},{2,10},{6,14},... | collective-permute-start | bytes 3145736 | tf_op jit(solution)/shard_map/ppermute | solution.py:201
  3.0 13.6 %collective-permute-start.4 = (bf16[512,512]{1,0:T(8,128)(2,1)S(1)}, bf16[512,512]{1,0:T(8,128)(2,1)S(1)}, u32[]{:S(2)}, u32[]{:S(2)}) collective-permute-start(bf16[512,512]{1,0:T(8,128)(2,1)S(1)} %constant_dynamic-slice_fusion), channel_id=1, source_target_pairs={{1,0},{2,1},{3,2},{19,3},{18,19},{17,18},{16,17},{0,16},{5,4},{6,5... | collective-permute-start | bytes 1572872 | tf_op jit(solution)/shard_map/ppermute | solution.py:321
  4.7 13.7 %collective-permute-start.3 = (bf16[512,512]{1,0:T(8,128)(2,1)S(1)}, bf16[512,512]{1,0:T(8,128)(2,1)}, u32[]{:S(2)}, u32[]{:S(2)}) collective-permute-start(bf16[512,512]{1,0:T(8,128)(2,1)S(1)} %constant_dynamic-slice_fusion), channel_id=1, source_target_pairs={{0,1},{1,2},{2,3},{3,19},{19,18},{18,17},{17,16},{16,0},{4,5},{5,6... | collective-permute-start | bytes 1572872 | tf_op jit(solution)/shard_map/ppermute | solution.py:320
  5.1 42.4 %collective-permute-start = (bf16[128,4096]{1,0:T(8,128)(2,1)}, bf16[128,4096]{1,0:T(8,128)(2,1)}, u32[]{:S(2)}, u32[]{:S(2)}) collective-permute-start(bf16[128,4096]{1,0:T(8,128)(2,1)} %bitcast.27), channel_id=1, source_target_pairs={{0,4},{4,0},{8,12},{12,8},{1,5},{5,1},{9,13},{13,9},{2,6},{6,2},{1... | collective-permute-start | bytes 3145736 | tf_op jit(solution)/shard_map/ppermute | solution.py:201
  16.6 15.0 %copy-start.2 = (bf16[512,512]{1,0:T(8,128)(2,1)}, bf16[512,512]{1,0:T(8,128)(2,1)S(1)}, u32[]{:S(2)}) copy-start(bf16[512,512]{1,0:T(8,128)(2,1)S(1)} %collective-permute-done.4) | copy-start | bytes 1572868
  16.6 13.0 %collective-permute-start.6 = (bf16[512,512]{1,0:T(8,128)(2,1)S(1)}, bf16[512,512]{1,0:T(8,128)(2,1)}, u32[]{:S(2)}, u32[]{:S(2)}) collective-permute-start(bf16[512,512]{1,0:T(8,128)(2,1)S(1)} %collective-permute-done.4), channel_id=1, source_target_pairs={{1,0},{2,1},{3,2},{19,3},{18,19},{17,18},{16,17},{0,16},{5,4},{6,5... | collective-permute-start | bytes 1572872 | tf_op jit(solution)/shard_map/ppermute | solution.py:321
  18.3 13.0 %collective-permute-start.5 = (bf16[512,512]{1,0:T(8,128)(2,1)}, bf16[512,512]{1,0:T(8,128)(2,1)}, u32[]{:S(2)}, u32[]{:S(2)}) collective-permute-start(bf16[512,512]{1,0:T(8,128)(2,1)} %collective-permute-done.3), channel_id=1, source_target_pairs={{0,1},{1,2},{2,3},{3,19},{19,18},{18,17},{17,16},{16,0},{4,5},{5,6... | collective-permute-start | bytes 1572872 | tf_op jit(solution)/shard_map/ppermute | solution.py:320
  26.4 21.0 %collective-permute-start.2 = (bf16[128,4096]{1,0:T(8,128)(2,1)}, bf16[128,4096]{1,0:T(8,128)(2,1)}, u32[]{:S(2)}, u32[]{:S(2)}) collective-permute-start(bf16[128,4096]{1,0:T(8,128)(2,1)} %collective-permute-done.1), channel_id=1, source_target_pairs={{0,4},{4,0},{8,12},{12,8},{1,5},{5,1},{9,13},{13,9},{2,6},{6,2},{1... | collective-permute-start | bytes 3145736 | tf_op jit(solution)/shard_map/ppermute | solution.py:201
  29.6 16.1 %collective-permute-start.8 = (bf16[512,512]{1,0:T(8,128)(2,1)}, bf16[512,512]{1,0:T(8,128)(2,1)S(1)}, u32[]{:S(2)}, u32[]{:S(2)}) collective-permute-start(bf16[512,512]{1,0:T(8,128)(2,1)} %collective-permute-done.6), channel_id=1, source_target_pairs={{1,0},{2,1},{3,2},{19,3},{18,19},{17,18},{16,17},{0,16},{5,4},{6,5... | collective-permute-start | bytes 1572872 | tf_op jit(solution)/shard_map/ppermute | solution.py:321
  31.3 13.9 %collective-permute-start.7 = (bf16[512,512]{1,0:T(8,128)(2,1)}, bf16[512,512]{1,0:T(8,128)(2,1)S(1)}, u32[]{:S(2)}, u32[]{:S(2)}) collective-permute-start(bf16[512,512]{1,0:T(8,128)(2,1)} %collective-permute-done.5), channel_id=1, source_target_pairs={{0,1},{1,2},{2,3},{3,19},{19,18},{18,17},{17,16},{16,0},{4,5},{5,6... | collective-permute-start | bytes 1572872 | tf_op jit(solution)/shard_map/ppermute | solution.py:320
  45.3 8.5 %collective-permute-start.9 = (bf16[256,512]{1,0:T(8,128)(2,1)S(1)}, bf16[256,512]{1,0:T(8,128)(2,1)S(1)}, u32[]{:S(2)}, u32[]{:S(2)}) collective-permute-start(bf16[256,512]{1,0:T(8,128)(2,1)S(1)} %slice.30), channel_id=1, source_target_pairs={{0,1},{1,2},{2,3},{3,19},{19,18},{18,17},{17,16},{16,0},{4,5},{5,6... | collective-permute-start | bytes 786440 | tf_op jit(solution)/shard_map/ppermute | solution.py:326
  45.7 5.6 %copy-start.3 = (bf16[512,512]{1,0:T(8,128)(2,1)S(1)}, bf16[512,512]{1,0:T(8,128)(2,1)}, u32[]{:S(2)}) copy-start(bf16[512,512]{1,0:T(8,128)(2,1)} %copy-done.2) | copy-start | bytes 1572868
  45.8 8.7 %collective-permute-start.10 = (bf16[256,512]{1,0:T(8,128)(2,1)S(1)}, bf16[256,512]{1,0:T(8,128)(2,1)S(1)}, u32[]{:S(2)}, u32[]{:S(2)}) collective-permute-start(bf16[256,512]{1,0:T(8,128)(2,1)S(1)} %slice.31), channel_id=1, source_target_pairs={{1,0},{2,1},{3,2},{19,3},{18,19},{17,18},{16,17},{0,16},{5,4},{6,5... | collective-permute-start | bytes 786440 | tf_op jit(solution)/shard_map/ppermute | solution.py:327
  57.8 38.9 %copy-start.1 = (s32[1,8]{1,0:T(1,128)S(1)}, s32[1,8]{1,0:T(1,128)}, u32[]{:S(2)}) copy-start(s32[1,8]{1,0:T(1,128)} %order_ref.1) | copy-start | bytes 100
  60.3 16.9 %all-to-all-start.1 = ((bf16[4,512,128]{2,1,0:T(8,128)(2,1)}), bf16[4,512,128]{2,1,0:T(8,128)(2,1)S(1)}, u32[]{:S(2)}, u32[]{:S(2)}) async-start(bf16[4,512,128]{2,1,0:T(8,128)(2,1)} %pair_rope.1), calls=%async_computation.1 | async-start | bytes 1048576 | tf_op jit(solution)/shard_map/all_to_all | solution.py:365
  77.2 19.5 %all-to-all-start = ((bf16[16,128,128]{2,1,0:T(8,128)(2,1)}), bf16[16,128,128]{2,1,0:T(8,128)(2,1)S(1)}, u32[]{:S(2)}, u32[]{:S(2)}) async-start(bf16[16,128,128]{2,1,0:T(8,128)(2,1)} %query_rope.1), calls=%async_computation | async-start | bytes 1048576 | tf_op jit(solution)/shard_map/all_to_all | solution.py:355
  81.0 15.7 %collective-permute-start.11 = (bf16[4,512,128]{2,1,0:T(8,128)(2,1)S(1)}, bf16[4,512,128]{2,1,0:T(8,128)(2,1)}, u32[]{:S(2)}, u32[]{:S(2)}) collective-permute-start(bf16[4,512,128]{2,1,0:T(8,128)(2,1)S(1)} %all-to-all-done.1.mine_ref), channel_id=1, source_target_pairs={{0,4},{4,0},{8,12},{12,8},{1,5},{5,1},{9,13},{13,9},{2,6},{6,2},{1... | collective-permute-start | bytes 1572872 | tf_op jit(solution)/shard_map/ppermute | solution.py:201

commit v2 on v1

--- a/solution.py
+++ b/solution.py
@@ -188,14 +188,6 @@
     return token_output[None]
 
 
-def ring_route(dp_size, cycle_size):
-    order = []
-    for row in range(dp_size):
-        steps = range(cycle_size) if row % 2 == 0 else reversed(range(cycle_size))
-        order += [row * cycle_size + step for step in steps]
-    return order
-
-
 def swap(block, distance):
     size = lax.axis_size("ulysses")
     return lax.ppermute(block, "ulysses", [(i, i ^ distance) for i in range(size)])
@@ -218,11 +210,16 @@
         out_ref[place] = rope_head(rows, cosine, sine).astype(jnp.bfloat16)
 
 
-def pair_rope_kernel(total_ref, cosine_ref, sine_ref, out_ref):
+def pair_rope_kernel(block_ref, total_ref, hidden_ref, weight_ref, cosine_ref, sine_ref, *refs):
+    out_refs, sum_ref = refs[:-1], refs[-1]
+    sum_ref[...] = total_ref[...] + jnp.dot(
+        hidden_ref[...], weight_ref[...], preferred_element_type=jnp.float32
+    )
     cosine, sine = cosine_ref[...], sine_ref[...]
-    for head in range(out_ref.shape[0]):
-        rows = total_ref[:, head * HD : (head + 1) * HD]
-        out_ref[head] = rope_head(rows, cosine, sine).astype(jnp.bfloat16)
+    for distance, out_ref in enumerate(out_refs):
+        head = lax.rem(block_ref[0] + distance, len(out_refs))
+        rows = sum_ref[:, pl.ds(pl.multiple_of(head * HD, HD), HD)]
+        out_ref[...] = rope_head(rows, cosine, sine).astype(jnp.bfloat16)
 
 
 def order_heads_kernel(head_order, block_ref, out_ref):
@@ -230,28 +227,36 @@
         out_ref[:, head * HD : (head + 1) * HD] = block_ref[place]
 
 
-def attention_kernel(order_ref, place_ref, query_ref, mine_ref, theirs_ref, out_ref, key_rows, value_rows):
+def attention_kernel(order_ref, place_ref, query_ref, *refs):
     spans = order_ref.shape[1]
+    blocks = spans // 2
+    mine_refs, theirs_refs = refs[:blocks], refs[blocks : 2 * blocks]
+    out_ref, key_rows, value_rows = refs[2 * blocks :]
     sources, token_rows = query_ref.shape[0], query_ref.shape[2]
     per_span = sources // 2
     span_rows = per_span * token_rows
-    place = place_ref[0]
+    place, block_here = place_ref[0], place_ref[1]
     keys_here = place % 2 == 0
+    for distance in range(blocks):
+        block = lax.rem(block_here + blocks - distance, blocks)
+        for half in range(2):
+            first = order_ref[0, 2 * block + half] * span_rows
+            for part in range(per_span):
+                slot = jnp.bitwise_xor(half * per_span + part, place)
+                other = jnp.bitwise_xor(slot, 1)
+                mine = mine_refs[distance][pl.ds(pl.multiple_of(slot * token_rows, token_rows), token_rows), :]
+                theirs = theirs_refs[distance][
+                    pl.ds(pl.multiple_of(other * token_rows, token_rows), token_rows), :
+                ]
+                rows = pl.ds(pl.multiple_of(first + part * token_rows, token_rows), token_rows)
+                key_rows[rows, :] = jnp.where(keys_here, mine, theirs)
+                value_rows[rows, :] = jnp.where(keys_here, theirs, mine)
     stored = []
     for position in range(spans):
         span = jnp.int32(0)
         for candidate in range(1, spans):
             span = jnp.where(order_ref[0, candidate] == position, candidate, span)
         stored.append((span // 2, span % 2))
-    for position, (block, half) in enumerate(stored):
-        for part in range(per_span):
-            slot = jnp.bitwise_xor(half * per_span + part, place)
-            other = jnp.bitwise_xor(slot, 1)
-            mine = mine_ref[block, pl.ds(pl.multiple_of(slot * token_rows, token_rows), token_rows), :]
-            theirs = theirs_ref[block, pl.ds(pl.multiple_of(other * token_rows, token_rows), token_rows), :]
-            rows = pl.ds(position * span_rows + part * token_rows, token_rows)
-            key_rows[rows, :] = jnp.where(keys_here, mine, theirs)
-            value_rows[rows, :] = jnp.where(keys_here, theirs, mine)
     row_index = lax.broadcasted_iota(jnp.int32, (span_rows, span_rows), 0)
     column_index = lax.broadcasted_iota(jnp.int32, (span_rows, span_rows), 1)
     for position, (block, half) in enumerate(stored):
@@ -291,43 +296,6 @@
     piece = lax.dynamic_slice(
         pair_weight, (0, core * kv_width + chip * columns), (shard_rows, columns)
     )
-    order = ring_route(dp_size, cycle_size)
-    shards_total = len(order)
-    forward = [(order[i], order[(i + 1) % shards_total]) for i in range(shards_total)]
-    backward = [(target, source) for source, target in forward]
-    walked = jnp.where(dp_index % 2 == 0, cycle_index, cycle_size - 1 - cycle_index)
-    ring_place = dp_index * cycle_size + walked
-
-    def shard_at(place):
-        place = jnp.remainder(place, shards_total)
-        row, step = place // cycle_size, place % cycle_size
-        return row * cycle_size + jnp.where(row % 2 == 0, step, cycle_size - 1 - step)
-
-    partner = swap(own_hidden, 1)
-    slots = [own_hidden, partner]
-    for distance in range(2, ulysses_size, 2):
-        far = swap(own_hidden, distance)
-        slots += [far, swap(far, 1)]
-    hidden = jnp.concatenate(slots, axis=0)
-
-    def term(weight_rows, first_row):
-        left = lax.dynamic_slice(hidden, (0, first_row), (block_rows, weight_rows.shape[0]))
-        return jnp.dot(left, weight_rows, preferred_element_type=jnp.float32)
-
-    total = term(piece, shard_at(ring_place) * shard_rows)
-    ahead = behind = piece
-    for step in range(1, shards_total // 2):
-        ahead = lax.ppermute(ahead, ("dp", "blk"), forward)
-        behind = lax.ppermute(behind, ("dp", "blk"), backward)
-        total = total + term(ahead, shard_at(ring_place - step) * shard_rows)
-        total = total + term(behind, shard_at(ring_place + step) * shard_rows)
-    half_rows = shard_rows // 2
-    opposite = shard_at(ring_place + shards_total // 2) * shard_rows
-    ahead = lax.ppermute(ahead[:half_rows], ("dp", "blk"), forward)
-    behind = lax.ppermute(behind[half_rows:], ("dp", "blk"), backward)
-    total = total + term(ahead, opposite)
-    total = total + term(behind, opposite + half_rows)
-
     slot_devices = jnp.bitwise_xor(ulysses_index, jnp.arange(ulysses_size, dtype=jnp.int32))
     order_row = span_order[0]
     span_values = lax.dynamic_slice(order_row, (2 * cycle_index,), (2,))
@@ -350,34 +318,92 @@
         out_shape=jax.ShapeDtypeStruct((QH, token_rows, HD), jnp.bfloat16),
         in_specs=[VMEM] * 3,
         out_specs=VMEM,
+        compiler_params=pltpu.CompilerParams(vmem_limit_bytes=8 * 1024 * 1024),
         name="query_rope",
     )(queries[0], own_cosine, own_sine)
+    def ahead(block, distance=1):
+        return lax.ppermute(block, "blk", [(i, (i + distance) % cycle_size) for i in range(cycle_size)])
+
+    def across(block):
+        return lax.ppermute(block, "dp", [(i, dp_size - 1 - i) for i in range(dp_size)])
+
+    def first_row(distance, row):
+        return (row * cycle_size + jnp.remainder(cycle_index - distance, cycle_size)) * shard_rows
+
+    other_row = dp_size - 1 - dp_index
+    far_slots = [swap(own_hidden, distance) for distance in range(2, ulysses_size, 2)]
+    partner = swap(own_hidden, 1)
+    crossed = across(piece)
+    received = [(piece, first_row(0, dp_index))]
+    travelling = piece
+    hidden = total = None
+
+    def add_terms(total, received):
+        for rows, row in received:
+            left = lax.dynamic_slice(hidden, (0, row), (block_rows, shard_rows))
+            term = jnp.dot(left, rows, preferred_element_type=jnp.float32)
+            total = term if total is None else total + term
+        return total
+
+    for distance in range(1, cycle_size):
+        travelling = ahead(travelling)
+        if distance == cycle_size - 1:
+            total = add_terms(total, received)
+            received = []
+            travelling, total = lax.optimization_barrier((travelling, total))
+        if distance == 1:
+            rotated, pair_cosine, pair_sine, travelling = lax.optimization_barrier(
+                (rotated, pair_cosine, pair_sine, travelling)
+            )
+        travelling, crossed = lax.optimization_barrier((travelling, crossed))
+        received += [
+            (crossed, first_row(distance - 1, other_row)),
+            (travelling, first_row(distance, dp_index)),
+        ]
+        crossed = across(travelling)
+        if distance == cycle_size - 2:
+            *far_slots, travelling = lax.optimization_barrier((*far_slots, travelling))
+            slots = [own_hidden, partner]
+            for far in far_slots:
+                slots += [far, swap(far, 1)]
+            hidden = jnp.concatenate(slots, axis=0)
+    received.append((crossed, first_row(cycle_size - 1, other_row)))
+    last_piece, last_row = received.pop()
+    total = add_terms(total, received)
+    rotated, travelling = lax.optimization_barrier((rotated, travelling))
     query_rows = lax.all_to_all(rotated, ("ulysses", "blk"), split_axis=0, concat_axis=0, tiled=True)
     query_rows = query_rows.reshape(ulysses_size, cycle_size, token_rows, HD)
-
-    pair = pl.pallas_call(
+    last_hidden = lax.dynamic_slice(hidden, (0, last_row), (block_rows, shard_rows))
+    last_piece, total, last_hidden = lax.optimization_barrier((last_piece, total, last_hidden))
+
+    *pairs, = pl.pallas_call(
         pair_rope_kernel,
-        out_shape=jax.ShapeDtypeStruct((cycle_size, block_rows, HD), jnp.bfloat16),
-        in_specs=[VMEM] * 3,
-        out_specs=VMEM,
+        out_shape=[jax.ShapeDtypeStruct((block_rows, HD), jnp.bfloat16)] * cycle_size,
+        in_specs=[SMEM] + [VMEM] * 5,
+        out_specs=[VMEM] * cycle_size,
+        scratch_shapes=[pltpu.VMEM((block_rows, columns), jnp.float32)],
+        compiler_params=pltpu.CompilerParams(vmem_limit_bytes=12 * 1024 * 1024),
         name="pair_rope",
-    )(total, pair_cosine, pair_sine)
-    mine = lax.all_to_all(pair, "blk", split_axis=0, concat_axis=0, tiled=True)
-    theirs = swap(mine, 1)
+    )(cycle_index.astype(jnp.int32).reshape(1), total, last_hidden, last_piece, pair_cosine, pair_sine)
+    *pairs, query_rows = lax.optimization_barrier((*pairs, query_rows))
+    mine, theirs = [pairs[0]] + [None] * (cycle_size - 1), [swap(pairs[0], 1)] + [None] * (cycle_size - 1)
+    for distance in sorted(range(1, cycle_size), key=lambda d: -min(d, cycle_size - d)):
+        mine[distance] = ahead(pairs[distance], distance)
+        theirs[distance] = swap(mine[distance], 1)
 
     sequence_rows = cycle_size * block_rows
     attended = pl.pallas_call(
         attention_kernel,
         out_shape=jax.ShapeDtypeStruct((ulysses_size, cycle_size, token_rows, HD), jnp.bfloat16),
-        in_specs=[SMEM, SMEM, VMEM, VMEM, VMEM],
+        in_specs=[SMEM, SMEM] + [VMEM] * (1 + 2 * cycle_size),
         out_specs=VMEM,
         scratch_shapes=[
             pltpu.VMEM((sequence_rows, HD), jnp.bfloat16),
             pltpu.VMEM((sequence_rows, HD), jnp.bfloat16),
         ],
-        compiler_params=pltpu.CompilerParams(vmem_limit_bytes=40 * 1024 * 1024),
+        compiler_params=pltpu.CompilerParams(vmem_limit_bytes=24 * 1024 * 1024),
         name="attention",
-    )(span_order, ulysses_index.astype(jnp.int32).reshape(1), query_rows, mine, theirs)
+    )(span_order, jnp.stack([ulysses_index, cycle_index]).astype(jnp.int32), query_rows, *mine, *theirs)
     heads = lax.all_to_all(
         attended.reshape(QH, token_rows, HD), ("ulysses", "blk"), split_axis=0, concat_axis=0, tiled=True
     )
@@ -386,6 +412,7 @@
         out_shape=jax.ShapeDtypeStruct((token_rows, QH * HD), jnp.bfloat16),
         in_specs=[VMEM],
         out_specs=VMEM,
+        compiler_params=pltpu.CompilerParams(vmem_limit_bytes=8 * 1024 * 1024),
         name="order_heads",
     )(heads)
     return rows[None]
@@ -398,7 +425,7 @@
         and sizes["ulysses"] * sizes["blk"] == QH
         and QH == 2 * KVH
         and sizes["ulysses"] & (sizes["ulysses"] - 1) == 0
-        and sizes["dp"] % 2 == 0
+        and sizes["dp"] == 2
     )
     return jax.shard_map(
         whole_cycle_shards if whole_cycle else general_shards,

time: 124 us -> 114 us (0.919)
  waiting for transfers between devices: 56.2 us -> 39.3 us
  local copies, waits for them, and re-layouts: 1.47 us -> 5.79 us
  Pallas kernels: 12.6 us -> 8.44 us
  matrix products: 7.86 us -> 11.5 us
  blocking collectives: 19 us -> 22.1 us
  other arithmetic: 7.19 us -> 5.86 us
    all_to_all x1, waiting for transfers between devices: 15.3 us -> 0.01 us  [whole_cycle_shards(): lax.all_to_all(rotated, ('ulysses', 'blk'), split_axis=0, concat_axis=0,...]
    ppermute x8 -> x10, waiting for transfers between devices: 23 us -> 36.8 us  [the longest x6 28 us: ahead(): lax.ppermute(block, 'blk', [(i, (i + distance) % cycle_size) for i in ran...]
    all_to_all x1 -> x0, waiting for transfers between devices: 10.2 us -> none  [whole_cycle_shards(): mine = lax.all_to_all(pair, 'blk', split_axis=0, concat_axis=0, tiled=True)]
    ppermute x8 -> x10, starting transfers between devices: 8.26 us -> 14.8 us  [the longest x6 9.57 us: ahead(): lax.ppermute(block, 'blk', [(i, (i + distance) % cycle_size) for i in ran...]
    ppermute x4 -> x7, waiting for transfers between devices: 7.75 us -> 2.51 us  [swap(): lax.ppermute(block, 'ulysses', [(i, i ^ distance) for i in range(size)])]
    all_to_all x1 -> x0, starting transfers between devices: 3.8 us -> none  [whole_cycle_shards(): mine = lax.all_to_all(pair, 'blk', split_axis=0, concat_axis=0, tiled=True)]
    dot_general x9 -> x7, matrix products: 7.86 us -> 11.5 us  [add_terms(): term = jnp.dot(left, rows, preferred_element_type=jnp.float32)]
    unnamed x8 -> x10, local copies, waits for them, and re-layouts: 0.02 us -> 3.3 us
  transfers between devices with their start and end apart: 14 -> 18, of which waited for: 6 -> 9; matrix products, arithmetic and copies ran while one was open for 11% -> 17% of each run, Pallas kernels for 2% -> 2%
where the time goes in v2:
time: 114 us
  waiting for transfers between devices  39.3 us (34%)
  blocking collectives  22.1 us (19%)
  starting transfers between devices  20.4 us (18%)
  matrix products  11.5 us (10%)
  Pallas kernels  8.44 us (7%)
  other arithmetic  5.86 us (5%)
  local copies, waits for them, and re-layouts  5.79 us (5%)
    ppermute x6, waiting for transfers between devices, ahead(): lax.ppermute(block, 'blk', [(i, (i + distance) % cycle_size) for i in ran...  28 us
    all_to_all x1, blocking collectives, whole_cycle_shards(): lax.all_to_all(attended.reshape(QH, token_rows, HD), ('ulysses', 'blk'),...  22.1 us
    dot_general x7, matrix products, add_terms(): term = jnp.dot(left, rows, preferred_element_type=jnp.float32)  11.5 us
    ppermute x6, starting transfers between devices, ahead(): lax.ppermute(block, 'blk', [(i, (i + distance) % cycle_size) for i in ran...  9.57 us
    ppermute x4, waiting for transfers between devices, across(): lax.ppermute(block, 'dp', [(i, dp_size - 1 - i) for i in range(dp_size)])  8.76 us
    pallas_call x1, Pallas kernels, whole_cycle_shards(): pl.pallas_call(attention_kernel, out_shape=jax.ShapeDtypeStruct((ulysses_...  5.59 us
    ppermute x4, starting transfers between devices, across(): lax.ppermute(block, 'dp', [(i, dp_size - 1 - i) for i in range(dp_size)])  5.21 us
    all_to_all x1, starting transfers between devices, whole_cycle_shards(): lax.all_to_all(rotated, ('ulysses', 'blk'), split_axis=0, concat_axis=0,...  3.58 us
  transfers between devices with their start and end apart: 18, of which 9 were waited for; matrix products, arithmetic and copies ran while one was open for 17% of the time, Pallas kernels for 2%

profile of v2, /device:TPU:0, one launch (start us, length us, event | category | flops | bytes accessed | tf_op | source)
XLA Modules:
  0.0 113.6 jit_solution(5923494425534318626)
XLA Ops:
  0.0 1.6 %copy-done = bf16[512,2048]{1,0:T(8,128)(2,1)S(1)} copy-done((bf16[512,2048]{1,0:T(8,128)(2,1)S(1)}, bf16[512,2048]{1,0:T(8,128)(2,1)}, u32[]{:S(2)}) %copy-start) | copy-done | bytes 2097176
  1.6 3.1 %collective-permute-start.1 = (bf16[512,512]{1,0:T(8,128)(2,1)S(1)}, bf16[512,512]{1,0:T(8,128)(2,1)}, u32[]{:S(2)}, u32[]{:S(2)}) collective-permute-start(bf16[512,512]{1,0:T(8,128)(2,1)S(1)} %constant_dynamic-slice_fusion.1), channel_id=1, source_target_pairs={{0,1},{1,2},{2,3},{3,0},{4,5},{5,6},{6,7},{7,4},{8,9},{9,10},{10,1... | collective-permute-start | bytes 1572872 | tf_op jit(solution)/shard_map/ppermute | solution.py:325
  4.7 1.5 %collective-permute-start.2 = (bf16[512,512]{1,0:T(8,128)(2,1)S(1)}, bf16[512,512]{1,0:T(8,128)(2,1)}, u32[]{:S(2)}, u32[]{:S(2)}) collective-permute-start(bf16[512,512]{1,0:T(8,128)(2,1)S(1)} %constant_dynamic-slice_fusion.1), channel_id=1, source_target_pairs={{0,16},{16,0},{1,17},{17,1},{2,18},{18,2},{3,19},{19,3},{4,20},{20... | collective-permute-start | bytes 1572872 | tf_op jit(solution)/shard_map/ppermute | solution.py:328
  6.2 1.5 %collective-permute-start = (bf16[128,4096]{1,0:T(8,128)(2,1)}, bf16[128,4096]{1,0:T(8,128)(2,1)}, u32[]{:S(2)}, u32[]{:S(2)}) collective-permute-start(bf16[128,4096]{1,0:T(8,128)(2,1)} %bitcast.2), channel_id=1, source_target_pairs={{0,8},{4,12},{8,0},{12,4},{1,9},{5,13},{9,1},{13,5},{2,10},{6,14},... | collective-permute-start | bytes 3145736 | tf_op jit(solution)/shard_map/ppermute | solution.py:193
  14.6 4.2 %collective-permute-done.1 = bf16[512,512]{1,0:T(8,128)(2,1)} collective-permute-done((bf16[512,512]{1,0:T(8,128)(2,1)S(1)}, bf16[512,512]{1,0:T(8,128)(2,1)}, u32[]{:S(2)}, u32[]{:S(2)}) %collective-permute-start.1) | collective-permute-done | bytes 524320 | tf_op jit(solution)/shard_map/ppermute | solution.py:325
  19.8 1.5 %collective-permute-start.4 = (bf16[512,512]{1,0:T(8,128)(2,1)}, bf16[512,512]{1,0:T(8,128)(2,1)}, u32[]{:S(2)}, u32[]{:S(2)}) collective-permute-start(bf16[512,512]{1,0:T(8,128)(2,1)} %collective-permute-done.1), channel_id=1, source_target_pairs={{0,16},{16,0},{1,17},{17,1},{2,18},{18,2},{3,19},{19,3},{4,20},{20... | collective-permute-start | bytes 1572872 | tf_op jit(solution)/shard_map/ppermute | solution.py:328
  21.3 12.7 %collective-permute-done.3 = bf16[512,512]{1,0:T(8,128)(2,1)} collective-permute-done((bf16[512,512]{1,0:T(8,128)(2,1)}, bf16[512,512]{1,0:T(8,128)(2,1)}, u32[]{:S(2)}, u32[]{:S(2)}) %collective-permute-start.3) | collective-permute-done | bytes 524320 | tf_op jit(solution)/shard_map/ppermute | solution.py:325
  35.5 1.6 %collective-permute-done.7 = bf16[128,4096]{1,0:T(8,128)(2,1)} collective-permute-done((bf16[128,4096]{1,0:T(8,128)(2,1)}, bf16[128,4096]{1,0:T(8,128)(2,1)}, u32[]{:S(2)}, u32[]{:S(2)}) %collective-permute-start.7) | collective-permute-done | bytes 1048608 | tf_op jit(solution)/shard_map/ppermute | solution.py:193
  37.0 2.4 %pad_maximum_fusion = bf16[512,4096]{1,0:T(8,128)(2,1)S(1)} fusion(bf16[128,4096]{1,0:T(8,128)(2,1)} %collective-permute-done.7, bf16[128,4096]{1,0:T(8,128)(2,1)} %collective-permute-done, bf16[128,4096]{1,0:T(8,128)(2,1)} %collective-permute-done.6, bf16[128,4096]{1,0:T(8,128)(2,1)} %bitcast.2), kind=kLoop, calls=%fused_computation | loop fusion | flops 16777216 | bytes 8388608 | tf_op jit(solution)/shard_map/concatenate | solution.py:369
  39.4 1.9 %fusion.13 = f32[512,512]{1,0:T(8,128)S(1)} fusion(bf16[512,512]{1,0:T(8,128)(2,1)} %collective-permute-done.1, bf16[512,4096]{1,0:T(8,128)(2,1)S(1)} %pad_maximum_fusion, s32[]{:T(128)S(6)} %select_n.108), kind=kOutput, calls=%fused_computation.14 | convolution fusion | flops 268435456 | bytes 2097156 | tf_op jit(solution)/shard_map/dot_general | solution.py:344
  42.8 1.5 %fusion.15 = f32[512,512]{1,0:T(8,128)S(1)} fusion(bf16[512,512]{1,0:T(8,128)(2,1)} %collective-permute-done.2, bf16[512,4096]{1,0:T(8,128)(2,1)S(1)} %pad_maximum_fusion, s32[]{:T(128)S(6)} %select_n.106), kind=kOutput, calls=%fused_computation.16 | convolution fusion | flops 268435456 | bytes 2097156 | tf_op jit(solution)/shard_map/dot_general | solution.py:344
  44.3 1.5 %fusion.11 = f32[512,512]{1,0:T(8,128)S(1)} fusion(bf16[512,512]{1,0:T(8,128)(2,1)} %collective-permute-done.4, bf16[512,4096]{1,0:T(8,128)(2,1)S(1)} %pad_maximum_fusion, s32[]{:T(128)S(6)} %select_n.109), kind=kOutput, calls=%fused_computation.12 | convolution fusion | flops 268435456 | bytes 2097156 | tf_op jit(solution)/shard_map/dot_general | solution.py:344
  45.8 1.5 %fusion.2 = f32[512,512]{1,0:T(8,128)} fusion(f32[512,512]{1,0:T(8,128)S(1)} %fusion.9, f32[512,512]{1,0:T(8,128)S(1)} %fusion.11, f32[512,512]{1,0:T(8,128)S(1)} %fusion.13, f32[512,512]{1,0:T(8,128)S(1)} %fusion.15, bf16[512,512]{1,0:T(8,128)(2,1)S(1)} %constant_dynamic-slice_fusion.1, bf16[512,4096]{1,0:T(8,128)(2,1)S(1)} %pad_maximum_fusion, ...), kind=kOutput, calls=%fused_computation.4 | convolution fusion | flops 269484032 | bytes 6291460 | tf_op jit(solution)/shard_map/dot_general | solution.py:344
  47.3 4.1 %collective-permute-done.5 = bf16[512,512]{1,0:T(8,128)(2,1)} collective-permute-done((bf16[512,512]{1,0:T(8,128)(2,1)}, bf16[512,512]{1,0:T(8,128)(2,1)}, u32[]{:S(2)}, u32[]{:S(2)}) %collective-permute-start.5) | collective-permute-done | bytes 524320 | tf_op jit(solution)/shard_map/ppermute | solution.py:325
  51.5 3.6 %all-to-all-start = ((bf16[16,128,128]{2,1,0:T(8,128)(2,1)}), bf16[16,128,128]{2,1,0:T(8,128)(2,1)S(1)}, u32[]{:S(2)}, u32[]{:S(2)}) async-start(bf16[16,128,128]{2,1,0:T(8,128)(2,1)} %query_rope.1), calls=%async_computation | async-start | bytes 1048576 | tf_op jit(solution)/shard_map/all_to_all | solution.py:374
  57.0 1.6 %fusion.7 = f32[512,512]{1,0:T(8,128)S(1)} fusion(bf16[512,512]{1,0:T(8,128)(2,1)} %collective-permute-done.8, bf16[512,4096]{1,0:T(8,128)(2,1)} %copy-done.4, s32[]{:T(128)S(6)} %select_n.112), kind=kOutput, calls=%fused_computation.8 | convolution fusion | flops 268435456 | bytes 2097156 | tf_op jit(solution)/shard_map/dot_general | solution.py:344
  58.6 2.0 %add_add_fusion.total_ref = f32[512,512]{1,0:T(8,128)S(1)} fusion(f32[512,512]{1,0:T(8,128)} %fusion.2, f32[512,512]{1,0:T(8,128)S(1)} %fusion.7, bf16[512,512]{1,0:T(8,128)(2,1)} %collective-permute-done.5, bf16[512,4096]{1,0:T(8,128)(2,1)} %copy-done.4, s32[]{:T(128)S(6)} %select_n.114), kind=kOutput, calls=%fused_computation.5 | convolution fusion | flops 268959744 | bytes 4194308 | tf_op jit(solution)/shard_map/dot_general | solution.py:344
  60.6 8.8 %collective-permute-done.9.weight_ref = bf16[512,512]{1,0:T(8,128)(2,1)S(1)} collective-permute-done((bf16[512,512]{1,0:T(8,128)(2,1)}, bf16[512,512]{1,0:T(8,128)(2,1)S(1)}, u32[]{:S(2)}, u32[]{:S(2)}) %collective-permute-start.9) | collective-permute-done | bytes 524320 | tf_op jit(solution)/shard_map/ppermute | solution.py:328
  70.9 1.6 %collective-permute-start.10 = (bf16[512,128]{1,0:T(8,128)(2,1)}, bf16[512,128]{1,0:T(8,128)(2,1)S(1)}, u32[]{:S(2)}, u32[]{:S(2)}) collective-permute-start(bf16[512,128]{1,0:T(8,128)(2,1)} %copy-done.3), channel_id=1, source_target_pairs={{0,1},{1,2},{2,3},{3,0},{4,5},{5,6},{6,7},{7,4},{8,9},{9,10},{10,1... | collective-permute-start | bytes 393224 | tf_op jit(solution)/shard_map/ppermute | solution.py:325
  72.6 2.4 %collective-permute-start.11 = (bf16[512,128]{1,0:T(8,128)(2,1)S(1)}, bf16[512,128]{1,0:T(8,128)(2,1)S(1)}, u32[]{:S(2)}, u32[]{:S(2)}) collective-permute-start(bf16[512,128]{1,0:T(8,128)(2,1)S(1)} %get-tuple-element.57), channel_id=1, source_target_pairs={{0,2},{1,3},{2,0},{3,1},{4,6},{5,7},{6,4},{7,5},{8,10},{9,11},{10,... | collective-permute-start | bytes 393224 | tf_op jit(solution)/shard_map/ppermute | solution.py:325
  76.4 3.0 %collective-permute-done.10.refs_1_ = bf16[512,128]{1,0:T(8,128)(2,1)S(1)} collective-permute-done((bf16[512,128]{1,0:T(8,128)(2,1)}, bf16[512,128]{1,0:T(8,128)(2,1)S(1)}, u32[]{:S(2)}, u32[]{:S(2)}) %collective-permute-start.10) | collective-permute-done | bytes 131104 | tf_op jit(solution)/shard_map/ppermute | solution.py:325
  79.5 4.0 %collective-permute-done.11.refs_2_ = bf16[512,128]{1,0:T(8,128)(2,1)S(1)} collective-permute-done((bf16[512,128]{1,0:T(8,128)(2,1)S(1)}, bf16[512,128]{1,0:T(8,128)(2,1)S(1)}, u32[]{:S(2)}, u32[]{:S(2)}) %collective-permute-start.11) | collective-permute-done | bytes 131104 | tf_op jit(solution)/shard_map/ppermute | solution.py:325
  85.0 5.6 %attention.1 = bf16[4,4,128,128]{3,2,1,0:T(8,128)(2,1)S(1)} custom-call(s32[1,8]{1,0:T(1,128)S(1)} %copy-done.2, s32[2]{0:T(128)S(1)} %pad_add_fusion.place_ref, bf16[4,4,128,128]{3,2,1,0:T(8,128)(2,1)S(1)} %bitcast.23, bf16[512,128]{1,0:T(8,128)(2,1)S(1)} %get-tuple-element.55.refs_0_, bf16[512,128]{1,0:T(8,128)(2,1)S(1)} %collective-permute-done.10.refs_1_, ...), custom_call_target="tpu_custom_call" | custom-call | tf_op jit(solution)/shard_map/attention/pallas_call | solution.py:395
  90.6 22.1 %all_to_all.10.refs_0_ = bf16[16,128,128]{2,1,0:T(8,128)(2,1)S(1)} all-to-all(bf16[16,128,128]{2,1,0:T(8,128)(2,1)S(1)} %bitcast.24), channel_id=1, replica_groups=mesh['dp'=2,'ulysses'=4,'blk'=4] {'ulysses','blk'}, dimensions={0} | all-to-all | bytes 1048576 | tf_op jit(solution)/shard_map/all_to_all | solution.py:407
  (46 shorter events, 18.1 us)
Async XLA Ops:
  0.0 1.6 %copy-start = (bf16[512,2048]{1,0:T(8,128)(2,1)S(1)}, bf16[512,2048]{1,0:T(8,128)(2,1)}, u32[]{:S(2)}) copy-start(bf16[512,2048]{1,0:T(8,128)(2,1)} %param.7) | copy-start | bytes 6291460
  1.6 17.1 %collective-permute-start.1 = (bf16[512,512]{1,0:T(8,128)(2,1)S(1)}, bf16[512,512]{1,0:T(8,128)(2,1)}, u32[]{:S(2)}, u32[]{:S(2)}) collective-permute-start(bf16[512,512]{1,0:T(8,128)(2,1)S(1)} %constant_dynamic-slice_fusion.1), channel_id=1, source_target_pairs={{0,1},{1,2},{2,3},{3,0},{4,5},{5,6},{6,7},{7,4},{8,9},{9,10},{10,1... | collective-permute-start | bytes 1572872 | tf_op jit(solution)/shard_map/ppermute | solution.py:325
  4.7 14.1 %collective-permute-start.2 = (bf16[512,512]{1,0:T(8,128)(2,1)S(1)}, bf16[512,512]{1,0:T(8,128)(2,1)}, u32[]{:S(2)}, u32[]{:S(2)}) collective-permute-start(bf16[512,512]{1,0:T(8,128)(2,1)S(1)} %constant_dynamic-slice_fusion.1), channel_id=1, source_target_pairs={{0,16},{16,0},{1,17},{17,1},{2,18},{18,2},{3,19},{19,3},{4,20},{20... | collective-permute-start | bytes 1572872 | tf_op jit(solution)/shard_map/ppermute | solution.py:328
  6.2 27.8 %collective-permute-start = (bf16[128,4096]{1,0:T(8,128)(2,1)}, bf16[128,4096]{1,0:T(8,128)(2,1)}, u32[]{:S(2)}, u32[]{:S(2)}) collective-permute-start(bf16[128,4096]{1,0:T(8,128)(2,1)} %bitcast.2), channel_id=1, source_target_pairs={{0,8},{4,12},{8,0},{12,4},{1,9},{5,13},{9,1},{13,5},{2,10},{6,14},... | collective-permute-start | bytes 3145736 | tf_op jit(solution)/shard_map/ppermute | solution.py:193
  12.3 1.0 copy-start.1
  18.8 15.2 %collective-permute-start.3 = (bf16[512,512]{1,0:T(8,128)(2,1)}, bf16[512,512]{1,0:T(8,128)(2,1)}, u32[]{:S(2)}, u32[]{:S(2)}) collective-permute-start(bf16[512,512]{1,0:T(8,128)(2,1)} %collective-permute-done.1), channel_id=1, source_target_pairs={{0,1},{1,2},{2,3},{3,0},{4,5},{5,6},{6,7},{7,4},{8,9},{9,10},{10,1... | collective-permute-start | bytes 1572872 | tf_op jit(solution)/shard_map/ppermute | solution.py:325
  19.8 14.2 %collective-permute-start.4 = (bf16[512,512]{1,0:T(8,128)(2,1)}, bf16[512,512]{1,0:T(8,128)(2,1)}, u32[]{:S(2)}, u32[]{:S(2)}) collective-permute-start(bf16[512,512]{1,0:T(8,128)(2,1)} %collective-permute-done.1), channel_id=1, source_target_pairs={{0,16},{16,0},{1,17},{17,1},{2,18},{18,2},{3,19},{19,3},{4,20},{20... | collective-permute-start | bytes 1572872 | tf_op jit(solution)/shard_map/ppermute | solution.py:328
  21.3 14.2 %collective-permute-start.6 = (bf16[128,4096]{1,0:T(8,128)(2,1)}, bf16[128,4096]{1,0:T(8,128)(2,1)}, u32[]{:S(2)}, u32[]{:S(2)}) collective-permute-start(bf16[128,4096]{1,0:T(8,128)(2,1)} %bitcast.2), channel_id=1, source_target_pairs={{0,4},{4,0},{8,12},{12,8},{1,5},{5,1},{9,13},{13,9},{2,6},{6,2},{1... | collective-permute-start | bytes 3145736 | tf_op jit(solution)/shard_map/ppermute | solution.py:193
  34.0 3.0 %collective-permute-start.7 = (bf16[128,4096]{1,0:T(8,128)(2,1)}, bf16[128,4096]{1,0:T(8,128)(2,1)}, u32[]{:S(2)}, u32[]{:S(2)}) collective-permute-start(bf16[128,4096]{1,0:T(8,128)(2,1)} %collective-permute-done), channel_id=1, source_target_pairs={{0,4},{4,0},{8,12},{12,8},{1,5},{5,1},{9,13},{13,9},{2,6},{6,2},{1... | collective-permute-start | bytes 3145736 | tf_op jit(solution)/shard_map/ppermute | solution.py:193
  34.1 17.4 %collective-permute-start.8 = (bf16[512,512]{1,0:T(8,128)(2,1)}, bf16[512,512]{1,0:T(8,128)(2,1)}, u32[]{:S(2)}, u32[]{:S(2)}) collective-permute-start(bf16[512,512]{1,0:T(8,128)(2,1)} %collective-permute-done.3), channel_id=1, source_target_pairs={{0,16},{16,0},{1,17},{17,1},{2,18},{18,2},{3,19},{19,3},{4,20},{20... | collective-permute-start | bytes 1572872 | tf_op jit(solution)/shard_map/ppermute | solution.py:328
  35.4 16.0 %collective-permute-start.5 = (bf16[512,512]{1,0:T(8,128)(2,1)}, bf16[512,512]{1,0:T(8,128)(2,1)}, u32[]{:S(2)}, u32[]{:S(2)}) collective-permute-start(bf16[512,512]{1,0:T(8,128)(2,1)} %collective-permute-done.3), channel_id=1, source_target_pairs={{0,1},{1,2},{2,3},{3,0},{4,5},{5,6},{6,7},{7,4},{8,9},{9,10},{10,1... | collective-permute-start | bytes 1572872 | tf_op jit(solution)/shard_map/ppermute | solution.py:325
  39.4 6.4 %copy-start.4 = (bf16[512,4096]{1,0:T(8,128)(2,1)}, bf16[512,4096]{1,0:T(8,128)(2,1)S(1)}, u32[]{:S(2)}) copy-start(bf16[512,4096]{1,0:T(8,128)(2,1)S(1)} %pad_maximum_fusion) | copy-start | bytes 12582916
  51.5 19.5 %all-to-all-start = ((bf16[16,128,128]{2,1,0:T(8,128)(2,1)}), bf16[16,128,128]{2,1,0:T(8,128)(2,1)S(1)}, u32[]{:S(2)}, u32[]{:S(2)}) async-start(bf16[16,128,128]{2,1,0:T(8,128)(2,1)} %query_rope.1), calls=%async_computation | async-start | bytes 1048576 | tf_op jit(solution)/shard_map/all_to_all | solution.py:374
  55.1 14.3 %collective-permute-start.9 = (bf16[512,512]{1,0:T(8,128)(2,1)}, bf16[512,512]{1,0:T(8,128)(2,1)S(1)}, u32[]{:S(2)}, u32[]{:S(2)}) collective-permute-start(bf16[512,512]{1,0:T(8,128)(2,1)} %collective-permute-done.5), channel_id=1, source_target_pairs={{0,16},{16,0},{1,17},{17,1},{2,18},{18,2},{3,19},{19,3},{4,20},{20... | collective-permute-start | bytes 1572872 | tf_op jit(solution)/shard_map/ppermute | solution.py:328
  57.0 28.0 %copy-start.2 = (s32[1,8]{1,0:T(1,128)S(1)}, s32[1,8]{1,0:T(1,128)}, u32[]{:S(2)}) copy-start(s32[1,8]{1,0:T(1,128)} %order_ref.1) | copy-start | bytes 100
  70.2 0.7 copy-start.3
  70.9 8.5 %collective-permute-start.10 = (bf16[512,128]{1,0:T(8,128)(2,1)}, bf16[512,128]{1,0:T(8,128)(2,1)S(1)}, u32[]{:S(2)}, u32[]{:S(2)}) collective-permute-start(bf16[512,128]{1,0:T(8,128)(2,1)} %copy-done.3), channel_id=1, source_target_pairs={{0,1},{1,2},{2,3},{3,0},{4,5},{5,6},{6,7},{7,4},{8,9},{9,10},{10,1... | collective-permute-start | bytes 393224 | tf_op jit(solution)/shard_map/ppermute | solution.py:325
  72.6 10.9 %collective-permute-start.11 = (bf16[512,128]{1,0:T(8,128)(2,1)S(1)}, bf16[512,128]{1,0:T(8,128)(2,1)S(1)}, u32[]{:S(2)}, u32[]{:S(2)}) collective-permute-start(bf16[512,128]{1,0:T(8,128)(2,1)S(1)} %get-tuple-element.57), channel_id=1, source_target_pairs={{0,2},{1,3},{2,0},{3,1},{4,6},{5,7},{6,4},{7,5},{8,10},{9,11},{10,... | collective-permute-start | bytes 393224 | tf_op jit(solution)/shard_map/ppermute | solution.py:325
  74.9 8.5 %collective-permute-start.12 = (bf16[512,128]{1,0:T(8,128)(2,1)S(1)}, bf16[512,128]{1,0:T(8,128)(2,1)S(1)}, u32[]{:S(2)}, u32[]{:S(2)}) collective-permute-start(bf16[512,128]{1,0:T(8,128)(2,1)S(1)} %get-tuple-element.58), channel_id=1, source_target_pairs={{0,3},{1,0},{2,1},{3,2},{4,7},{5,4},{6,5},{7,6},{8,11},{9,8},{10,9... | collective-permute-start | bytes 393224 | tf_op jit(solution)/shard_map/ppermute | solution.py:325
  76.4 7.6 %collective-permute-start.13 = (bf16[512,128]{1,0:T(8,128)(2,1)S(1)}, bf16[512,128]{1,0:T(8,128)(2,1)S(1)}, u32[]{:S(2)}, u32[]{:S(2)}) collective-permute-start(bf16[512,128]{1,0:T(8,128)(2,1)S(1)} %get-tuple-element.55.refs_0_), channel_id=1, source_target_pairs={{0,4},{4,0},{8,12},{12,8},{1,5},{5,1},{9,13},{13,9},{2,6},{6,2},{1... | collective-permute-start | bytes 393224 | tf_op jit(solution)/shard_map/ppermute | solution.py:193
  79.5 4.6 %collective-permute-start.14 = (bf16[512,128]{1,0:T(8,128)(2,1)S(1)}, bf16[512,128]{1,0:T(8,128)(2,1)S(1)}, u32[]{:S(2)}, u32[]{:S(2)}) collective-permute-start(bf16[512,128]{1,0:T(8,128)(2,1)S(1)} %collective-permute-done.10.refs_1_), channel_id=1, source_target_pairs={{0,4},{4,0},{8,12},{12,8},{1,5},{5,1},{9,13},{13,9},{2,6},{6,2},{1... | collective-permute-start | bytes 393224 | tf_op jit(solution)/shard_map/ppermute | solution.py:193
  83.4 1.3 %collective-permute-start.15 = (bf16[512,128]{1,0:T(8,128)(2,1)S(1)}, bf16[512,128]{1,0:T(8,128)(2,1)S(1)}, u32[]{:S(2)}, u32[]{:S(2)}) collective-permute-start(bf16[512,128]{1,0:T(8,128)(2,1)S(1)} %collective-permute-done.11.refs_2_), channel_id=1, source_target_pairs={{0,4},{4,0},{8,12},{12,8},{1,5},{5,1},{9,13},{13,9},{2,6},{6,2},{1... | collective-permute-start | bytes 393224 | tf_op jit(solution)/shard_map/ppermute | solution.py:193
  83.4 1.5 %collective-permute-start.16 = (bf16[512,128]{1,0:T(8,128)(2,1)S(1)}, bf16[512,128]{1,0:T(8,128)(2,1)S(1)}, u32[]{:S(2)}, u32[]{:S(2)}) collective-permute-start(bf16[512,128]{1,0:T(8,128)(2,1)S(1)} %collective-permute-done.12.refs_3_), channel_id=1, source_target_pairs={{0,4},{4,0},{8,12},{12,8},{1,5},{5,1},{9,13},{13,9},{2,6},{6,2},{1... | collective-permute-start | bytes 393224 | tf_op jit(solution)/shard_map/ppermute | solution.py:193

commit v3 on v2

--- a/solution.py
+++ b/solution.py
@@ -1,3 +1,4 @@
+import functools
 import math
 
 import jax
@@ -210,10 +211,21 @@
         out_ref[place] = rope_head(rows, cosine, sine).astype(jnp.bfloat16)
 
 
-def pair_rope_kernel(block_ref, total_ref, hidden_ref, weight_ref, cosine_ref, sine_ref, *refs):
+def terms_kernel(count, rows_ref, hidden_ref, *refs):
+    out_ref = refs[-1]
+    total = refs[count][...] if len(refs) > count + 1 else None
+    for index, chunk_ref in enumerate(refs[:count]):
+        depth = chunk_ref.shape[0]
+        columns = pl.ds(pl.multiple_of(rows_ref[index], depth), depth)
+        term = jnp.dot(hidden_ref[:, columns], chunk_ref[...], preferred_element_type=jnp.float32)
+        total = term if total is None else total + term
+    out_ref[...] = total
+
+
+def pair_rope_kernel(block_ref, total_ref, hidden_ref, chunk_ref, cosine_ref, sine_ref, *refs):
     out_refs, sum_ref = refs[:-1], refs[-1]
     sum_ref[...] = total_ref[...] + jnp.dot(
-        hidden_ref[...], weight_ref[...], preferred_element_type=jnp.float32
+        hidden_ref[...], chunk_ref[...], preferred_element_type=jnp.float32
     )
     cosine, sine = cosine_ref[...], sine_ref[...]
     for distance, out_ref in enumerate(out_refs):
@@ -232,7 +244,7 @@
     blocks = spans // 2
     mine_refs, theirs_refs = refs[:blocks], refs[blocks : 2 * blocks]
     out_ref, key_rows, value_rows = refs[2 * blocks :]
-    sources, token_rows = query_ref.shape[0], query_ref.shape[2]
+    sources, token_rows = query_ref.shape[1:3]
     per_span = sources // 2
     span_rows = per_span * token_rows
     place, block_here = place_ref[0], place_ref[1]
@@ -260,7 +272,7 @@
     row_index = lax.broadcasted_iota(jnp.int32, (span_rows, span_rows), 0)
     column_index = lax.broadcasted_iota(jnp.int32, (span_rows, span_rows), 1)
     for position, (block, half) in enumerate(stored):
-        query = query_ref[pl.ds(half * per_span, per_span), block].reshape(span_rows, HD)
+        query = query_ref[block, pl.ds(half * per_span, per_span)].reshape(span_rows, HD)
         reach = (position + 1) * span_rows
         score = tile_scores(query, key_rows[:reach, :])
         last = jnp.where(column_index <= row_index, score[:, position * span_rows :], -jnp.inf)
@@ -272,7 +284,7 @@
             weights.astype(jnp.bfloat16), value_rows[:reach, :], preferred_element_type=jnp.float32
         )
         rows = (numerator / denominator).astype(jnp.bfloat16)
-        out_ref[pl.ds(half * per_span, per_span), block] = rows.reshape(per_span, token_rows, HD)
+        out_ref[block, pl.ds(half * per_span, per_span)] = rows.reshape(per_span, token_rows, HD)
 
 
 VMEM = pl.BlockSpec(memory_space=pltpu.VMEM)
@@ -296,6 +308,7 @@
     piece = lax.dynamic_slice(
         pair_weight, (0, core * kv_width + chip * columns), (shard_rows, columns)
     )
+
     slot_devices = jnp.bitwise_xor(ulysses_index, jnp.arange(ulysses_size, dtype=jnp.int32))
     order_row = span_order[0]
     span_values = lax.dynamic_slice(order_row, (2 * cycle_index,), (2,))
@@ -309,9 +322,9 @@
 
     head_order = [
         (chip_place * cycle_size + block) * 2 + core_place
+        for block in range(cycle_size)
         for chip_place in range(ulysses_size // 2)
         for core_place in range(2)
-        for block in range(cycle_size)
     ]
     rotated = pl.pallas_call(
         lambda *refs: query_rope_kernel(head_order, *refs),
@@ -333,24 +346,23 @@
     other_row = dp_size - 1 - dp_index
     far_slots = [swap(own_hidden, distance) for distance in range(2, ulysses_size, 2)]
     partner = swap(own_hidden, 1)
-    crossed = across(piece)
+    hidden = None
+
+    def add_terms(chunks, total):
+        before = [] if total is None else [total]
+        return pl.pallas_call(
+            functools.partial(terms_kernel, len(chunks)),
+            out_shape=jax.ShapeDtypeStruct((block_rows, columns), jnp.float32),
+            in_specs=[SMEM] + [VMEM] * (1 + len(chunks) + len(before)),
+            out_specs=VMEM,
+            compiler_params=pltpu.CompilerParams(vmem_limit_bytes=16 * 1024 * 1024),
+            name="terms",
+        )(jnp.stack([row for _, row in chunks]), hidden, *(chunk for chunk, _ in chunks), *before)
+
+    travelling, crossed = piece, across(piece)
     received = [(piece, first_row(0, dp_index))]
-    travelling = piece
-    hidden = total = None
-
-    def add_terms(total, received):
-        for rows, row in received:
-            left = lax.dynamic_slice(hidden, (0, row), (block_rows, shard_rows))
-            term = jnp.dot(left, rows, preferred_element_type=jnp.float32)
-            total = term if total is None else total + term
-        return total
-
-    for distance in range(1, cycle_size):
+    for distance in range(1, cycle_size - 1):
         travelling = ahead(travelling)
-        if distance == cycle_size - 1:
-            total = add_terms(total, received)
-            received = []
-            travelling, total = lax.optimization_barrier((travelling, total))
         if distance == 1:
             rotated, pair_cosine, pair_sine, travelling = lax.optimization_barrier(
                 (rotated, pair_cosine, pair_sine, travelling)
@@ -361,22 +373,28 @@
             (travelling, first_row(distance, dp_index)),
         ]
         crossed = across(travelling)
-        if distance == cycle_size - 2:
-            *far_slots, travelling = lax.optimization_barrier((*far_slots, travelling))
-            slots = [own_hidden, partner]
-            for far in far_slots:
-                slots += [far, swap(far, 1)]
-            hidden = jnp.concatenate(slots, axis=0)
-    received.append((crossed, first_row(cycle_size - 1, other_row)))
-    last_piece, last_row = received.pop()
-    total = add_terms(total, received)
-    rotated, travelling = lax.optimization_barrier((rotated, travelling))
-    query_rows = lax.all_to_all(rotated, ("ulysses", "blk"), split_axis=0, concat_axis=0, tiled=True)
-    query_rows = query_rows.reshape(ulysses_size, cycle_size, token_rows, HD)
+
+    *far_slots, travelling = lax.optimization_barrier((*far_slots, travelling))
+    slots = [own_hidden, partner]
+    for far in far_slots:
+        slots += [far, swap(far, 1)]
+    hidden = jnp.concatenate(slots, axis=0)
+    total = add_terms(received, None)
+    rotated, total = lax.optimization_barrier((rotated, total))
+    query_rows = lax.all_to_all(rotated, ("blk", "ulysses"), split_axis=0, concat_axis=0, tiled=True)
+    query_rows = query_rows.reshape(cycle_size, ulysses_size, token_rows, HD)
+
+    travelling = ahead(travelling)
+    travelling, crossed, total = lax.optimization_barrier((travelling, crossed, total))
+    received = [
+        (crossed, first_row(cycle_size - 2, other_row)),
+        (travelling, first_row(cycle_size - 1, dp_index)),
+    ]
+    last_piece, last_row = across(travelling), first_row(cycle_size - 1, other_row)
+    total = add_terms(received, total)
     last_hidden = lax.dynamic_slice(hidden, (0, last_row), (block_rows, shard_rows))
     last_piece, total, last_hidden = lax.optimization_barrier((last_piece, total, last_hidden))
-
-    *pairs, = pl.pallas_call(
+    pairs = pl.pallas_call(
         pair_rope_kernel,
         out_shape=[jax.ShapeDtypeStruct((block_rows, HD), jnp.bfloat16)] * cycle_size,
         in_specs=[SMEM] + [VMEM] * 5,
@@ -394,7 +412,7 @@
     sequence_rows = cycle_size * block_rows
     attended = pl.pallas_call(
         attention_kernel,
-        out_shape=jax.ShapeDtypeStruct((ulysses_size, cycle_size, token_rows, HD), jnp.bfloat16),
+        out_shape=jax.ShapeDtypeStruct((cycle_size, ulysses_size, token_rows, HD), jnp.bfloat16),
         in_specs=[SMEM, SMEM] + [VMEM] * (1 + 2 * cycle_size),
         out_specs=VMEM,
         scratch_shapes=[
@@ -405,7 +423,7 @@
         name="attention",
     )(span_order, jnp.stack([ulysses_index, cycle_index]).astype(jnp.int32), query_rows, *mine, *theirs)
     heads = lax.all_to_all(
-        attended.reshape(QH, token_rows, HD), ("ulysses", "blk"), split_axis=0, concat_axis=0, tiled=True
+        attended.reshape(QH, token_rows, HD), ("blk", "ulysses"), split_axis=0, concat_axis=0, tiled=True
     )
     rows = pl.pallas_call(
         lambda *refs: order_heads_kernel(head_order, *refs),

time: 114 us -> 110 us (0.965)
  matrix products: 11.5 us -> 0 us
  local copies, waits for them, and re-layouts: 5.79 us -> 12.6 us
  Pallas kernels: 8.44 us -> 13.7 us
  waiting for transfers between devices: 39.3 us -> 34.7 us
  blocking collectives: 22.1 us -> 20.8 us
    dot_general x7 -> x0, matrix products: 11.5 us -> none  [add_terms(): term = jnp.dot(left, rows, preferred_element_type=jnp.float32)]
    unnamed x10 -> x30, local copies, waits for them, and re-layouts: 3.3 us -> 11 us
    pallas_call x1 -> x3, Pallas kernels: 5.59 us -> 10.6 us  [the longest x1 6.1 us: whole_cycle_shards(): pl.pallas_call(attention_kernel, out_shape=jax.ShapeDtypeStruct((cycle_si...]
    ppermute x6, waiting for transfers between devices: 28 us -> 23.7 us  [ahead(): lax.ppermute(block, 'blk', [(i, (i + distance) % cycle_size) for i in ran...]
    all_to_all x1, blocking collectives: 22.1 us -> 20.8 us  [whole_cycle_shards(): lax.all_to_all(attended.reshape(QH, token_rows, HD), ('blk', 'ulysses'),...]
  transfers between devices with their start and end apart: 18 -> 18, of which waited for: 9 -> 9; matrix products, arithmetic and copies ran while one was open for 17% -> 7% of each run, Pallas kernels for 2% -> 6%
where the time goes in v3:
time: 110 us; the launch traced here: 109 us
  waiting for transfers between devices  34.7 us (32%)
  blocking collectives  20.8 us (19%)
  starting transfers between devices  20.6 us (19%)
  Pallas kernels  13.7 us (12%)
  local copies, waits for them, and re-layouts  12.6 us (11%)
  other arithmetic  6.58 us (6%)
    ppermute x6, waiting for transfers between devices, ahead(): lax.ppermute(block, 'blk', [(i, (i + distance) % cycle_size) for i in ran...  23.7 us
    all_to_all x1, blocking collectives, whole_cycle_shards(): lax.all_to_all(attended.reshape(QH, token_rows, HD), ('blk', 'ulysses'),...  20.8 us
    unnamed x30, local copies, waits for them, and re-layouts  11 us
    ppermute x6, starting transfers between devices, ahead(): lax.ppermute(block, 'blk', [(i, (i + distance) % cycle_size) for i in ran...  8.85 us
    ppermute x4, waiting for transfers between devices, across(): lax.ppermute(block, 'dp', [(i, dp_size - 1 - i) for i in range(dp_size)])  8.52 us
    pallas_call x1, Pallas kernels, whole_cycle_shards(): pl.pallas_call(attention_kernel, out_shape=jax.ShapeDtypeStruct((cycle_si...  6.1 us
    ppermute x4, starting transfers between devices, across(): lax.ppermute(block, 'dp', [(i, dp_size - 1 - i) for i in range(dp_size)])  5.13 us
    all_to_all x1, starting transfers between devices, whole_cycle_shards(): lax.all_to_all(rotated, ('blk', 'ulysses'), split_axis=0, concat_axis=0,...  4.63 us
  transfers between devices with their start and end apart: 18, of which 9 were waited for; matrix products, arithmetic and copies ran while one was open for 7% of the time, Pallas kernels for 6%

profile of v3, /device:TPU:0, one launch (start us, length us, event | category | flops | bytes accessed | tf_op | source)
XLA Modules:
  0.0 109.2 jit_solution(4272627827906156682)
XLA Ops:
  0.0 1.6 %copy-done = bf16[512,2048]{1,0:T(8,128)(2,1)S(1)} copy-done((bf16[512,2048]{1,0:T(8,128)(2,1)S(1)}, bf16[512,2048]{1,0:T(8,128)(2,1)}, u32[]{:S(2)}) %copy-start) | copy-done | bytes 2097176
  1.6 3.1 %collective-permute-start.1 = (bf16[512,512]{1,0:T(8,128)(2,1)S(1)}, bf16[512,512]{1,0:T(8,128)(2,1)S(1)}, u32[]{:S(2)}, u32[]{:S(2)}) collective-permute-start(bf16[512,512]{1,0:T(8,128)(2,1)S(1)} %constant_dynamic-slice_fusion.1.refs_0_), channel_id=1, source_target_pairs={{0,1},{1,2},{2,3},{3,0},{4,5},{5,6},{6,7},{7,4},{8,9},{9,10},{10,1... | collective-permute-start | bytes 1572872 | tf_op jit(solution)/shard_map/ppermute | solution.py:338
  4.7 1.5 %collective-permute-start.2 = (bf16[512,512]{1,0:T(8,128)(2,1)S(1)}, bf16[512,512]{1,0:T(8,128)(2,1)}, u32[]{:S(2)}, u32[]{:S(2)}) collective-permute-start(bf16[512,512]{1,0:T(8,128)(2,1)S(1)} %constant_dynamic-slice_fusion.1.refs_0_), channel_id=1, source_target_pairs={{0,16},{16,0},{1,17},{17,1},{2,18},{18,2},{3,19},{19,3},{4,20},{20... | collective-permute-start | bytes 1572872 | tf_op jit(solution)/shard_map/ppermute | solution.py:341
  6.2 1.5 %collective-permute-start = (bf16[128,4096]{1,0:T(8,128)(2,1)}, bf16[128,4096]{1,0:T(8,128)(2,1)}, u32[]{:S(2)}, u32[]{:S(2)}) collective-permute-start(bf16[128,4096]{1,0:T(8,128)(2,1)} %bitcast.2), channel_id=1, source_target_pairs={{0,8},{4,12},{8,0},{12,4},{1,9},{5,13},{9,1},{13,5},{2,10},{6,14},... | collective-permute-start | bytes 3145736 | tf_op jit(solution)/shard_map/ppermute | solution.py:194
  9.1 1.4 %fusion.5 = f32[512]{0:T(512)S(1)} fusion(s32[]{:T(128)} %bitcast.6, s32[]{:T(128)} %bitcast.5, s32[4]{0:T(128)S(1)} %xor_multiply_fusion), kind=kLoop, calls=%fused_computation.17 | loop fusion | flops 8704 | bytes 2072 | tf_op jit(solution)/shard_map/convert_element_type | solution.py:45
  15.2 3.4 %collective-permute-done.1.refs_2_ = bf16[512,512]{1,0:T(8,128)(2,1)S(1)} collective-permute-done((bf16[512,512]{1,0:T(8,128)(2,1)S(1)}, bf16[512,512]{1,0:T(8,128)(2,1)S(1)}, u32[]{:S(2)}, u32[]{:S(2)}) %collective-permute-start.1) | collective-permute-done | bytes 524320 | tf_op jit(solution)/shard_map/ppermute | solution.py:338
  19.8 1.5 %collective-permute-start.4 = (bf16[512,512]{1,0:T(8,128)(2,1)S(1)}, bf16[512,512]{1,0:T(8,128)(2,1)S(1)}, u32[]{:S(2)}, u32[]{:S(2)}) collective-permute-start(bf16[512,512]{1,0:T(8,128)(2,1)S(1)} %collective-permute-done.1.refs_2_), channel_id=1, source_target_pairs={{0,16},{16,0},{1,17},{17,1},{2,18},{18,2},{3,19},{19,3},{4,20},{20... | collective-permute-start | bytes 1572872 | tf_op jit(solution)/shard_map/ppermute | solution.py:341
  22.1 11.5 %collective-permute-done.3.refs_4_ = bf16[512,512]{1,0:T(8,128)(2,1)S(1)} collective-permute-done((bf16[512,512]{1,0:T(8,128)(2,1)S(1)}, bf16[512,512]{1,0:T(8,128)(2,1)S(1)}, u32[]{:S(2)}, u32[]{:S(2)}) %collective-permute-start.3) | collective-permute-done | bytes 524320 | tf_op jit(solution)/shard_map/ppermute | solution.py:338
  36.6 1.6 %collective-permute-done.8 = bf16[128,4096]{1,0:T(8,128)(2,1)} collective-permute-done((bf16[128,4096]{1,0:T(8,128)(2,1)}, bf16[128,4096]{1,0:T(8,128)(2,1)}, u32[]{:S(2)}, u32[]{:S(2)}) %collective-permute-start.8) | collective-permute-done | bytes 1048608 | tf_op jit(solution)/shard_map/ppermute | solution.py:194
  38.2 2.4 %pad_maximum_fusion.hidden_ref = bf16[512,4096]{1,0:T(8,128)(2,1)S(1)} fusion(bf16[128,4096]{1,0:T(8,128)(2,1)} %collective-permute-done.8, bf16[128,4096]{1,0:T(8,128)(2,1)} %collective-permute-done, bf16[128,4096]{1,0:T(8,128)(2,1)} %collective-permute-done.7, bf16[128,4096]{1,0:T(8,128)(2,1)} %bitcast.2), kind=kLoop, calls=%fused_computation | loop fusion | flops 16777216 | bytes 8388608 | tf_op jit(solution)/shard_map/concatenate | solution.py:381
  41.7 2.6 %terms.2.refs_2_ = f32[512,512]{1,0:T(8,128)S(1)} custom-call(s32[5]{0:T(128)S(1)} %stack.44.rows_ref, bf16[512,4096]{1,0:T(8,128)(2,1)S(1)} %pad_maximum_fusion.hidden_ref, bf16[512,512]{1,0:T(8,128)(2,1)S(1)} %copy-done.4, bf16[512,512]{1,0:T(8,128)(2,1)} %collective-permute-done.2.refs_1_, bf16[512,512]{1,0:T(8,128)(2,1)S(1)} %copy-done.8, ...), custom_call_target="tpu_custom_call" | custom-call | tf_op jit(solution)/shard_map/terms/pallas_call | solution.py:353
  44.3 2.0 %copy-done.1 = bf16[512,4096]{1,0:T(8,128)(2,1)} copy-done((bf16[512,4096]{1,0:T(8,128)(2,1)}, bf16[512,4096]{1,0:T(8,128)(2,1)S(1)}, u32[]{:S(2)}) %copy-start.1) | copy-done | bytes 4194328
  46.2 4.6 %all-to-all-start = ((bf16[16,128,128]{2,1,0:T(8,128)(2,1)}), bf16[16,128,128]{2,1,0:T(8,128)(2,1)}, u32[]{:S(2)}, u32[]{:S(2)}) async-start(bf16[16,128,128]{2,1,0:T(8,128)(2,1)} %copy-done.5), calls=%async_computation | async-start | bytes 1048576 | tf_op jit(solution)/shard_map/all_to_all | solution.py:384
  50.9 1.9 %collective-permute-done.5.refs_1_ = bf16[512,512]{1,0:T(8,128)(2,1)} collective-permute-done((bf16[512,512]{1,0:T(8,128)(2,1)}, bf16[512,512]{1,0:T(8,128)(2,1)}, u32[]{:S(2)}, u32[]{:S(2)}) %collective-permute-start.5) | collective-permute-done | bytes 524320 | tf_op jit(solution)/shard_map/ppermute | solution.py:338
  53.6 2.2 %copy-done.2 = bf16[512,4096]{1,0:T(8,128)(2,1)S(1)} copy-done((bf16[512,4096]{1,0:T(8,128)(2,1)S(1)}, bf16[512,4096]{1,0:T(8,128)(2,1)}, u32[]{:S(2)}) %copy-start.2) | copy-done | bytes 4194328
  55.8 2.0 %terms.3.total_ref = f32[512,512]{1,0:T(8,128)S(1)} custom-call(s32[2]{0:T(128)S(1)} %pad_add_fusion.1.rows_ref, bf16[512,4096]{1,0:T(8,128)(2,1)S(1)} %copy-done.2, bf16[512,512]{1,0:T(8,128)(2,1)} %collective-permute-done.6.refs_0_, bf16[512,512]{1,0:T(8,128)(2,1)} %collective-permute-done.5.refs_1_, f32[512,512]{1,0:T(8,128)S(1)} %terms.2.refs_2_), custom_call_target="tpu_custom_call" | custom-call | tf_op jit(solution)/shard_map/terms/pallas_call | solution.py:353
  57.8 8.5 %collective-permute-done.9.chunk_ref = bf16[512,512]{1,0:T(8,128)(2,1)} collective-permute-done((bf16[512,512]{1,0:T(8,128)(2,1)}, bf16[512,512]{1,0:T(8,128)(2,1)}, u32[]{:S(2)}, u32[]{:S(2)}) %collective-permute-start.9) | collective-permute-done | bytes 524320 | tf_op jit(solution)/shard_map/ppermute | solution.py:341
  66.4 1.9 %pair_rope.1 = (bf16[512,128]{1,0:T(8,128)(2,1)S(1)}, bf16[512,128]{1,0:T(8,128)(2,1)S(1)}, bf16[512,128]{1,0:T(8,128)(2,1)S(1)}, bf16[512,128]{1,0:T(8,128)(2,1)S(1)}) custom-call(s32[1]{0:T(128)} %bitcast.1.block_ref, f32[512,512]{1,0:T(8,128)S(1)} %terms.3.total_ref, bf16[512,512]{1,0:T(8,128)(2,1)S(1)} %constant_dynamic-slice_fusion.hidden_ref, ...), custom_call_target="tpu_custom_call" | custom-call | tf_op jit(solution)/shard_map/pair_rope/pallas_call | solution.py:397
  69.1 2.4 %collective-permute-start.11 = (bf16[512,128]{1,0:T(8,128)(2,1)S(1)}, bf16[512,128]{1,0:T(8,128)(2,1)S(1)}, u32[]{:S(2)}, u32[]{:S(2)}) collective-permute-start(bf16[512,128]{1,0:T(8,128)(2,1)S(1)} %get-tuple-element.57), channel_id=1, source_target_pairs={{0,2},{1,3},{2,0},{3,1},{4,6},{5,7},{6,4},{7,5},{8,10},{9,11},{10,... | collective-permute-start | bytes 393224 | tf_op jit(solution)/shard_map/ppermute | solution.py:338
  71.5 1.5 %collective-permute-start.12 = (bf16[512,128]{1,0:T(8,128)(2,1)S(1)}, bf16[512,128]{1,0:T(8,128)(2,1)S(1)}, u32[]{:S(2)}, u32[]{:S(2)}) collective-permute-start(bf16[512,128]{1,0:T(8,128)(2,1)S(1)} %get-tuple-element.58), channel_id=1, source_target_pairs={{0,3},{1,0},{2,1},{3,2},{4,7},{5,4},{6,5},{7,6},{8,11},{9,8},{10,9... | collective-permute-start | bytes 393224 | tf_op jit(solution)/shard_map/ppermute | solution.py:338
  72.9 3.7 %collective-permute-done.10.refs_1_ = bf16[512,128]{1,0:T(8,128)(2,1)S(1)} collective-permute-done((bf16[512,128]{1,0:T(8,128)(2,1)S(1)}, bf16[512,128]{1,0:T(8,128)(2,1)S(1)}, u32[]{:S(2)}, u32[]{:S(2)}) %collective-permute-start.10) | collective-permute-done | bytes 131104 | tf_op jit(solution)/shard_map/ppermute | solution.py:338
  76.6 3.2 %collective-permute-done.11.refs_2_ = bf16[512,128]{1,0:T(8,128)(2,1)S(1)} collective-permute-done((bf16[512,128]{1,0:T(8,128)(2,1)S(1)}, bf16[512,128]{1,0:T(8,128)(2,1)S(1)}, u32[]{:S(2)}, u32[]{:S(2)}) %collective-permute-start.11) | collective-permute-done | bytes 131104 | tf_op jit(solution)/shard_map/ppermute | solution.py:338
  81.3 6.1 %attention.1 = bf16[4,4,128,128]{3,2,1,0:T(8,128)(2,1)S(1)} custom-call(s32[1,8]{1,0:T(1,128)S(1)} %copy-done.14, s32[2]{0:T(128)S(1)} %pad_add_fusion.place_ref, bf16[4,4,128,128]{3,2,1,0:T(8,128)(2,1)} %bitcast.14.query_ref, bf16[512,128]{1,0:T(8,128)(2,1)S(1)} %get-tuple-element.55.refs_0_, bf16[512,128]{1,0:T(8,128)(2,1)S(1)} %collective-permute-done.10.refs_1_, ...), custom_call_target="tpu_custom_call" | custom-call | tf_op jit(solution)/shard_map/attention/pallas_call | solution.py:413
  87.4 20.8 %all_to_all.10.refs_0_ = bf16[16,128,128]{2,1,0:T(8,128)(2,1)S(1)} all-to-all(bf16[16,128,128]{2,1,0:T(8,128)(2,1)S(1)} %bitcast.23), channel_id=1, replica_groups=mesh['dp'=2,'ulysses'=4,'blk'=4] {'blk','ulysses'}, dimensions={0} | all-to-all | bytes 1048576 | tf_op jit(solution)/shard_map/all_to_all | solution.py:425
  (63 shorter events, 16.3 us)
Async XLA Ops:
  1.6 36.6 %copy-start.3 = (bf16[512,512]{1,0:T(8,128)(2,1)}, bf16[512,512]{1,0:T(8,128)(2,1)S(1)}, u32[]{:S(2)}) copy-start(bf16[512,512]{1,0:T(8,128)(2,1)S(1)} %constant_dynamic-slice_fusion.1.refs_0_) | copy-start | bytes 1572868
  1.6 17.0 %collective-permute-start.1 = (bf16[512,512]{1,0:T(8,128)(2,1)S(1)}, bf16[512,512]{1,0:T(8,128)(2,1)S(1)}, u32[]{:S(2)}, u32[]{:S(2)}) collective-permute-start(bf16[512,512]{1,0:T(8,128)(2,1)S(1)} %constant_dynamic-slice_fusion.1.refs_0_), channel_id=1, source_target_pairs={{0,1},{1,2},{2,3},{3,0},{4,5},{5,6},{6,7},{7,4},{8,9},{9,10},{10,1... | collective-permute-start | bytes 1572872 | tf_op jit(solution)/shard_map/ppermute | solution.py:338
  4.7 14.0 %collective-permute-start.2 = (bf16[512,512]{1,0:T(8,128)(2,1)S(1)}, bf16[512,512]{1,0:T(8,128)(2,1)}, u32[]{:S(2)}, u32[]{:S(2)}) collective-permute-start(bf16[512,512]{1,0:T(8,128)(2,1)S(1)} %constant_dynamic-slice_fusion.1.refs_0_), channel_id=1, source_target_pairs={{0,16},{16,0},{1,17},{17,1},{2,18},{18,2},{3,19},{19,3},{4,20},{20... | collective-permute-start | bytes 1572872 | tf_op jit(solution)/shard_map/ppermute | solution.py:341
  6.2 29.0 %collective-permute-start = (bf16[128,4096]{1,0:T(8,128)(2,1)}, bf16[128,4096]{1,0:T(8,128)(2,1)}, u32[]{:S(2)}, u32[]{:S(2)}) collective-permute-start(bf16[128,4096]{1,0:T(8,128)(2,1)} %bitcast.2), channel_id=1, source_target_pairs={{0,8},{4,12},{8,0},{12,4},{1,9},{5,13},{9,1},{13,5},{2,10},{6,14},... | collective-permute-start | bytes 3145736 | tf_op jit(solution)/shard_map/ppermute | solution.py:194
  18.7 14.9 %collective-permute-start.3 = (bf16[512,512]{1,0:T(8,128)(2,1)S(1)}, bf16[512,512]{1,0:T(8,128)(2,1)S(1)}, u32[]{:S(2)}, u32[]{:S(2)}) collective-permute-start(bf16[512,512]{1,0:T(8,128)(2,1)S(1)} %collective-permute-done.1.refs_2_), channel_id=1, source_target_pairs={{0,1},{1,2},{2,3},{3,0},{4,5},{5,6},{6,7},{7,4},{8,9},{9,10},{10,1... | collective-permute-start | bytes 1572872 | tf_op jit(solution)/shard_map/ppermute | solution.py:338
  19.8 13.8 %collective-permute-start.4 = (bf16[512,512]{1,0:T(8,128)(2,1)S(1)}, bf16[512,512]{1,0:T(8,128)(2,1)S(1)}, u32[]{:S(2)}, u32[]{:S(2)}) collective-permute-start(bf16[512,512]{1,0:T(8,128)(2,1)S(1)} %collective-permute-done.1.refs_2_), channel_id=1, source_target_pairs={{0,16},{16,0},{1,17},{17,1},{2,18},{18,2},{3,19},{19,3},{4,20},{20... | collective-permute-start | bytes 1572872 | tf_op jit(solution)/shard_map/ppermute | solution.py:341
  22.1 14.5 %collective-permute-start.7 = (bf16[128,4096]{1,0:T(8,128)(2,1)}, bf16[128,4096]{1,0:T(8,128)(2,1)}, u32[]{:S(2)}, u32[]{:S(2)}) collective-permute-start(bf16[128,4096]{1,0:T(8,128)(2,1)} %bitcast.2), channel_id=1, source_target_pairs={{0,4},{4,0},{8,12},{12,8},{1,5},{5,1},{9,13},{13,9},{2,6},{6,2},{1... | collective-permute-start | bytes 3145736 | tf_op jit(solution)/shard_map/ppermute | solution.py:194
  35.2 3.0 %collective-permute-start.8 = (bf16[128,4096]{1,0:T(8,128)(2,1)}, bf16[128,4096]{1,0:T(8,128)(2,1)}, u32[]{:S(2)}, u32[]{:S(2)}) collective-permute-start(bf16[128,4096]{1,0:T(8,128)(2,1)} %collective-permute-done), channel_id=1, source_target_pairs={{0,4},{4,0},{8,12},{12,8},{1,5},{5,1},{9,13},{13,9},{2,6},{6,2},{1... | collective-permute-start | bytes 3145736 | tf_op jit(solution)/shard_map/ppermute | solution.py:194
  35.3 5.4 %copy-start.8 = (bf16[512,512]{1,0:T(8,128)(2,1)S(1)}, bf16[512,512]{1,0:T(8,128)(2,1)}, u32[]{:S(2)}) copy-start(bf16[512,512]{1,0:T(8,128)(2,1)} %copy-done.7) | copy-start | bytes 1572868
  35.3 5.4 %copy-start.10 = (bf16[512,512]{1,0:T(8,128)(2,1)S(1)}, bf16[512,512]{1,0:T(8,128)(2,1)}, u32[]{:S(2)}) copy-start(bf16[512,512]{1,0:T(8,128)(2,1)} %copy-done.9) | copy-start | bytes 1572868
  35.3 5.4 %copy-start.12 = (bf16[512,512]{1,0:T(8,128)(2,1)S(1)}, bf16[512,512]{1,0:T(8,128)(2,1)}, u32[]{:S(2)}) copy-start(bf16[512,512]{1,0:T(8,128)(2,1)} %copy-done.11) | copy-start | bytes 1572868
  35.3 17.5 %collective-permute-start.6 = (bf16[512,512]{1,0:T(8,128)(2,1)}, bf16[512,512]{1,0:T(8,128)(2,1)}, u32[]{:S(2)}, u32[]{:S(2)}) collective-permute-start(bf16[512,512]{1,0:T(8,128)(2,1)} %copy-done.9), channel_id=1, source_target_pairs={{0,16},{16,0},{1,17},{17,1},{2,18},{18,2},{3,19},{19,3},{4,20},{20... | collective-permute-start | bytes 1572872 | tf_op jit(solution)/shard_map/ppermute | solution.py:341
  36.6 16.2 %collective-permute-start.5 = (bf16[512,512]{1,0:T(8,128)(2,1)}, bf16[512,512]{1,0:T(8,128)(2,1)}, u32[]{:S(2)}, u32[]{:S(2)}) collective-permute-start(bf16[512,512]{1,0:T(8,128)(2,1)} %copy-done.9), channel_id=1, source_target_pairs={{0,1},{1,2},{2,3},{3,0},{4,5},{5,6},{6,7},{7,4},{8,9},{9,10},{10,1... | collective-permute-start | bytes 1572872 | tf_op jit(solution)/shard_map/ppermute | solution.py:338
  46.2 22.0 %all-to-all-start = ((bf16[16,128,128]{2,1,0:T(8,128)(2,1)}), bf16[16,128,128]{2,1,0:T(8,128)(2,1)}, u32[]{:S(2)}, u32[]{:S(2)}) async-start(bf16[16,128,128]{2,1,0:T(8,128)(2,1)} %copy-done.5), calls=%async_computation | async-start | bytes 1048576 | tf_op jit(solution)/shard_map/all_to_all | solution.py:384
  52.8 13.6 %collective-permute-start.9 = (bf16[512,512]{1,0:T(8,128)(2,1)}, bf16[512,512]{1,0:T(8,128)(2,1)}, u32[]{:S(2)}, u32[]{:S(2)}) collective-permute-start(bf16[512,512]{1,0:T(8,128)(2,1)} %collective-permute-done.5.refs_1_), channel_id=1, source_target_pairs={{0,16},{16,0},{1,17},{17,1},{2,18},{18,2},{3,19},{19,3},{4,20},{20... | collective-permute-start | bytes 1572872 | tf_op jit(solution)/shard_map/ppermute | solution.py:341
  55.8 10.5 %copy-start.6 = (f32[512,128]{1,0:T(8,128)S(1)}, f32[512,128]{1,0:T(8,128)}, u32[]{:S(2)}) copy-start(f32[512,128]{1,0:T(8,128)} %get-tuple-element.48.sine_ref) | copy-start | bytes 786436
  55.8 25.5 %copy-start.14 = (s32[1,8]{1,0:T(1,128)S(1)}, s32[1,8]{1,0:T(1,128)}, u32[]{:S(2)}) copy-start(s32[1,8]{1,0:T(1,128)} %order_ref.1) | copy-start | bytes 100
  68.3 8.3 %collective-permute-start.10 = (bf16[512,128]{1,0:T(8,128)(2,1)S(1)}, bf16[512,128]{1,0:T(8,128)(2,1)S(1)}, u32[]{:S(2)}, u32[]{:S(2)}) collective-permute-start(bf16[512,128]{1,0:T(8,128)(2,1)S(1)} %get-tuple-element.56), channel_id=1, source_target_pairs={{0,1},{1,2},{2,3},{3,0},{4,5},{5,6},{6,7},{7,4},{8,9},{9,10},{10,1... | collective-permute-start | bytes 393224 | tf_op jit(solution)/shard_map/ppermute | solution.py:338
  69.1 10.7 %collective-permute-start.11 = (bf16[512,128]{1,0:T(8,128)(2,1)S(1)}, bf16[512,128]{1,0:T(8,128)(2,1)S(1)}, u32[]{:S(2)}, u32[]{:S(2)}) collective-permute-start(bf16[512,128]{1,0:T(8,128)(2,1)S(1)} %get-tuple-element.57), channel_id=1, source_target_pairs={{0,2},{1,3},{2,0},{3,1},{4,6},{5,7},{6,4},{7,5},{8,10},{9,11},{10,... | collective-permute-start | bytes 393224 | tf_op jit(solution)/shard_map/ppermute | solution.py:338
  71.5 8.3 %collective-permute-start.12 = (bf16[512,128]{1,0:T(8,128)(2,1)S(1)}, bf16[512,128]{1,0:T(8,128)(2,1)S(1)}, u32[]{:S(2)}, u32[]{:S(2)}) collective-permute-start(bf16[512,128]{1,0:T(8,128)(2,1)S(1)} %get-tuple-element.58), channel_id=1, source_target_pairs={{0,3},{1,0},{2,1},{3,2},{4,7},{5,4},{6,5},{7,6},{8,11},{9,8},{10,9... | collective-permute-start | bytes 393224 | tf_op jit(solution)/shard_map/ppermute | solution.py:338
  72.9 7.4 %collective-permute-start.13 = (bf16[512,128]{1,0:T(8,128)(2,1)S(1)}, bf16[512,128]{1,0:T(8,128)(2,1)S(1)}, u32[]{:S(2)}, u32[]{:S(2)}) collective-permute-start(bf16[512,128]{1,0:T(8,128)(2,1)S(1)} %get-tuple-element.55.refs_0_), channel_id=1, source_target_pairs={{0,4},{4,0},{8,12},{12,8},{1,5},{5,1},{9,13},{13,9},{2,6},{6,2},{1... | collective-permute-start | bytes 393224 | tf_op jit(solution)/shard_map/ppermute | solution.py:194
  76.6 3.8 %collective-permute-start.14 = (bf16[512,128]{1,0:T(8,128)(2,1)S(1)}, bf16[512,128]{1,0:T(8,128)(2,1)S(1)}, u32[]{:S(2)}, u32[]{:S(2)}) collective-permute-start(bf16[512,128]{1,0:T(8,128)(2,1)S(1)} %collective-permute-done.10.refs_1_), channel_id=1, source_target_pairs={{0,4},{4,0},{8,12},{12,8},{1,5},{5,1},{9,13},{13,9},{2,6},{6,2},{1... | collective-permute-start | bytes 393224 | tf_op jit(solution)/shard_map/ppermute | solution.py:194
  79.8 1.3 %collective-permute-start.15 = (bf16[512,128]{1,0:T(8,128)(2,1)S(1)}, bf16[512,128]{1,0:T(8,128)(2,1)S(1)}, u32[]{:S(2)}, u32[]{:S(2)}) collective-permute-start(bf16[512,128]{1,0:T(8,128)(2,1)S(1)} %collective-permute-done.11.refs_2_), channel_id=1, source_target_pairs={{0,4},{4,0},{8,12},{12,8},{1,5},{5,1},{9,13},{13,9},{2,6},{6,2},{1... | collective-permute-start | bytes 393224 | tf_op jit(solution)/shard_map/ppermute | solution.py:194
  79.8 1.5 %collective-permute-start.16 = (bf16[512,128]{1,0:T(8,128)(2,1)S(1)}, bf16[512,128]{1,0:T(8,128)(2,1)S(1)}, u32[]{:S(2)}, u32[]{:S(2)}) collective-permute-start(bf16[512,128]{1,0:T(8,128)(2,1)S(1)} %collective-permute-done.12.refs_3_), channel_id=1, source_target_pairs={{0,4},{4,0},{8,12},{12,8},{1,5},{5,1},{9,13},{13,9},{2,6},{6,2},{1... | collective-permute-start | bytes 393224 | tf_op jit(solution)/shard_map/ppermute | solution.py:194
  (9 other events, 11.1 us)

commit v4 on v3

--- a/solution.py
+++ b/solution.py
@@ -6,6 +6,7 @@
 from jax import lax
 from jax.experimental import pallas as pl
 from jax.experimental.pallas import tpu as pltpu
+from jax.sharding import Mesh
 from jax.sharding import PartitionSpec as P
 
 KVH = 8
@@ -15,6 +16,7 @@
 
 
 LOG_BASE = math.log(500000.0)
+LOG2_E = math.log2(math.e)
 
 
 def from_behind(block, axis, distance):
@@ -189,9 +191,9 @@
     return token_output[None]
 
 
-def swap(block, distance):
-    size = lax.axis_size("ulysses")
-    return lax.ppermute(block, "ulysses", [(i, i ^ distance) for i in range(size)])
+def exchange(block, axis, distance):
+    size = lax.axis_size(axis)
+    return lax.ppermute(block, axis, [(i, i ^ distance) for i in range(size)])
 
 
 def wide_tables(positions, yarn_divisor):
@@ -204,106 +206,171 @@
     return head * cosine + pltpu.roll(head, HD // 2, 1) * signed_sine
 
 
-def query_rope_kernel(head_order, query_ref, cosine_ref, sine_ref, out_ref):
+def query_rope_kernel(pair_order, query_ref, cosine_ref, sine_ref, out_ref):
     cosine, sine = cosine_ref[...], sine_ref[...]
-    for place, head in enumerate(head_order):
-        rows = query_ref[:, head * HD : (head + 1) * HD].astype(jnp.float32)
-        out_ref[place] = rope_head(rows, cosine, sine).astype(jnp.bfloat16)
-
-
-def terms_kernel(count, rows_ref, hidden_ref, *refs):
-    out_ref = refs[-1]
-    total = refs[count][...] if len(refs) > count + 1 else None
-    for index, chunk_ref in enumerate(refs[:count]):
-        depth = chunk_ref.shape[0]
+    width = out_ref.shape[2]
+    for place, pair in enumerate(pair_order):
+        for start in range(0, width, HD):
+            column = pair * width + start
+            rows = query_ref[:, column : column + HD].astype(jnp.float32)
+            out_ref[place, :, start : start + HD] = rope_head(rows, cosine, sine).astype(jnp.bfloat16)
+
+
+def load_terms(rows_ref, slot_refs, piece_refs, hidden_rows, pieces, sems):
+    token_rows = slot_refs[0].shape[0]
+    copies = []
+    for index, piece_ref in enumerate(piece_refs):
+        depth = piece_ref.shape[0]
         columns = pl.ds(pl.multiple_of(rows_ref[index], depth), depth)
-        term = jnp.dot(hidden_ref[:, columns], chunk_ref[...], preferred_element_type=jnp.float32)
+        started = [pltpu.make_async_copy(piece_ref, pieces.at[index], sems.at[index, 0])]
+        for slot, slot_ref in enumerate(slot_refs):
+            rows = hidden_rows.at[index, pl.ds(slot * token_rows, token_rows)]
+            started.append(pltpu.make_async_copy(slot_ref.at[:, columns], rows, sems.at[index, slot + 1]))
+        for copy in started:
+            copy.start()
+        copies.append(started)
+    return copies
+
+
+def terms_kernel(slots, count, rows_ref, *refs):
+    slot_refs, piece_refs = refs[:slots], refs[slots : slots + count]
+    out_ref, next_hidden_ref, hidden_rows, pieces, sems, next_sems = refs[slots + count :]
+    copies = load_terms(rows_ref, slot_refs, piece_refs, hidden_rows, pieces, sems)
+    token_rows, depth = slot_refs[0].shape[0], piece_refs[0].shape[0]
+    columns = pl.ds(pl.multiple_of(rows_ref[count], depth), depth)
+    next_copies = [
+        pltpu.make_async_copy(
+            slot_ref.at[:, columns],
+            next_hidden_ref.at[pl.ds(slot * token_rows, token_rows)],
+            next_sems.at[slot],
+        )
+        for slot, slot_ref in enumerate(slot_refs)
+    ]
+    for copy in next_copies:
+        copy.start()
+    total = None
+    for index, started in enumerate(copies):
+        for copy in started:
+            copy.wait()
+        term = jnp.dot(hidden_rows[index], pieces[index], preferred_element_type=jnp.float32)
         total = term if total is None else total + term
     out_ref[...] = total
-
-
-def pair_rope_kernel(block_ref, total_ref, hidden_ref, chunk_ref, cosine_ref, sine_ref, *refs):
+    for copy in next_copies:
+        copy.wait()
+
+
+def pair_rope_kernel(place_ref, total_ref, hidden_ref, piece_ref, cosine_ref, sine_ref, *refs):
     out_refs, sum_ref = refs[:-1], refs[-1]
     sum_ref[...] = total_ref[...] + jnp.dot(
-        hidden_ref[...], chunk_ref[...], preferred_element_type=jnp.float32
+        hidden_ref[...], piece_ref[...], preferred_element_type=jnp.float32
     )
     cosine, sine = cosine_ref[...], sine_ref[...]
     for distance, out_ref in enumerate(out_refs):
-        head = lax.rem(block_ref[0] + distance, len(out_refs))
+        head = lax.rem(place_ref[1] + distance, len(out_refs))
         rows = sum_ref[:, pl.ds(pl.multiple_of(head * HD, HD), HD)]
         out_ref[...] = rope_head(rows, cosine, sine).astype(jnp.bfloat16)
 
 
-def order_heads_kernel(head_order, block_ref, out_ref):
-    for place, head in enumerate(head_order):
-        out_ref[:, head * HD : (head + 1) * HD] = block_ref[place]
+def order_heads_kernel(place_ref, *refs):
+    out_ref = refs[-1]
+    blocks = (len(refs) - 1) // 2
+    chip, block_here = place_ref[0] // 2, place_ref[1]
+    width = refs[0].shape[-1]
+    for distance in range(blocks):
+        block = lax.rem(block_here + blocks - distance, blocks)
+        near, far = refs[distance], refs[blocks + distance]
+        for source, rows in ((chip, near[...] if distance == 0 else near[0]), (1 - chip, far[...])):
+            pair = source * blocks + block
+            out_ref[:, pl.ds(pl.multiple_of(pair * width, width), width)] = rows
 
 
 def attention_kernel(order_ref, place_ref, query_ref, *refs):
     spans = order_ref.shape[1]
     blocks = spans // 2
     mine_refs, theirs_refs = refs[:blocks], refs[blocks : 2 * blocks]
-    out_ref, key_rows, value_rows = refs[2 * blocks :]
-    sources, token_rows = query_ref.shape[1:3]
-    per_span = sources // 2
-    span_rows = per_span * token_rows
+    near_ref, far_ref, *both_refs = refs[2 * blocks : 3 * blocks + 1]
+    key_rows, value_rows, out_rows = refs[3 * blocks + 1 :]
+    token_rows = query_ref.shape[1]
+    span_rows = 2 * token_rows
     place, block_here = place_ref[0], place_ref[1]
-    keys_here = place % 2 == 0
+    chip, core = place // 2, place % 2
     for distance in range(blocks):
         block = lax.rem(block_here + blocks - distance, blocks)
         for half in range(2):
             first = order_ref[0, 2 * block + half] * span_rows
-            for part in range(per_span):
-                slot = jnp.bitwise_xor(half * per_span + part, place)
+            for part in range(2):
+                slot = jnp.bitwise_xor(half * 2 + part, place)
                 other = jnp.bitwise_xor(slot, 1)
                 mine = mine_refs[distance][pl.ds(pl.multiple_of(slot * token_rows, token_rows), token_rows), :]
                 theirs = theirs_refs[distance][
                     pl.ds(pl.multiple_of(other * token_rows, token_rows), token_rows), :
                 ]
                 rows = pl.ds(pl.multiple_of(first + part * token_rows, token_rows), token_rows)
-                key_rows[rows, :] = jnp.where(keys_here, mine, theirs)
-                value_rows[rows, :] = jnp.where(keys_here, theirs, mine)
+                key_rows[rows, :] = jnp.where(core == 0, mine, theirs)
+                value_rows[rows, :] = jnp.where(core == 0, theirs, mine)
     stored = []
     for position in range(spans):
         span = jnp.int32(0)
         for candidate in range(1, spans):
             span = jnp.where(order_ref[0, candidate] == position, candidate, span)
-        stored.append((span // 2, span % 2))
-    row_index = lax.broadcasted_iota(jnp.int32, (span_rows, span_rows), 0)
-    column_index = lax.broadcasted_iota(jnp.int32, (span_rows, span_rows), 1)
-    for position, (block, half) in enumerate(stored):
-        query = query_ref[block, pl.ds(half * per_span, per_span)].reshape(span_rows, HD)
-        reach = (position + 1) * span_rows
-        score = tile_scores(query, key_rows[:reach, :])
-        last = jnp.where(column_index <= row_index, score[:, position * span_rows :], -jnp.inf)
-        score = jnp.concatenate([score[:, : position * span_rows], last], axis=1) if position else last
+        stored.append(span)
+    square = (2 * token_rows, span_rows)
+    row_index = lax.broadcasted_iota(jnp.int32, square, 0) % token_rows + core * token_rows
+    allowed = lax.broadcasted_iota(jnp.int32, square, 1) <= row_index
+
+    def scores(position):
+        pair = query_ref[stored[position]]
+        query = jnp.concatenate([pair[:, :HD], pair[:, HD:]], axis=0)
+        score = lax.dot_general(
+            query,
+            key_rows[: (position + 1) * span_rows, :],
+            (((1,), (1,)), ((), ())),
+            preferred_element_type=jnp.float32,
+        )
+        start = position * span_rows
+        last = jnp.where(allowed, score[:, start:], -jnp.inf)
+        return jnp.concatenate([score[:, :start], last], axis=1) if position else last
+
+    score = scores(spans - 1)
+    for position in reversed(range(spans)):
+        following = scores(position - 1) if position else None
         row_top = jnp.max(score, axis=1, keepdims=True)
-        weights = jnp.exp(score - row_top)
+        weights = jnp.exp2((score - row_top) * (LOG2_E / math.sqrt(HD)))
         denominator = jnp.sum(weights, axis=1, keepdims=True)
         numerator = jnp.dot(
-            weights.astype(jnp.bfloat16), value_rows[:reach, :], preferred_element_type=jnp.float32
+            weights.astype(jnp.bfloat16),
+            value_rows[: (position + 1) * span_rows, :],
+            preferred_element_type=jnp.float32,
         )
         rows = (numerator / denominator).astype(jnp.bfloat16)
-        out_ref[block, pl.ds(half * per_span, per_span)] = rows.reshape(per_span, token_rows, HD)
+        out_rows[stored[position]] = jnp.concatenate([rows[:token_rows], rows[token_rows:]], axis=1)
+        score = following
+    near_ref[...] = out_rows[2 * block_here + chip]
+    far_ref[...] = out_rows[2 * block_here + 1 - chip]
+    for distance, both_ref in enumerate(both_refs, 1):
+        block = lax.rem(block_here + distance, blocks)
+        both_ref[0] = out_rows[2 * block + chip]
+        both_ref[1] = out_rows[2 * block + 1 - chip]
 
 
 VMEM = pl.BlockSpec(memory_space=pltpu.VMEM)
+ANY = pl.BlockSpec(memory_space=pl.ANY)
 SMEM = pl.BlockSpec(memory_space=pltpu.SMEM)
 
 
 def whole_cycle_shards(hidden_in, queries, pair_weight, span_order, yarn_divisor):
     own_hidden = hidden_in[0]
     token_rows = own_hidden.shape[0]
-    ulysses_size, cycle_size = lax.axis_size("ulysses"), lax.axis_size("blk")
+    ulysses_size, cycle_size = 2 * lax.axis_size("chip"), lax.axis_size("blk")
     dp_size = lax.axis_size("dp")
-    ulysses_index, cycle_index = lax.axis_index("ulysses"), lax.axis_index("blk")
+    chip, core = lax.axis_index("chip"), lax.axis_index("core")
+    ulysses_index, cycle_index = 2 * chip + core, lax.axis_index("blk")
     dp_index = lax.axis_index("dp")
     block_rows = token_rows * ulysses_size
     span_rows = block_rows // 2
     shard_rows = pair_weight.shape[0]
     kv_width = KVH * HD
     columns = cycle_size * HD
-    core, chip = ulysses_index % 2, ulysses_index // 2
 
     piece = lax.dynamic_slice(
         pair_weight, (0, core * kv_width + chip * columns), (shard_rows, columns)
@@ -320,20 +387,18 @@
     pair_cosine = jnp.where(core == 0, cosine, 1.0)
     pair_sine = jnp.where(core == 0, sine, 0.0)
 
-    head_order = [
-        (chip_place * cycle_size + block) * 2 + core_place
-        for block in range(cycle_size)
-        for chip_place in range(ulysses_size // 2)
-        for core_place in range(2)
+    pair_order = [
+        place * cycle_size + block for block in range(cycle_size) for place in range(ulysses_size // 2)
     ]
     rotated = pl.pallas_call(
-        lambda *refs: query_rope_kernel(head_order, *refs),
-        out_shape=jax.ShapeDtypeStruct((QH, token_rows, HD), jnp.bfloat16),
+        functools.partial(query_rope_kernel, pair_order),
+        out_shape=jax.ShapeDtypeStruct((len(pair_order), token_rows, 2 * HD), jnp.bfloat16),
         in_specs=[VMEM] * 3,
         out_specs=VMEM,
         compiler_params=pltpu.CompilerParams(vmem_limit_bytes=8 * 1024 * 1024),
         name="query_rope",
     )(queries[0], own_cosine, own_sine)
+
     def ahead(block, distance=1):
         return lax.ppermute(block, "blk", [(i, (i + distance) % cycle_size) for i in range(cycle_size)])
 
@@ -344,55 +409,52 @@
         return (row * cycle_size + jnp.remainder(cycle_index - distance, cycle_size)) * shard_rows
 
     other_row = dp_size - 1 - dp_index
-    far_slots = [swap(own_hidden, distance) for distance in range(2, ulysses_size, 2)]
-    partner = swap(own_hidden, 1)
-    hidden = None
-
-    def add_terms(chunks, total):
-        before = [] if total is None else [total]
-        return pl.pallas_call(
-            functools.partial(terms_kernel, len(chunks)),
-            out_shape=jax.ShapeDtypeStruct((block_rows, columns), jnp.float32),
-            in_specs=[SMEM] + [VMEM] * (1 + len(chunks) + len(before)),
-            out_specs=VMEM,
-            compiler_params=pltpu.CompilerParams(vmem_limit_bytes=16 * 1024 * 1024),
-            name="terms",
-        )(jnp.stack([row for _, row in chunks]), hidden, *(chunk for chunk, _ in chunks), *before)
+    far = exchange(own_hidden, "chip", 1)
+    partner = exchange(own_hidden, "core", 1)
 
     travelling, crossed = piece, across(piece)
-    received = [(piece, first_row(0, dp_index))]
+    received = [piece]
+    firsts = [first_row(0, dp_index)]
+    for distance in range(1, cycle_size):
+        firsts += [first_row(distance - 1, other_row), first_row(distance, dp_index)]
+    rows = jnp.stack([*firsts, first_row(cycle_size - 1, other_row)])
+    place = jnp.stack([ulysses_index, cycle_index]).astype(jnp.int32)
     for distance in range(1, cycle_size - 1):
         travelling = ahead(travelling)
         if distance == 1:
-            rotated, pair_cosine, pair_sine, travelling = lax.optimization_barrier(
-                (rotated, pair_cosine, pair_sine, travelling)
+            rotated, pair_cosine, pair_sine, rows, place, travelling = lax.optimization_barrier(
+                (rotated, pair_cosine, pair_sine, rows, place, travelling)
             )
         travelling, crossed = lax.optimization_barrier((travelling, crossed))
-        received += [
-            (crossed, first_row(distance - 1, other_row)),
-            (travelling, first_row(distance, dp_index)),
-        ]
+        received += [crossed, travelling]
         crossed = across(travelling)
 
-    *far_slots, travelling = lax.optimization_barrier((*far_slots, travelling))
-    slots = [own_hidden, partner]
-    for far in far_slots:
-        slots += [far, swap(far, 1)]
-    hidden = jnp.concatenate(slots, axis=0)
-    total = add_terms(received, None)
-    rotated, total = lax.optimization_barrier((rotated, total))
-    query_rows = lax.all_to_all(rotated, ("blk", "ulysses"), split_axis=0, concat_axis=0, tiled=True)
-    query_rows = query_rows.reshape(cycle_size, ulysses_size, token_rows, HD)
+    far, travelling = lax.optimization_barrier((far, travelling))
+    hidden = [own_hidden, partner, far, exchange(far, "core", 1)]
+    *hidden, rotated = lax.optimization_barrier((*hidden, rotated))
+    query_rows = lax.all_to_all(rotated, ("blk", "chip"), split_axis=0, concat_axis=0, tiled=True)
 
     travelling = ahead(travelling)
-    travelling, crossed, total = lax.optimization_barrier((travelling, crossed, total))
-    received = [
-        (crossed, first_row(cycle_size - 2, other_row)),
-        (travelling, first_row(cycle_size - 1, dp_index)),
-    ]
-    last_piece, last_row = across(travelling), first_row(cycle_size - 1, other_row)
-    total = add_terms(received, total)
-    last_hidden = lax.dynamic_slice(hidden, (0, last_row), (block_rows, shard_rows))
+    travelling, crossed = lax.optimization_barrier((travelling, crossed))
+    received += [crossed, travelling]
+    last_piece = across(travelling)
+    total, last_hidden = pl.pallas_call(
+        functools.partial(terms_kernel, ulysses_size, len(received)),
+        out_shape=[
+            jax.ShapeDtypeStruct((block_rows, columns), jnp.float32),
+            jax.ShapeDtypeStruct((block_rows, shard_rows), jnp.bfloat16),
+        ],
+        in_specs=[SMEM] + [ANY] * (ulysses_size + len(received)),
+        out_specs=[VMEM] * 2,
+        scratch_shapes=[
+            pltpu.VMEM((len(received), block_rows, shard_rows), jnp.bfloat16),
+            pltpu.VMEM((len(received), shard_rows, columns), jnp.bfloat16),
+            pltpu.SemaphoreType.DMA((len(received), ulysses_size + 1)),
+            pltpu.SemaphoreType.DMA((ulysses_size,)),
+        ],
+        compiler_params=pltpu.CompilerParams(vmem_limit_bytes=20 * 1024 * 1024),
+        name="terms",
+    )(rows, *hidden, *received)
     last_piece, total, last_hidden = lax.optimization_barrier((last_piece, total, last_hidden))
     pairs = pl.pallas_call(
         pair_rope_kernel,
@@ -402,52 +464,50 @@
         scratch_shapes=[pltpu.VMEM((block_rows, columns), jnp.float32)],
         compiler_params=pltpu.CompilerParams(vmem_limit_bytes=12 * 1024 * 1024),
         name="pair_rope",
-    )(cycle_index.astype(jnp.int32).reshape(1), total, last_hidden, last_piece, pair_cosine, pair_sine)
+    )(place, total, last_hidden, last_piece, pair_cosine, pair_sine)
     *pairs, query_rows = lax.optimization_barrier((*pairs, query_rows))
-    mine, theirs = [pairs[0]] + [None] * (cycle_size - 1), [swap(pairs[0], 1)] + [None] * (cycle_size - 1)
-    for distance in sorted(range(1, cycle_size), key=lambda d: -min(d, cycle_size - d)):
+    far_first = sorted(range(1, cycle_size), key=lambda distance: -min(distance, cycle_size - distance))
+    mine, theirs = {0: pairs[0]}, {0: exchange(pairs[0], "core", 1)}
+    for distance in far_first:
         mine[distance] = ahead(pairs[distance], distance)
-        theirs[distance] = swap(mine[distance], 1)
+        theirs[distance] = exchange(mine[distance], "core", 1)
+    in_order = range(cycle_size)
 
     sequence_rows = cycle_size * block_rows
-    attended = pl.pallas_call(
+    one = jax.ShapeDtypeStruct((token_rows, 2 * HD), jnp.bfloat16)
+    both = jax.ShapeDtypeStruct((2, token_rows, 2 * HD), jnp.bfloat16)
+    near, far, *rest = pl.pallas_call(
         attention_kernel,
-        out_shape=jax.ShapeDtypeStruct((cycle_size, ulysses_size, token_rows, HD), jnp.bfloat16),
+        out_shape=[one, one] + [both] * (cycle_size - 1),
         in_specs=[SMEM, SMEM] + [VMEM] * (1 + 2 * cycle_size),
-        out_specs=VMEM,
+        out_specs=[VMEM] * (cycle_size + 1),
         scratch_shapes=[
             pltpu.VMEM((sequence_rows, HD), jnp.bfloat16),
             pltpu.VMEM((sequence_rows, HD), jnp.bfloat16),
+            pltpu.VMEM((len(pair_order), token_rows, 2 * HD), jnp.bfloat16),
         ],
         compiler_params=pltpu.CompilerParams(vmem_limit_bytes=24 * 1024 * 1024),
         name="attention",
-    )(span_order, jnp.stack([ulysses_index, cycle_index]).astype(jnp.int32), query_rows, *mine, *theirs)
-    heads = lax.all_to_all(
-        attended.reshape(QH, token_rows, HD), ("blk", "ulysses"), split_axis=0, concat_axis=0, tiled=True
-    )
-    rows = pl.pallas_call(
-        lambda *refs: order_heads_kernel(head_order, *refs),
+    )(span_order, place, query_rows, *(mine[d] for d in in_order), *(theirs[d] for d in in_order))
+    arrived = {distance: ahead(rest[distance - 1], distance) for distance in far_first}
+    crossed = {0: exchange(far, "chip", 1)}
+    for distance in far_first:
+        crossed[distance] = exchange(arrived[distance][1], "chip", 1)
+    arrived[0] = near
+    heads = pl.pallas_call(
+        order_heads_kernel,
         out_shape=jax.ShapeDtypeStruct((token_rows, QH * HD), jnp.bfloat16),
-        in_specs=[VMEM],
+        in_specs=[SMEM] + [VMEM] * (2 * cycle_size),
         out_specs=VMEM,
         compiler_params=pltpu.CompilerParams(vmem_limit_bytes=8 * 1024 * 1024),
         name="order_heads",
-    )(heads)
-    return rows[None]
+    )(place, *(arrived[d] for d in in_order), *(crossed[d] for d in in_order))
+    return heads[None]
 
 
 def solution(mesh):
     sizes = dict(mesh.shape)
-    whole_cycle = (
-        sizes["blk"] == STEPS + 1
-        and sizes["ulysses"] * sizes["blk"] == QH
-        and QH == 2 * KVH
-        and sizes["ulysses"] & (sizes["ulysses"] - 1) == 0
-        and sizes["dp"] == 2
-    )
-    return jax.shard_map(
-        whole_cycle_shards if whole_cycle else general_shards,
-        mesh=mesh,
+    specs = dict(
         in_specs=(
             P("dp", ("blk", "ulysses"), None),
             P("dp", ("blk", "ulysses"), None),
@@ -458,3 +518,19 @@
         out_specs=P("dp", ("blk", "ulysses"), None),
         check_vma=False,
     )
+    whole_cycle = (
+        sizes["blk"] == STEPS + 1
+        and sizes["ulysses"] == 4
+        and sizes["dp"] == 2
+        and sizes["ulysses"] * sizes["blk"] == QH == 2 * KVH
+    )
+    if not whole_cycle:
+        return jax.shard_map(general_shards, mesh=mesh, **specs)
+    chips = Mesh(
+        mesh.devices.reshape(sizes["dp"], sizes["ulysses"] // 2, 2, sizes["blk"]),
+        ("dp", "chip", "core", "blk"),
+    )
+    rows = P("dp", ("blk", "chip", "core"), None)
+    specs["in_specs"] = (rows, rows, *specs["in_specs"][2:])
+    specs["out_specs"] = rows
+    return jax.shard_map(whole_cycle_shards, mesh=chips, **specs)

time: 110 us -> 105 us (0.955)
  blocking collectives: 20.8 us -> 0 us
  starting transfers between devices: 20.6 us -> 30.4 us
  waiting for transfers between devices: 34.7 us -> 41.8 us
  other arithmetic: 6.58 us -> 5.35 us
    all_to_all x1 -> x0, blocking collectives: 20.8 us -> none  [whole_cycle_shards(): lax.all_to_all(attended.reshape(QH, token_rows, HD), ('blk', 'ulysses'),...]
    ppermute x6 -> x9, waiting for transfers between devices: 23.7 us -> 34.9 us  [ahead(): lax.ppermute(block, 'blk', [(i, (i + distance) % cycle_size) for i in ran...]
    ppermute x4, waiting for transfers between devices: 8.52 us -> 1.87 us  [across(): lax.ppermute(block, 'dp', [(i, dp_size - 1 - i) for i in range(dp_size)])]
    ppermute x7 -> x11, starting transfers between devices: 2.01 us -> 6.54 us  [exchange(): return lax.ppermute(block, axis, [(i, i ^ distance) for i in range(size)])]
    ppermute x6 -> x9, starting transfers between devices: 8.85 us -> 12.7 us  [ahead(): lax.ppermute(block, 'blk', [(i, (i + distance) % cycle_size) for i in ran...]
    ppermute x7 -> x11, waiting for transfers between devices: 2.52 us -> 5.04 us  [exchange(): return lax.ppermute(block, axis, [(i, i ^ distance) for i in range(size)])]
    concatenate x1 -> x0, other arithmetic: 2.42 us -> none  [whole_cycle_shards(): hidden = jnp.concatenate(slots, axis=0)]
    select_n x1, other arithmetic: 0.89 us -> 2.09 us  [whole_cycle_shards(): pair_cosine = jnp.where(core == 0, cosine, 1.0)]
  transfers between devices with their start and end apart: 18 -> 25, of which waited for: 9 -> 13; matrix products, arithmetic and copies ran while one was open for 7% -> 7% of each run, Pallas kernels for 6% -> 7%
where the time goes in v4:
time: 105 us; the launch traced here: 104 us
  waiting for transfers between devices  41.8 us (40%)
  starting transfers between devices  30.4 us (29%)
  local copies, waits for them, and re-layouts  13.7 us (13%)
  Pallas kernels  13.1 us (12%)
  other arithmetic  5.35 us (5%)
    ppermute x9, waiting for transfers between devices, ahead(): lax.ppermute(block, 'blk', [(i, (i + distance) % cycle_size) for i in ran...  34.9 us
    ppermute x9, starting transfers between devices, ahead(): lax.ppermute(block, 'blk', [(i, (i + distance) % cycle_size) for i in ran...  12.7 us
    unnamed x32, local copies, waits for them, and re-layouts  12.2 us
    ppermute x11, starting transfers between devices, exchange(): return lax.ppermute(block, axis, [(i, i ^ distance) for i in range(size)])  6.54 us
    ppermute x4, starting transfers between devices, across(): lax.ppermute(block, 'dp', [(i, dp_size - 1 - i) for i in range(dp_size)])  5.69 us
    all_to_all x1, starting transfers between devices, whole_cycle_shards(): lax.all_to_all(rotated, ('blk', 'chip'), split_axis=0, concat_axis=0, til...  5.44 us
    ppermute x11, waiting for transfers between devices, exchange(): return lax.ppermute(block, axis, [(i, i ^ distance) for i in range(size)])  5.04 us
    pallas_call x1, Pallas kernels, whole_cycle_shards(): pl.pallas_call(functools.partial(terms_kernel, ulysses_size, len(received...  4.46 us
  transfers between devices with their start and end apart: 25, of which 13 were waited for; matrix products, arithmetic and copies ran while one was open for 7% of the time, Pallas kernels for 7%

profile of v4, /device:TPU:0, one launch (start us, length us, event | category | flops | bytes accessed | tf_op | source)
XLA Modules:
  0.0 104.5 jit_solution(9721390814230100278)
XLA Ops:
  0.0 1.6 %copy-done = bf16[512,2048]{1,0:T(8,128)(2,1)S(1)} copy-done((bf16[512,2048]{1,0:T(8,128)(2,1)S(1)}, bf16[512,2048]{1,0:T(8,128)(2,1)}, u32[]{:S(2)}) %copy-start) | copy-done | bytes 2097176
  1.6 3.1 %collective-permute-start = (bf16[512,512]{1,0:T(8,128)(2,1)S(1)}, bf16[512,512]{1,0:T(8,128)(2,1)S(1)}, u32[]{:S(2)}, u32[]{:S(2)}) collective-permute-start(bf16[512,512]{1,0:T(8,128)(2,1)S(1)} %constant_dynamic-slice_fusion.refs_4_), channel_id=1, source_target_pairs={{0,1},{1,2},{2,3},{3,0},{4,5},{5,6},{6,7},{7,4},{8,9},{9,10},{10,1... | collective-permute-start | bytes 1572872 | tf_op jit(solution)/shard_map/ppermute | solution.py:403
  4.7 1.5 %collective-permute-start.2 = (bf16[512,512]{1,0:T(8,128)(2,1)S(1)}, bf16[512,512]{1,0:T(8,128)(2,1)}, u32[]{:S(2)}, u32[]{:S(2)}) collective-permute-start(bf16[512,512]{1,0:T(8,128)(2,1)S(1)} %constant_dynamic-slice_fusion.refs_4_), channel_id=1, source_target_pairs={{0,16},{16,0},{1,17},{17,1},{2,18},{18,2},{3,19},{19,3},{4,20},{20... | collective-permute-start | bytes 1572872 | tf_op jit(solution)/shard_map/ppermute | solution.py:406
  6.2 1.5 %collective-permute-start.1 = (bf16[128,4096]{1,0:T(8,128)(2,1)}, bf16[128,4096]{1,0:T(8,128)(2,1)}, u32[]{:S(2)}, u32[]{:S(2)}) collective-permute-start(bf16[128,4096]{1,0:T(8,128)(2,1)} %bitcast.28), channel_id=1, source_target_pairs={{0,8},{8,0},{1,9},{9,1},{2,10},{10,2},{3,11},{11,3},{4,12},{12,4},... | collective-permute-start | bytes 3145736 | tf_op jit(solution)/shard_map/ppermute | solution.py:196
  9.8 1.4 %fusion.5 = f32[512]{0:T(512)S(1)} fusion(s32[]{:T(128)} %bitcast.3, s32[]{:T(128)} %bitcast.2, s32[4]{0:T(128)S(1)} %xor_multiply_fusion), kind=kLoop, calls=%fused_computation.19 | loop fusion | flops 8704 | bytes 2072 | tf_op jit(solution)/shard_map/convert_element_type | solution.py:47
  14.8 2.1 %maximum_select_fusion = (f32[512,128]{1,0:T(8,128)S(1)}, f32[512,128]{1,0:T(8,128)}) fusion(f32[512,64]{1,0:T(8,128)} %copy-done.15, pred[]{:T(512)S(6)} %eq.15, f32[512,64]{1,0:T(8,128)} %copy-done.13, f32[512,64]{1,0:T(8,128)} %copy-done.14), kind=kLoop, calls=%fused_computation.2 | loop fusion | flops 262144 | bytes 917505 | tf_op jit(solution)/shard_map/jit(_where)/select_n | solution.py:387
  16.9 1.8 %collective-permute-done.refs_6_ = bf16[512,512]{1,0:T(8,128)(2,1)S(1)} collective-permute-done((bf16[512,512]{1,0:T(8,128)(2,1)S(1)}, bf16[512,512]{1,0:T(8,128)(2,1)S(1)}, u32[]{:S(2)}, u32[]{:S(2)}) %collective-permute-start) | collective-permute-done | bytes 524320 | tf_op jit(solution)/shard_map/ppermute | solution.py:403
  19.8 1.5 %collective-permute-start.4 = (bf16[512,512]{1,0:T(8,128)(2,1)S(1)}, bf16[512,512]{1,0:T(8,128)(2,1)S(1)}, u32[]{:S(2)}, u32[]{:S(2)}) collective-permute-start(bf16[512,512]{1,0:T(8,128)(2,1)S(1)} %collective-permute-done.refs_6_), channel_id=1, source_target_pairs={{0,16},{16,0},{1,17},{17,1},{2,18},{18,2},{3,19},{19,3},{4,20},{20... | collective-permute-start | bytes 1572872 | tf_op jit(solution)/shard_map/ppermute | solution.py:406
  22.1 11.6 %collective-permute-done.3.refs_8_ = bf16[512,512]{1,0:T(8,128)(2,1)} collective-permute-done((bf16[512,512]{1,0:T(8,128)(2,1)S(1)}, bf16[512,512]{1,0:T(8,128)(2,1)}, u32[]{:S(2)}, u32[]{:S(2)}) %collective-permute-start.3) | collective-permute-done | bytes 524320 | tf_op jit(solution)/shard_map/ppermute | solution.py:403
  38.3 5.4 %all-to-all-start = ((bf16[8,128,256]{2,1,0:T(8,128)(2,1)}), bf16[8,128,256]{2,1,0:T(8,128)(2,1)S(1)}, u32[]{:S(2)}, u32[]{:S(2)}) async-start(bf16[8,128,256]{2,1,0:T(8,128)(2,1)} %query_rope.1), calls=%async_computation | async-start | bytes 1048576 | tf_op jit(solution)/shard_map/all_to_all | solution.py:435
  43.8 7.6 %collective-permute-done.5.refs_10_ = bf16[512,512]{1,0:T(8,128)(2,1)} collective-permute-done((bf16[512,512]{1,0:T(8,128)(2,1)}, bf16[512,512]{1,0:T(8,128)(2,1)}, u32[]{:S(2)}, u32[]{:S(2)}) %collective-permute-start.5) | collective-permute-done | bytes 524320 | tf_op jit(solution)/shard_map/ppermute | solution.py:403
  58.4 4.5 %terms.1 = (f32[512,512]{1,0:T(8,128)S(1)}, bf16[512,512]{1,0:T(8,128)(2,1)S(1)}) custom-call(s32[8]{0:T(128)S(1)} %stack.44.rows_ref, bf16[128,4096]{1,0:T(8,128)(2,1)S(1)} %bitcast.30, bf16[128,4096]{1,0:T(8,128)(2,1)S(1)} %copy-done.3, bf16[128,4096]{1,0:T(8,128)(2,1)} %collective-permute-done.1.refs_2_, bf16[128,4096]{1,0:T(8,128)(2,1)S(1)} %copy-done.5, ...), custom_call_target="tpu_custom_call" | custom-call | tf_op jit(solution)/shard_map/terms/pallas_call | solution.py:441
  62.9 1.9 %collective-permute-done.7.piece_ref = bf16[512,512]{1,0:T(8,128)(2,1)S(1)} collective-permute-done((bf16[512,512]{1,0:T(8,128)(2,1)}, bf16[512,512]{1,0:T(8,128)(2,1)S(1)}, u32[]{:S(2)}, u32[]{:S(2)}) %collective-permute-start.7) | collective-permute-done | bytes 524320 | tf_op jit(solution)/shard_map/ppermute | solution.py:406
  64.8 2.1 %pair_rope.1 = (bf16[512,128]{1,0:T(8,128)(2,1)S(1)}, bf16[512,128]{1,0:T(8,128)(2,1)}, bf16[512,128]{1,0:T(8,128)(2,1)}, bf16[512,128]{1,0:T(8,128)(2,1)}) custom-call(s32[2]{0:T(128)S(1)} %pad_add_fusion.place_ref, f32[512,512]{1,0:T(8,128)S(1)} %get-tuple-element.61.total_ref, bf16[512,512]{1,0:T(8,128)(2,1)S(1)} %get-tuple-element.62.hidden_ref, ...), custom_call_target="tpu_custom_call" | custom-call | tf_op jit(solution)/shard_map/pair_rope/pallas_call | solution.py:459
  66.9 1.9 %collective-permute-start.11 = (bf16[512,128]{1,0:T(8,128)(2,1)}, bf16[512,128]{1,0:T(8,128)(2,1)S(1)}, u32[]{:S(2)}, u32[]{:S(2)}) collective-permute-start(bf16[512,128]{1,0:T(8,128)(2,1)} %get-tuple-element.74), channel_id=1, source_target_pairs={{0,2},{1,3},{2,0},{3,1},{4,6},{5,7},{6,4},{7,5},{8,10},{9,11},{10,... | collective-permute-start | bytes 393224 | tf_op jit(solution)/shard_map/ppermute | solution.py:403
  68.8 1.9 %collective-permute-start.12 = (bf16[512,128]{1,0:T(8,128)(2,1)}, bf16[512,128]{1,0:T(8,128)(2,1)S(1)}, u32[]{:S(2)}, u32[]{:S(2)}) collective-permute-start(bf16[512,128]{1,0:T(8,128)(2,1)} %get-tuple-element.75), channel_id=1, source_target_pairs={{0,3},{1,0},{2,1},{3,2},{4,7},{5,4},{6,5},{7,6},{8,11},{9,8},{10,9... | collective-permute-start | bytes 393224 | tf_op jit(solution)/shard_map/ppermute | solution.py:403
  70.7 4.6 %collective-permute-done.10.refs_1_ = bf16[512,128]{1,0:T(8,128)(2,1)S(1)} collective-permute-done((bf16[512,128]{1,0:T(8,128)(2,1)}, bf16[512,128]{1,0:T(8,128)(2,1)S(1)}, u32[]{:S(2)}, u32[]{:S(2)}) %collective-permute-start.10) | collective-permute-done | bytes 131104 | tf_op jit(solution)/shard_map/ppermute | solution.py:403
  75.3 3.2 %collective-permute-done.11.refs_2_ = bf16[512,128]{1,0:T(8,128)(2,1)S(1)} collective-permute-done((bf16[512,128]{1,0:T(8,128)(2,1)}, bf16[512,128]{1,0:T(8,128)(2,1)S(1)}, u32[]{:S(2)}, u32[]{:S(2)}) %collective-permute-start.11) | collective-permute-done | bytes 131104 | tf_op jit(solution)/shard_map/ppermute | solution.py:403
  80.1 4.0 %attention.1 = (bf16[128,256]{1,0:T(8,128)(2,1)S(1)}, bf16[128,256]{1,0:T(8,128)(2,1)S(1)}, bf16[2,128,256]{2,1,0:T(8,128)(2,1)S(1)}, bf16[2,128,256]{2,1,0:T(8,128)(2,1)S(1)}, bf16[2,128,256]{2,1,0:T(8,128)(2,1)S(1)}) custom-call(s32[1,8]{1,0:T(1,128)S(1)} %copy-done.12, s32[2]{0:T(128)S(1)} %pad_add_fusion.place_ref, ...), custom_call_target="tpu_custom_call" | custom-call | tf_op jit(solution)/shard_map/attention/pallas_call | solution.py:479
  84.1 2.2 %collective-permute-start.17 = (bf16[2,128,256]{2,1,0:T(8,128)(2,1)S(1)}, bf16[2,128,256]{2,1,0:T(8,128)(2,1)S(1)}, u32[]{:S(2)}, u32[]{:S(2)}) collective-permute-start(bf16[2,128,256]{2,1,0:T(8,128)(2,1)S(1)} %get-tuple-element.77), channel_id=1, source_target_pairs={{0,1},{1,2},{2,3},{3,0},{4,5},{5,6},{6,7},{7,4},{8,9},{9,10},{10,1... | collective-permute-start | bytes 393224 | tf_op jit(solution)/shard_map/ppermute | solution.py:403
  87.4 1.4 %collective-permute-start.19 = (bf16[2,128,256]{2,1,0:T(8,128)(2,1)S(1)}, bf16[2,128,256]{2,1,0:T(8,128)(2,1)S(1)}, u32[]{:S(2)}, u32[]{:S(2)}) collective-permute-start(bf16[2,128,256]{2,1,0:T(8,128)(2,1)S(1)} %get-tuple-element.79), channel_id=1, source_target_pairs={{0,3},{1,0},{2,1},{3,2},{4,7},{5,4},{6,5},{7,6},{8,11},{9,8},{10,9... | collective-permute-start | bytes 393224 | tf_op jit(solution)/shard_map/ppermute | solution.py:403
  90.0 2.4 %collective-permute-done.17.refs_1_ = bf16[2,128,256]{2,1,0:T(8,128)(2,1)S(1)} collective-permute-done((bf16[2,128,256]{2,1,0:T(8,128)(2,1)S(1)}, bf16[2,128,256]{2,1,0:T(8,128)(2,1)S(1)}, u32[]{:S(2)}, u32[]{:S(2)}) %collective-permute-start.17) | collective-permute-done | bytes 131104 | tf_op jit(solution)/shard_map/ppermute | solution.py:403
  93.6 3.8 %collective-permute-done.18.refs_2_ = bf16[2,128,256]{2,1,0:T(8,128)(2,1)S(1)} collective-permute-done((bf16[2,128,256]{2,1,0:T(8,128)(2,1)S(1)}, bf16[2,128,256]{2,1,0:T(8,128)(2,1)S(1)}, u32[]{:S(2)}, u32[]{:S(2)}) %collective-permute-start.18) | collective-permute-done | bytes 131104 | tf_op jit(solution)/shard_map/ppermute | solution.py:403
  99.5 2.8 %collective-permute-done.22.refs_6_ = bf16[128,256]{1,0:T(8,128)(2,1)S(1)} collective-permute-done((bf16[128,256]{1,0:T(8,128)(2,1)S(1)}, bf16[128,256]{1,0:T(8,128)(2,1)S(1)}, u32[]{:S(2)}, u32[]{:S(2)}) %collective-permute-start.22) | collective-permute-done | bytes 65568 | tf_op jit(solution)/shard_map/ppermute | solution.py:196
  (77 shorter events, 28.5 us)
Async XLA Ops:
  1.6 17.0 %collective-permute-start = (bf16[512,512]{1,0:T(8,128)(2,1)S(1)}, bf16[512,512]{1,0:T(8,128)(2,1)S(1)}, u32[]{:S(2)}, u32[]{:S(2)}) collective-permute-start(bf16[512,512]{1,0:T(8,128)(2,1)S(1)} %constant_dynamic-slice_fusion.refs_4_), channel_id=1, source_target_pairs={{0,1},{1,2},{2,3},{3,0},{4,5},{5,6},{6,7},{7,4},{8,9},{9,10},{10,1... | collective-permute-start | bytes 1572872 | tf_op jit(solution)/shard_map/ppermute | solution.py:403
  4.7 14.0 %collective-permute-start.2 = (bf16[512,512]{1,0:T(8,128)(2,1)S(1)}, bf16[512,512]{1,0:T(8,128)(2,1)}, u32[]{:S(2)}, u32[]{:S(2)}) collective-permute-start(bf16[512,512]{1,0:T(8,128)(2,1)S(1)} %constant_dynamic-slice_fusion.refs_4_), channel_id=1, source_target_pairs={{0,16},{16,0},{1,17},{17,1},{2,18},{18,2},{3,19},{19,3},{4,20},{20... | collective-permute-start | bytes 1572872 | tf_op jit(solution)/shard_map/ppermute | solution.py:406
  6.2 28.3 %collective-permute-start.1 = (bf16[128,4096]{1,0:T(8,128)(2,1)}, bf16[128,4096]{1,0:T(8,128)(2,1)}, u32[]{:S(2)}, u32[]{:S(2)}) collective-permute-start(bf16[128,4096]{1,0:T(8,128)(2,1)} %bitcast.28), channel_id=1, source_target_pairs={{0,8},{8,0},{1,9},{9,1},{2,10},{10,2},{3,11},{11,3},{4,12},{12,4},... | collective-permute-start | bytes 3145736 | tf_op jit(solution)/shard_map/ppermute | solution.py:196
  18.7 15.0 %collective-permute-start.3 = (bf16[512,512]{1,0:T(8,128)(2,1)S(1)}, bf16[512,512]{1,0:T(8,128)(2,1)}, u32[]{:S(2)}, u32[]{:S(2)}) collective-permute-start(bf16[512,512]{1,0:T(8,128)(2,1)S(1)} %collective-permute-done.refs_6_), channel_id=1, source_target_pairs={{0,1},{1,2},{2,3},{3,0},{4,5},{5,6},{6,7},{7,4},{8,9},{9,10},{10,1... | collective-permute-start | bytes 1572872 | tf_op jit(solution)/shard_map/ppermute | solution.py:403
  19.8 13.9 %collective-permute-start.4 = (bf16[512,512]{1,0:T(8,128)(2,1)S(1)}, bf16[512,512]{1,0:T(8,128)(2,1)S(1)}, u32[]{:S(2)}, u32[]{:S(2)}) collective-permute-start(bf16[512,512]{1,0:T(8,128)(2,1)S(1)} %collective-permute-done.refs_6_), channel_id=1, source_target_pairs={{0,16},{16,0},{1,17},{17,1},{2,18},{18,2},{3,19},{19,3},{4,20},{20... | collective-permute-start | bytes 1572872 | tf_op jit(solution)/shard_map/ppermute | solution.py:406
  22.1 13.8 %collective-permute-start.8 = (bf16[128,4096]{1,0:T(8,128)(2,1)}, bf16[128,4096]{1,0:T(8,128)(2,1)S(1)}, u32[]{:S(2)}, u32[]{:S(2)}) collective-permute-start(bf16[128,4096]{1,0:T(8,128)(2,1)} %bitcast.29), channel_id=1, source_target_pairs={{0,4},{4,0},{1,5},{5,1},{2,6},{6,2},{3,7},{7,3},{8,12},{12,8},{9,1... | collective-permute-start | bytes 3145736 | tf_op jit(solution)/shard_map/ppermute | solution.py:196
  34.5 2.9 %collective-permute-start.9 = (bf16[128,4096]{1,0:T(8,128)(2,1)}, bf16[128,4096]{1,0:T(8,128)(2,1)S(1)}, u32[]{:S(2)}, u32[]{:S(2)}) collective-permute-start(bf16[128,4096]{1,0:T(8,128)(2,1)} %collective-permute-done.1.refs_2_), channel_id=1, source_target_pairs={{0,4},{4,0},{1,5},{5,1},{2,6},{6,2},{3,7},{7,3},{8,12},{12,8},{9,1... | collective-permute-start | bytes 3145736 | tf_op jit(solution)/shard_map/ppermute | solution.py:196
  34.5 16.9 %collective-permute-start.5 = (bf16[512,512]{1,0:T(8,128)(2,1)}, bf16[512,512]{1,0:T(8,128)(2,1)}, u32[]{:S(2)}, u32[]{:S(2)}) collective-permute-start(bf16[512,512]{1,0:T(8,128)(2,1)} %collective-permute-done.3.refs_8_), channel_id=1, source_target_pairs={{0,1},{1,2},{2,3},{3,0},{4,5},{5,6},{6,7},{7,4},{8,9},{9,10},{10,1... | collective-permute-start | bytes 1572872 | tf_op jit(solution)/shard_map/ppermute | solution.py:403
  34.5 16.9 %collective-permute-start.6 = (bf16[512,512]{1,0:T(8,128)(2,1)}, bf16[512,512]{1,0:T(8,128)(2,1)}, u32[]{:S(2)}, u32[]{:S(2)}) collective-permute-start(bf16[512,512]{1,0:T(8,128)(2,1)} %collective-permute-done.3.refs_8_), channel_id=1, source_target_pairs={{0,16},{16,0},{1,17},{17,1},{2,18},{18,2},{3,19},{19,3},{4,20},{20... | collective-permute-start | bytes 1572872 | tf_op jit(solution)/shard_map/ppermute | solution.py:406
  38.3 28.6 %all-to-all-start = ((bf16[8,128,256]{2,1,0:T(8,128)(2,1)}), bf16[8,128,256]{2,1,0:T(8,128)(2,1)S(1)}, u32[]{:S(2)}, u32[]{:S(2)}) async-start(bf16[8,128,256]{2,1,0:T(8,128)(2,1)} %query_rope.1), calls=%async_computation | async-start | bytes 1048576 | tf_op jit(solution)/shard_map/all_to_all | solution.py:435
  51.4 13.4 %collective-permute-start.7 = (bf16[512,512]{1,0:T(8,128)(2,1)}, bf16[512,512]{1,0:T(8,128)(2,1)S(1)}, u32[]{:S(2)}, u32[]{:S(2)}) collective-permute-start(bf16[512,512]{1,0:T(8,128)(2,1)} %collective-permute-done.5.refs_10_), channel_id=1, source_target_pairs={{0,16},{16,0},{1,17},{17,1},{2,18},{18,2},{3,19},{19,3},{4,20},{20... | collective-permute-start | bytes 1572872 | tf_op jit(solution)/shard_map/ppermute | solution.py:406
  66.9 8.4 %collective-permute-start.10 = (bf16[512,128]{1,0:T(8,128)(2,1)}, bf16[512,128]{1,0:T(8,128)(2,1)S(1)}, u32[]{:S(2)}, u32[]{:S(2)}) collective-permute-start(bf16[512,128]{1,0:T(8,128)(2,1)} %get-tuple-element.73), channel_id=1, source_target_pairs={{0,1},{1,2},{2,3},{3,0},{4,5},{5,6},{6,7},{7,4},{8,9},{9,10},{10,1... | collective-permute-start | bytes 393224 | tf_op jit(solution)/shard_map/ppermute | solution.py:403
  66.9 11.6 %collective-permute-start.11 = (bf16[512,128]{1,0:T(8,128)(2,1)}, bf16[512,128]{1,0:T(8,128)(2,1)S(1)}, u32[]{:S(2)}, u32[]{:S(2)}) collective-permute-start(bf16[512,128]{1,0:T(8,128)(2,1)} %get-tuple-element.74), channel_id=1, source_target_pairs={{0,2},{1,3},{2,0},{3,1},{4,6},{5,7},{6,4},{7,5},{8,10},{9,11},{10,... | collective-permute-start | bytes 393224 | tf_op jit(solution)/shard_map/ppermute | solution.py:403
  68.8 9.7 %collective-permute-start.12 = (bf16[512,128]{1,0:T(8,128)(2,1)}, bf16[512,128]{1,0:T(8,128)(2,1)S(1)}, u32[]{:S(2)}, u32[]{:S(2)}) collective-permute-start(bf16[512,128]{1,0:T(8,128)(2,1)} %get-tuple-element.75), channel_id=1, source_target_pairs={{0,3},{1,0},{2,1},{3,2},{4,7},{5,4},{6,5},{7,6},{8,11},{9,8},{10,9... | collective-permute-start | bytes 393224 | tf_op jit(solution)/shard_map/ppermute | solution.py:403
  70.7 8.3 %collective-permute-start.13 = (bf16[512,128]{1,0:T(8,128)(2,1)S(1)}, bf16[512,128]{1,0:T(8,128)(2,1)S(1)}, u32[]{:S(2)}, u32[]{:S(2)}) collective-permute-start(bf16[512,128]{1,0:T(8,128)(2,1)S(1)} %get-tuple-element.72.refs_0_), channel_id=1, source_target_pairs={{0,4},{4,0},{1,5},{5,1},{2,6},{6,2},{3,7},{7,3},{8,12},{12,8},{9,1... | collective-permute-start | bytes 393224 | tf_op jit(solution)/shard_map/ppermute | solution.py:196
  75.3 3.7 %collective-permute-start.14 = (bf16[512,128]{1,0:T(8,128)(2,1)S(1)}, bf16[512,128]{1,0:T(8,128)(2,1)S(1)}, u32[]{:S(2)}, u32[]{:S(2)}) collective-permute-start(bf16[512,128]{1,0:T(8,128)(2,1)S(1)} %collective-permute-done.10.refs_1_), channel_id=1, source_target_pairs={{0,4},{4,0},{1,5},{5,1},{2,6},{6,2},{3,7},{7,3},{8,12},{12,8},{9,1... | collective-permute-start | bytes 393224 | tf_op jit(solution)/shard_map/ppermute | solution.py:196
  78.5 1.5 %collective-permute-start.16 = (bf16[512,128]{1,0:T(8,128)(2,1)S(1)}, bf16[512,128]{1,0:T(8,128)(2,1)S(1)}, u32[]{:S(2)}, u32[]{:S(2)}) collective-permute-start(bf16[512,128]{1,0:T(8,128)(2,1)S(1)} %collective-permute-done.12.refs_3_), channel_id=1, source_target_pairs={{0,4},{4,0},{1,5},{5,1},{2,6},{6,2},{3,7},{7,3},{8,12},{12,8},{9,1... | collective-permute-start | bytes 393224 | tf_op jit(solution)/shard_map/ppermute | solution.py:196
  84.1 8.3 %collective-permute-start.17 = (bf16[2,128,256]{2,1,0:T(8,128)(2,1)S(1)}, bf16[2,128,256]{2,1,0:T(8,128)(2,1)S(1)}, u32[]{:S(2)}, u32[]{:S(2)}) collective-permute-start(bf16[2,128,256]{2,1,0:T(8,128)(2,1)S(1)} %get-tuple-element.77), channel_id=1, source_target_pairs={{0,1},{1,2},{2,3},{3,0},{4,5},{5,6},{6,7},{7,4},{8,9},{9,10},{10,1... | collective-permute-start | bytes 393224 | tf_op jit(solution)/shard_map/ppermute | solution.py:403
  86.3 11.1 %collective-permute-start.18 = (bf16[2,128,256]{2,1,0:T(8,128)(2,1)S(1)}, bf16[2,128,256]{2,1,0:T(8,128)(2,1)S(1)}, u32[]{:S(2)}, u32[]{:S(2)}) collective-permute-start(bf16[2,128,256]{2,1,0:T(8,128)(2,1)S(1)} %get-tuple-element.78), channel_id=1, source_target_pairs={{0,2},{1,3},{2,0},{3,1},{4,6},{5,7},{6,4},{7,5},{8,10},{9,11},{10,... | collective-permute-start | bytes 393224 | tf_op jit(solution)/shard_map/ppermute | solution.py:403
  87.4 11.3 %collective-permute-start.19 = (bf16[2,128,256]{2,1,0:T(8,128)(2,1)S(1)}, bf16[2,128,256]{2,1,0:T(8,128)(2,1)S(1)}, u32[]{:S(2)}, u32[]{:S(2)}) collective-permute-start(bf16[2,128,256]{2,1,0:T(8,128)(2,1)S(1)} %get-tuple-element.79), channel_id=1, source_target_pairs={{0,3},{1,0},{2,1},{3,2},{4,7},{5,4},{6,5},{7,6},{8,11},{9,8},{10,9... | collective-permute-start | bytes 393224 | tf_op jit(solution)/shard_map/ppermute | solution.py:403
  88.8 10.7 %collective-permute-start.20 = (bf16[128,256]{1,0:T(8,128)(2,1)S(1)}, bf16[128,256]{1,0:T(8,128)(2,1)S(1)}, u32[]{:S(2)}, u32[]{:S(2)}) collective-permute-start(bf16[128,256]{1,0:T(8,128)(2,1)S(1)} %get-tuple-element.80), channel_id=1, source_target_pairs={{0,8},{8,0},{1,9},{9,1},{2,10},{10,2},{3,11},{11,3},{4,12},{12,4},... | collective-permute-start | bytes 196616 | tf_op jit(solution)/shard_map/ppermute | solution.py:196
  92.4 7.1 %collective-permute-start.21 = (bf16[128,256]{1,0:T(8,128)(2,1)S(1)}, bf16[128,256]{1,0:T(8,128)(2,1)S(1)}, u32[]{:S(2)}, u32[]{:S(2)}) collective-permute-start(bf16[128,256]{1,0:T(8,128)(2,1)S(1)} %slice_bitcast_fusion.2), channel_id=1, source_target_pairs={{0,8},{8,0},{1,9},{9,1},{2,10},{10,2},{3,11},{11,3},{4,12},{12,4},... | collective-permute-start | bytes 196616 | tf_op jit(solution)/shard_map/ppermute | solution.py:196
  97.4 4.9 %collective-permute-start.22 = (bf16[128,256]{1,0:T(8,128)(2,1)S(1)}, bf16[128,256]{1,0:T(8,128)(2,1)S(1)}, u32[]{:S(2)}, u32[]{:S(2)}) collective-permute-start(bf16[128,256]{1,0:T(8,128)(2,1)S(1)} %slice_bitcast_fusion.1), channel_id=1, source_target_pairs={{0,8},{8,0},{1,9},{9,1},{2,10},{10,2},{3,11},{11,3},{4,12},{12,4},... | collective-permute-start | bytes 196616 | tf_op jit(solution)/shard_map/ppermute | solution.py:196
  98.6 4.4 %collective-permute-start.23 = (bf16[128,256]{1,0:T(8,128)(2,1)S(1)}, bf16[128,256]{1,0:T(8,128)(2,1)S(1)}, u32[]{:S(2)}, u32[]{:S(2)}) collective-permute-start(bf16[128,256]{1,0:T(8,128)(2,1)S(1)} %slice_bitcast_fusion), channel_id=1, source_target_pairs={{0,8},{8,0},{1,9},{9,1},{2,10},{10,2},{3,11},{11,3},{4,12},{12,4},... | collective-permute-start | bytes 196616 | tf_op jit(solution)/shard_map/ppermute | solution.py:196
  (17 other events, 44.3 us)

commit v5 on v4

--- a/solution.py
+++ b/solution.py
@@ -191,6 +191,10 @@
     return token_output[None]
 
 
+def far_first(size):
+    return sorted(range(1, size), key=lambda distance: -min(distance, size - distance))
+
+
 def exchange(block, axis, distance):
     size = lax.axis_size(axis)
     return lax.ppermute(block, axis, [(i, i ^ distance) for i in range(size)])
@@ -206,14 +210,25 @@
     return head * cosine + pltpu.roll(head, HD // 2, 1) * signed_sine
 
 
-def query_rope_kernel(pair_order, query_ref, cosine_ref, sine_ref, out_ref):
+def query_rope_kernel(place_ref, query_ref, cosine_ref, sine_ref, far_ref, *near_refs):
     cosine, sine = cosine_ref[...], sine_ref[...]
-    width = out_ref.shape[2]
-    for place, pair in enumerate(pair_order):
-        for start in range(0, width, HD):
-            column = pair * width + start
-            rows = query_ref[:, column : column + HD].astype(jnp.float32)
-            out_ref[place, :, start : start + HD] = rope_head(rows, cosine, sine).astype(jnp.bfloat16)
+    blocks, width = far_ref.shape[0], far_ref.shape[2]
+    chip, block_here = place_ref[0] // 2, place_ref[1]
+    for distance, near_ref in enumerate(near_refs):
+        block = lax.rem(block_here + distance, blocks)
+        for target, out_ref in ((chip, near_ref), (1 - chip, far_ref.at[distance])):
+            columns = pl.ds(pl.multiple_of((target * blocks + block) * width, width), width)
+            pair = query_ref[:, columns].astype(jnp.float32)
+            for start in range(0, width, HD):
+                rows = rope_head(pair[:, start : start + HD], cosine, sine)
+                out_ref[:, start : start + HD] = rows.astype(jnp.bfloat16)
+
+
+def pack_kernel(far_ref, *refs):
+    near_refs, out_refs = refs[: len(refs) // 2], refs[len(refs) // 2 :]
+    for distance, (near_ref, out_ref) in enumerate(zip(near_refs, out_refs), 1):
+        out_ref[0] = near_ref[...]
+        out_ref[1] = far_ref[distance]
 
 
 def load_terms(rows_ref, slot_refs, piece_refs, hidden_rows, pieces, sems):
@@ -275,27 +290,31 @@
     out_ref = refs[-1]
     blocks = (len(refs) - 1) // 2
     chip, block_here = place_ref[0] // 2, place_ref[1]
-    width = refs[0].shape[-1]
+    width = refs[0].shape[1]
     for distance in range(blocks):
         block = lax.rem(block_here + blocks - distance, blocks)
         near, far = refs[distance], refs[blocks + distance]
-        for source, rows in ((chip, near[...] if distance == 0 else near[0]), (1 - chip, far[...])):
+        for source, rows in ((chip, near[...]), (1 - chip, far[0] if distance == 0 else far[...])):
             pair = source * blocks + block
             out_ref[:, pl.ds(pl.multiple_of(pair * width, width), width)] = rows
 
 
-def attention_kernel(order_ref, place_ref, query_ref, *refs):
+def attention_kernel(order_ref, place_ref, *refs):
     spans = order_ref.shape[1]
     blocks = spans // 2
     mine_refs, theirs_refs = refs[:blocks], refs[blocks : 2 * blocks]
-    near_ref, far_ref, *both_refs = refs[2 * blocks : 3 * blocks + 1]
-    key_rows, value_rows, out_rows = refs[3 * blocks + 1 :]
-    token_rows = query_ref.shape[1]
+    near_query, far_query, *packed_queries = refs[2 * blocks : 3 * blocks + 1]
+    far_ref, *near_refs = refs[3 * blocks + 1 : -4]
+    key_rows, value_rows, query_rows, out_rows = refs[-4:]
+    token_rows = query_rows.shape[1]
     span_rows = 2 * token_rows
     place, block_here = place_ref[0], place_ref[1]
     chip, core = place // 2, place % 2
     for distance in range(blocks):
         block = lax.rem(block_here + blocks - distance, blocks)
+        packed = packed_queries[distance - 1] if distance else None
+        query_rows[2 * block + chip] = packed[0] if distance else near_query[...]
+        query_rows[2 * block + 1 - chip] = packed[1] if distance else far_query[0]
         for half in range(2):
             first = order_ref[0, 2 * block + half] * span_rows
             for part in range(2):
@@ -319,7 +338,7 @@
     allowed = lax.broadcasted_iota(jnp.int32, square, 1) <= row_index
 
     def scores(position):
-        pair = query_ref[stored[position]]
+        pair = query_rows[stored[position]]
         query = jnp.concatenate([pair[:, :HD], pair[:, HD:]], axis=0)
         score = lax.dot_general(
             query,
@@ -345,12 +364,10 @@
         rows = (numerator / denominator).astype(jnp.bfloat16)
         out_rows[stored[position]] = jnp.concatenate([rows[:token_rows], rows[token_rows:]], axis=1)
         score = following
-    near_ref[...] = out_rows[2 * block_here + chip]
-    far_ref[...] = out_rows[2 * block_here + 1 - chip]
-    for distance, both_ref in enumerate(both_refs, 1):
+    for distance, near_ref in enumerate(near_refs):
         block = lax.rem(block_here + distance, blocks)
-        both_ref[0] = out_rows[2 * block + chip]
-        both_ref[1] = out_rows[2 * block + 1 - chip]
+        near_ref[...] = out_rows[2 * block + chip]
+        far_ref[distance] = out_rows[2 * block + 1 - chip]
 
 
 VMEM = pl.BlockSpec(memory_space=pltpu.VMEM)
@@ -387,20 +404,24 @@
     pair_cosine = jnp.where(core == 0, cosine, 1.0)
     pair_sine = jnp.where(core == 0, sine, 0.0)
 
-    pair_order = [
-        place * cycle_size + block for block in range(cycle_size) for place in range(ulysses_size // 2)
-    ]
-    rotated = pl.pallas_call(
-        functools.partial(query_rope_kernel, pair_order),
-        out_shape=jax.ShapeDtypeStruct((len(pair_order), token_rows, 2 * HD), jnp.bfloat16),
-        in_specs=[VMEM] * 3,
-        out_specs=VMEM,
+    place = jnp.stack([ulysses_index, cycle_index]).astype(jnp.int32)
+    one = jax.ShapeDtypeStruct((token_rows, 2 * HD), jnp.bfloat16)
+    by_distance = jax.ShapeDtypeStruct((cycle_size, *one.shape), one.dtype)
+    far_queries, *near_queries = pl.pallas_call(
+        query_rope_kernel,
+        out_shape=[by_distance] + [one] * cycle_size,
+        in_specs=[SMEM] + [VMEM] * 3,
+        out_specs=[VMEM] * (1 + cycle_size),
         compiler_params=pltpu.CompilerParams(vmem_limit_bytes=8 * 1024 * 1024),
         name="query_rope",
-    )(queries[0], own_cosine, own_sine)
+    )(place, queries[0], own_cosine, own_sine)
 
     def ahead(block, distance=1):
         return lax.ppermute(block, "blk", [(i, (i + distance) % cycle_size) for i in range(cycle_size)])
+
+    def along_blocks(parts):
+        moved = {distance: ahead(parts[distance], distance) for distance in far_first(cycle_size)}
+        return [moved[distance] for distance in range(1, cycle_size)]
 
     def across(block):
         return lax.ppermute(block, "dp", [(i, dp_size - 1 - i) for i in range(dp_size)])
@@ -418,26 +439,35 @@
     for distance in range(1, cycle_size):
         firsts += [first_row(distance - 1, other_row), first_row(distance, dp_index)]
     rows = jnp.stack([*firsts, first_row(cycle_size - 1, other_row)])
-    place = jnp.stack([ulysses_index, cycle_index]).astype(jnp.int32)
     for distance in range(1, cycle_size - 1):
         travelling = ahead(travelling)
         if distance == 1:
-            rotated, pair_cosine, pair_sine, rows, place, travelling = lax.optimization_barrier(
-                (rotated, pair_cosine, pair_sine, rows, place, travelling)
+            far_queries, near_queries, pair_cosine, pair_sine, rows, place, travelling = (
+                lax.optimization_barrier(
+                    (far_queries, near_queries, pair_cosine, pair_sine, rows, place, travelling)
+                )
             )
         travelling, crossed = lax.optimization_barrier((travelling, crossed))
         received += [crossed, travelling]
         crossed = across(travelling)
 
-    far, travelling = lax.optimization_barrier((far, travelling))
+    far, far_queries, travelling = lax.optimization_barrier((far, far_queries, travelling))
     hidden = [own_hidden, partner, far, exchange(far, "core", 1)]
-    *hidden, rotated = lax.optimization_barrier((*hidden, rotated))
-    query_rows = lax.all_to_all(rotated, ("blk", "chip"), split_axis=0, concat_axis=0, tiled=True)
+    far_queries = exchange(far_queries, "chip", 1)
+    packed = pl.pallas_call(
+        pack_kernel,
+        out_shape=[jax.ShapeDtypeStruct((2, *one.shape), one.dtype)] * (cycle_size - 1),
+        in_specs=[VMEM] * cycle_size,
+        out_specs=[VMEM] * (cycle_size - 1),
+        compiler_params=pltpu.CompilerParams(vmem_limit_bytes=8 * 1024 * 1024),
+        name="pack",
+    )(far_queries, *near_queries[1:])
 
     travelling = ahead(travelling)
-    travelling, crossed = lax.optimization_barrier((travelling, crossed))
+    travelling, crossed, packed = lax.optimization_barrier((travelling, crossed, packed))
     received += [crossed, travelling]
     last_piece = across(travelling)
+    packed = along_blocks([None, *packed])
     total, last_hidden = pl.pallas_call(
         functools.partial(terms_kernel, ulysses_size, len(received)),
         out_shape=[
@@ -465,35 +495,39 @@
         compiler_params=pltpu.CompilerParams(vmem_limit_bytes=12 * 1024 * 1024),
         name="pair_rope",
     )(place, total, last_hidden, last_piece, pair_cosine, pair_sine)
-    *pairs, query_rows = lax.optimization_barrier((*pairs, query_rows))
-    far_first = sorted(range(1, cycle_size), key=lambda distance: -min(distance, cycle_size - distance))
+    pairs, packed = lax.optimization_barrier((pairs, packed))
     mine, theirs = {0: pairs[0]}, {0: exchange(pairs[0], "core", 1)}
-    for distance in far_first:
+    for distance in far_first(cycle_size):
         mine[distance] = ahead(pairs[distance], distance)
         theirs[distance] = exchange(mine[distance], "core", 1)
     in_order = range(cycle_size)
 
     sequence_rows = cycle_size * block_rows
-    one = jax.ShapeDtypeStruct((token_rows, 2 * HD), jnp.bfloat16)
-    both = jax.ShapeDtypeStruct((2, token_rows, 2 * HD), jnp.bfloat16)
-    near, far, *rest = pl.pallas_call(
+    far, *near = pl.pallas_call(
         attention_kernel,
-        out_shape=[one, one] + [both] * (cycle_size - 1),
-        in_specs=[SMEM, SMEM] + [VMEM] * (1 + 2 * cycle_size),
+        out_shape=[by_distance] + [one] * cycle_size,
+        in_specs=[SMEM, SMEM] + [VMEM] * (3 * cycle_size + 1),
         out_specs=[VMEM] * (cycle_size + 1),
         scratch_shapes=[
             pltpu.VMEM((sequence_rows, HD), jnp.bfloat16),
             pltpu.VMEM((sequence_rows, HD), jnp.bfloat16),
-            pltpu.VMEM((len(pair_order), token_rows, 2 * HD), jnp.bfloat16),
+            pltpu.VMEM((2 * cycle_size, token_rows, 2 * HD), jnp.bfloat16),
+            pltpu.VMEM((2 * cycle_size, token_rows, 2 * HD), jnp.bfloat16),
         ],
         compiler_params=pltpu.CompilerParams(vmem_limit_bytes=24 * 1024 * 1024),
         name="attention",
-    )(span_order, place, query_rows, *(mine[d] for d in in_order), *(theirs[d] for d in in_order))
-    arrived = {distance: ahead(rest[distance - 1], distance) for distance in far_first}
-    crossed = {0: exchange(far, "chip", 1)}
-    for distance in far_first:
-        crossed[distance] = exchange(arrived[distance][1], "chip", 1)
-    arrived[0] = near
+    )(
+        span_order,
+        place,
+        *(mine[d] for d in in_order),
+        *(theirs[d] for d in in_order),
+        near_queries[0],
+        far_queries,
+        *packed,
+    )
+    far = exchange(far, "chip", 1)
+    arrived = [near[0], *along_blocks(near)]
+    crossed = [far, *along_blocks(far)]
     heads = pl.pallas_call(
         order_heads_kernel,
         out_shape=jax.ShapeDtypeStruct((token_rows, QH * HD), jnp.bfloat16),
@@ -501,7 +535,7 @@
         out_specs=VMEM,
         compiler_params=pltpu.CompilerParams(vmem_limit_bytes=8 * 1024 * 1024),
         name="order_heads",
-    )(place, *(arrived[d] for d in in_order), *(crossed[d] for d in in_order))
+    )(place, *arrived, *crossed)
     return heads[None]
 
 

time: 105 us -> 96.3 us (0.917)
  local copies, waits for them, and re-layouts: 13.7 us -> 4.94 us
  starting transfers between devices: 30.4 us -> 31.5 us
    ppermute x9 -> x15, starting transfers between devices: 12.7 us -> 21.9 us  [ahead(): lax.ppermute(block, 'blk', [(i, (i + distance) % cycle_size) for i in ran...]
    unnamed x32 -> x16, local copies, waits for them, and re-layouts: 12.2 us -> 3.51 us
    ppermute x11 -> x9, waiting for transfers between devices: 5.04 us -> 11 us  [exchange(): return lax.ppermute(block, axis, [(i, i ^ distance) for i in range(size)])]
    all_to_all x1 -> x0, starting transfers between devices: 5.44 us -> none  [whole_cycle_shards(): lax.all_to_all(rotated, ('blk', 'chip'), split_axis=0, concat_axis=0, til...]
    ppermute x9 -> x15, waiting for transfers between devices: 34.9 us -> 30.2 us  [ahead(): lax.ppermute(block, 'blk', [(i, (i + distance) % cycle_size) for i in ran...]
    ppermute x11 -> x9, starting transfers between devices: 6.54 us -> 4.29 us  [exchange(): return lax.ppermute(block, axis, [(i, i ^ distance) for i in range(size)])]
    pallas_call x2 -> x3, Pallas kernels: 5.11 us -> 4.97 us  [the longest x1 4.11 us: whole_cycle_shards(): pl.pallas_call(attention_kernel, out_shape=[by_distance] + [one] * cycle_...]
  transfers between devices with their start and end apart: 25 -> 28, of which waited for: 13 -> 12; matrix products, arithmetic and copies ran while one was open for 7% -> 6% of each run, Pallas kernels for 7% -> 7%
where the time goes in v5:
time: 96.3 us; the launch traced here: 96 us
  waiting for transfers between devices  42.6 us (44%)
  starting transfers between devices  31.5 us (33%)
  Pallas kernels  12.2 us (13%)
  local copies, waits for them, and re-layouts  4.94 us (5%)
  other arithmetic  4.56 us (5%)
    ppermute x15, waiting for transfers between devices, ahead(): lax.ppermute(block, 'blk', [(i, (i + distance) % cycle_size) for i in ran...  30.2 us
    ppermute x15, starting transfers between devices, ahead(): lax.ppermute(block, 'blk', [(i, (i + distance) % cycle_size) for i in ran...  21.9 us
    ppermute x9, waiting for transfers between devices, exchange(): return lax.ppermute(block, axis, [(i, i ^ distance) for i in range(size)])  11 us
    ppermute x4, starting transfers between devices, across(): lax.ppermute(block, 'dp', [(i, dp_size - 1 - i) for i in range(dp_size)])  5.31 us
    pallas_call x1, Pallas kernels, whole_cycle_shards(): pl.pallas_call(functools.partial(terms_kernel, ulysses_size, len(received...  4.46 us
    ppermute x9, starting transfers between devices, exchange(): return lax.ppermute(block, axis, [(i, i ^ distance) for i in range(size)])  4.29 us
    pallas_call x1, Pallas kernels, whole_cycle_shards(): pl.pallas_call(attention_kernel, out_shape=[by_distance] + [one] * cycle_...  4.11 us
    unnamed x16, local copies, waits for them, and re-layouts  3.51 us
  transfers between devices with their start and end apart: 28, of which 12 were waited for; matrix products, arithmetic and copies ran while one was open for 6% of the time, Pallas kernels for 7%

profile of v5, /device:TPU:0, one launch (start us, length us, event | category | flops | bytes accessed | tf_op | source)
XLA Modules:
  0.0 96.0 jit_solution(6053658200150667718)
XLA Ops:
  0.0 1.6 %copy-done = bf16[512,2048]{1,0:T(8,128)(2,1)S(1)} copy-done((bf16[512,2048]{1,0:T(8,128)(2,1)S(1)}, bf16[512,2048]{1,0:T(8,128)(2,1)}, u32[]{:S(2)}) %copy-start) | copy-done | bytes 2097176
  1.6 3.1 %collective-permute-start = (bf16[512,512]{1,0:T(8,128)(2,1)S(1)}, bf16[512,512]{1,0:T(8,128)(2,1)S(1)}, u32[]{:S(2)}, u32[]{:S(2)}) collective-permute-start(bf16[512,512]{1,0:T(8,128)(2,1)S(1)} %constant_dynamic-slice_fusion.refs_4_), channel_id=1, source_target_pairs={{0,1},{1,2},{2,3},{3,0},{4,5},{5,6},{6,7},{7,4},{8,9},{9,10},{10,1... | collective-permute-start | bytes 1572872 | tf_op jit(solution)/shard_map/ppermute | solution.py:420
  4.7 1.5 %collective-permute-start.2 = (bf16[512,512]{1,0:T(8,128)(2,1)S(1)}, bf16[512,512]{1,0:T(8,128)(2,1)}, u32[]{:S(2)}, u32[]{:S(2)}) collective-permute-start(bf16[512,512]{1,0:T(8,128)(2,1)S(1)} %constant_dynamic-slice_fusion.refs_4_), channel_id=1, source_target_pairs={{0,16},{16,0},{1,17},{17,1},{2,18},{18,2},{3,19},{19,3},{4,20},{20... | collective-permute-start | bytes 1572872 | tf_op jit(solution)/shard_map/ppermute | solution.py:427
  6.2 1.5 %collective-permute-start.1 = (bf16[128,4096]{1,0:T(8,128)(2,1)}, bf16[128,4096]{1,0:T(8,128)(2,1)}, u32[]{:S(2)}, u32[]{:S(2)}) collective-permute-start(bf16[128,4096]{1,0:T(8,128)(2,1)} %bitcast.28), channel_id=1, source_target_pairs={{0,8},{8,0},{1,9},{9,1},{2,10},{10,2},{3,11},{11,3},{4,12},{12,4},... | collective-permute-start | bytes 3145736 | tf_op jit(solution)/shard_map/ppermute | solution.py:200
  15.0 1.5 %maximum_select_fusion = (f32[512,128]{1,0:T(8,128)S(1)}, f32[512,128]{1,0:T(8,128)S(1)}) fusion(f32[512,64]{1,0:T(8,128)} %copy-done.7, pred[]{:T(512)S(6)} %eq.15, f32[512,64]{1,0:T(8,128)} %copy-done.5, f32[512,64]{1,0:T(8,128)} %copy-done.6), kind=kLoop, calls=%fused_computation.2 | loop fusion | flops 262144 | bytes 917505 | tf_op jit(solution)/shard_map/jit(_where)/select_n | solution.py:404
  16.5 2.2 %collective-permute-done.refs_6_ = bf16[512,512]{1,0:T(8,128)(2,1)S(1)} collective-permute-done((bf16[512,512]{1,0:T(8,128)(2,1)S(1)}, bf16[512,512]{1,0:T(8,128)(2,1)S(1)}, u32[]{:S(2)}, u32[]{:S(2)}) %collective-permute-start) | collective-permute-done | bytes 524320 | tf_op jit(solution)/shard_map/ppermute | solution.py:420
  19.8 1.5 %collective-permute-start.4 = (bf16[512,512]{1,0:T(8,128)(2,1)S(1)}, bf16[512,512]{1,0:T(8,128)(2,1)S(1)}, u32[]{:S(2)}, u32[]{:S(2)}) collective-permute-start(bf16[512,512]{1,0:T(8,128)(2,1)S(1)} %collective-permute-done.refs_6_), channel_id=1, source_target_pairs={{0,16},{16,0},{1,17},{17,1},{2,18},{18,2},{3,19},{19,3},{4,20},{20... | collective-permute-start | bytes 1572872 | tf_op jit(solution)/shard_map/ppermute | solution.py:427
  21.3 12.3 %collective-permute-done.3.refs_8_ = bf16[512,512]{1,0:T(8,128)(2,1)S(1)} collective-permute-done((bf16[512,512]{1,0:T(8,128)(2,1)S(1)}, bf16[512,512]{1,0:T(8,128)(2,1)S(1)}, u32[]{:S(2)}, u32[]{:S(2)}) %collective-permute-start.3) | collective-permute-done | bytes 524320 | tf_op jit(solution)/shard_map/ppermute | solution.py:420
  35.1 1.5 %collective-permute-start.7 = (bf16[4,128,256]{2,1,0:T(8,128)(2,1)}, bf16[4,128,256]{2,1,0:T(8,128)(2,1)S(1)}, u32[]{:S(2)}, u32[]{:S(2)}) collective-permute-start(bf16[4,128,256]{2,1,0:T(8,128)(2,1)} %copy-done.4), channel_id=1, source_target_pairs={{0,8},{8,0},{1,9},{9,1},{2,10},{10,2},{3,11},{11,3},{4,12},{12,4},... | collective-permute-start | bytes 786440 | tf_op jit(solution)/shard_map/ppermute | solution.py:200
  36.6 7.4 %collective-permute-done.7.far_ref.refs_9_ = bf16[4,128,256]{2,1,0:T(8,128)(2,1)S(1)} collective-permute-done((bf16[4,128,256]{2,1,0:T(8,128)(2,1)}, bf16[4,128,256]{2,1,0:T(8,128)(2,1)S(1)}, u32[]{:S(2)}, u32[]{:S(2)}) %collective-permute-start.7) | collective-permute-done | bytes 262176 | tf_op jit(solution)/shard_map/ppermute | solution.py:200
  44.0 4.3 %collective-permute-done.5.refs_10_ = bf16[512,512]{1,0:T(8,128)(2,1)S(1)} collective-permute-done((bf16[512,512]{1,0:T(8,128)(2,1)S(1)}, bf16[512,512]{1,0:T(8,128)(2,1)S(1)}, u32[]{:S(2)}, u32[]{:S(2)}) %collective-permute-start.5) | collective-permute-done | bytes 524320 | tf_op jit(solution)/shard_map/ppermute | solution.py:420
  49.6 3.6 %collective-permute-start.13 = (bf16[2,128,256]{2,1,0:T(8,128)(2,1)S(1)}, bf16[2,128,256]{2,1,0:T(8,128)(2,1)S(1)}, u32[]{:S(2)}, u32[]{:S(2)}) collective-permute-start(bf16[2,128,256]{2,1,0:T(8,128)(2,1)S(1)} %get-tuple-element.93), channel_id=1, source_target_pairs={{0,3},{1,0},{2,1},{3,2},{4,7},{5,4},{6,5},{7,6},{8,11},{9,8},{10,9... | collective-permute-start | bytes 393224 | tf_op jit(solution)/shard_map/ppermute | solution.py:420
  53.2 4.5 %terms.1 = (f32[512,512]{1,0:T(8,128)S(1)}, bf16[512,512]{1,0:T(8,128)(2,1)S(1)}) custom-call(s32[8]{0:T(128)S(1)} %stack.47.rows_ref, bf16[128,4096]{1,0:T(8,128)(2,1)S(1)} %bitcast.30, bf16[128,4096]{1,0:T(8,128)(2,1)S(1)} %collective-permute-done.9.refs_1_, bf16[128,4096]{1,0:T(8,128)(2,1)} %collective-permute-done.1.refs_2_, ...), custom_call_target="tpu_custom_call" | custom-call | tf_op jit(solution)/shard_map/terms/pallas_call | solution.py:471
  61.5 1.8 %collective-permute-start.15 = (bf16[512,128]{1,0:T(8,128)(2,1)S(1)}, bf16[512,128]{1,0:T(8,128)(2,1)S(1)}, u32[]{:S(2)}, u32[]{:S(2)}) collective-permute-start(bf16[512,128]{1,0:T(8,128)(2,1)S(1)} %get-tuple-element.96), channel_id=1, source_target_pairs={{0,2},{1,3},{2,0},{3,1},{4,6},{5,7},{6,4},{7,5},{8,10},{9,11},{10,... | collective-permute-start | bytes 393224 | tf_op jit(solution)/shard_map/ppermute | solution.py:420
  64.4 3.5 %collective-permute-done.14.refs_1_ = bf16[512,128]{1,0:T(8,128)(2,1)S(1)} collective-permute-done((bf16[512,128]{1,0:T(8,128)(2,1)S(1)}, bf16[512,128]{1,0:T(8,128)(2,1)S(1)}, u32[]{:S(2)}, u32[]{:S(2)}) %collective-permute-start.14) | collective-permute-done | bytes 131104 | tf_op jit(solution)/shard_map/ppermute | solution.py:420
  67.9 3.8 %collective-permute-done.15.refs_2_ = bf16[512,128]{1,0:T(8,128)(2,1)S(1)} collective-permute-done((bf16[512,128]{1,0:T(8,128)(2,1)S(1)}, bf16[512,128]{1,0:T(8,128)(2,1)S(1)}, u32[]{:S(2)}, u32[]{:S(2)}) %collective-permute-start.15) | collective-permute-done | bytes 131104 | tf_op jit(solution)/shard_map/ppermute | solution.py:420
  73.2 4.1 %attention.1 = (bf16[4,128,256]{2,1,0:T(8,128)(2,1)S(1)}, bf16[128,256]{1,0:T(8,128)(2,1)S(1)}, bf16[128,256]{1,0:T(8,128)(2,1)S(1)}, bf16[128,256]{1,0:T(8,128)(2,1)S(1)}, bf16[128,256]{1,0:T(8,128)(2,1)S(1)}) custom-call(s32[1,8]{1,0:T(1,128)S(1)} %copy-done.3, s32[2]{0:T(128)S(1)} %pad_add_fusion.place_ref, ...), custom_call_target="tpu_custom_call" | custom-call | tf_op jit(solution)/shard_map/attention/pallas_call | solution.py:506
  78.1 2.9 %collective-permute-start.21 = (bf16[128,256]{1,0:T(8,128)(2,1)S(1)}, bf16[128,256]{1,0:T(8,128)(2,1)S(1)}, u32[]{:S(2)}, u32[]{:S(2)}) collective-permute-start(bf16[128,256]{1,0:T(8,128)(2,1)S(1)} %get-tuple-element.103), channel_id=1, source_target_pairs={{0,1},{1,2},{2,3},{3,0},{4,5},{5,6},{6,7},{7,4},{8,9},{9,10},{10,1... | collective-permute-start | bytes 196616 | tf_op jit(solution)/shard_map/ppermute | solution.py:420
  81.1 1.4 %collective-permute-start.22 = (bf16[128,256]{1,0:T(8,128)(2,1)S(1)}, bf16[128,256]{1,0:T(8,128)(2,1)S(1)}, u32[]{:S(2)}, u32[]{:S(2)}) collective-permute-start(bf16[128,256]{1,0:T(8,128)(2,1)S(1)} %get-tuple-element.104), channel_id=1, source_target_pairs={{0,2},{1,3},{2,0},{3,1},{4,6},{5,7},{6,4},{7,5},{8,10},{9,11},{10,... | collective-permute-start | bytes 196616 | tf_op jit(solution)/shard_map/ppermute | solution.py:420
  83.4 2.5 %collective-permute-done.24.refs_4_ = bf16[4,128,256]{2,1,0:T(8,128)(2,1)S(1)} collective-permute-done((bf16[4,128,256]{2,1,0:T(8,128)(2,1)S(1)}, bf16[4,128,256]{2,1,0:T(8,128)(2,1)S(1)}, u32[]{:S(2)}, u32[]{:S(2)}) %collective-permute-start.24) | collective-permute-done | bytes 262176 | tf_op jit(solution)/shard_map/ppermute | solution.py:200
  86.0 2.0 %collective-permute-start.25 = (bf16[128,256]{1,0:T(8,128)(2,1)S(1)}, bf16[128,256]{1,0:T(8,128)(2,1)S(1)}, u32[]{:S(2)}, u32[]{:S(2)}) collective-permute-start(bf16[128,256]{1,0:T(8,128)(2,1)S(1)} %get-tuple-element.109), channel_id=1, source_target_pairs={{0,1},{1,2},{2,3},{3,0},{4,5},{5,6},{6,7},{7,4},{8,9},{9,10},{10,1... | collective-permute-start | bytes 196616 | tf_op jit(solution)/shard_map/ppermute | solution.py:420
  88.0 1.6 %collective-permute-start.26 = (bf16[128,256]{1,0:T(8,128)(2,1)S(1)}, bf16[128,256]{1,0:T(8,128)(2,1)S(1)}, u32[]{:S(2)}, u32[]{:S(2)}) collective-permute-start(bf16[128,256]{1,0:T(8,128)(2,1)S(1)} %get-tuple-element.108), channel_id=1, source_target_pairs={{0,2},{1,3},{2,0},{3,1},{4,6},{5,7},{6,4},{7,5},{8,10},{9,11},{10,... | collective-permute-start | bytes 196616 | tf_op jit(solution)/shard_map/ppermute | solution.py:420
  90.4 2.1 %collective-permute-done.25.refs_5_ = bf16[128,256]{1,0:T(8,128)(2,1)S(1)} collective-permute-done((bf16[128,256]{1,0:T(8,128)(2,1)S(1)}, bf16[128,256]{1,0:T(8,128)(2,1)S(1)}, u32[]{:S(2)}, u32[]{:S(2)}) %collective-permute-start.25) | collective-permute-done | bytes 65568 | tf_op jit(solution)/shard_map/ppermute | solution.py:420
  92.5 2.1 %collective-permute-done.26.refs_6_ = bf16[128,256]{1,0:T(8,128)(2,1)S(1)} collective-permute-done((bf16[128,256]{1,0:T(8,128)(2,1)S(1)}, bf16[128,256]{1,0:T(8,128)(2,1)S(1)}, u32[]{:S(2)}, u32[]{:S(2)}) %collective-permute-start.26) | collective-permute-done | bytes 65568 | tf_op jit(solution)/shard_map/ppermute | solution.py:420
  (66 shorter events, 21.5 us)
Async XLA Ops:
  1.6 17.0 %collective-permute-start = (bf16[512,512]{1,0:T(8,128)(2,1)S(1)}, bf16[512,512]{1,0:T(8,128)(2,1)S(1)}, u32[]{:S(2)}, u32[]{:S(2)}) collective-permute-start(bf16[512,512]{1,0:T(8,128)(2,1)S(1)} %constant_dynamic-slice_fusion.refs_4_), channel_id=1, source_target_pairs={{0,1},{1,2},{2,3},{3,0},{4,5},{5,6},{6,7},{7,4},{8,9},{9,10},{10,1... | collective-permute-start | bytes 1572872 | tf_op jit(solution)/shard_map/ppermute | solution.py:420
  4.7 14.0 %collective-permute-start.2 = (bf16[512,512]{1,0:T(8,128)(2,1)S(1)}, bf16[512,512]{1,0:T(8,128)(2,1)}, u32[]{:S(2)}, u32[]{:S(2)}) collective-permute-start(bf16[512,512]{1,0:T(8,128)(2,1)S(1)} %constant_dynamic-slice_fusion.refs_4_), channel_id=1, source_target_pairs={{0,16},{16,0},{1,17},{17,1},{2,18},{18,2},{3,19},{19,3},{4,20},{20... | collective-permute-start | bytes 1572872 | tf_op jit(solution)/shard_map/ppermute | solution.py:427
  6.2 28.6 %collective-permute-start.1 = (bf16[128,4096]{1,0:T(8,128)(2,1)}, bf16[128,4096]{1,0:T(8,128)(2,1)}, u32[]{:S(2)}, u32[]{:S(2)}) collective-permute-start(bf16[128,4096]{1,0:T(8,128)(2,1)} %bitcast.28), channel_id=1, source_target_pairs={{0,8},{8,0},{1,9},{9,1},{2,10},{10,2},{3,11},{11,3},{4,12},{12,4},... | collective-permute-start | bytes 3145736 | tf_op jit(solution)/shard_map/ppermute | solution.py:200
  18.7 14.9 %collective-permute-start.3 = (bf16[512,512]{1,0:T(8,128)(2,1)S(1)}, bf16[512,512]{1,0:T(8,128)(2,1)S(1)}, u32[]{:S(2)}, u32[]{:S(2)}) collective-permute-start(bf16[512,512]{1,0:T(8,128)(2,1)S(1)} %collective-permute-done.refs_6_), channel_id=1, source_target_pairs={{0,1},{1,2},{2,3},{3,0},{4,5},{5,6},{6,7},{7,4},{8,9},{9,10},{10,1... | collective-permute-start | bytes 1572872 | tf_op jit(solution)/shard_map/ppermute | solution.py:420
  19.8 13.8 %collective-permute-start.4 = (bf16[512,512]{1,0:T(8,128)(2,1)S(1)}, bf16[512,512]{1,0:T(8,128)(2,1)S(1)}, u32[]{:S(2)}, u32[]{:S(2)}) collective-permute-start(bf16[512,512]{1,0:T(8,128)(2,1)S(1)} %collective-permute-done.refs_6_), channel_id=1, source_target_pairs={{0,16},{16,0},{1,17},{17,1},{2,18},{18,2},{3,19},{19,3},{4,20},{20... | collective-permute-start | bytes 1572872 | tf_op jit(solution)/shard_map/ppermute | solution.py:427
  21.3 28.3 %collective-permute-start.9 = (bf16[128,4096]{1,0:T(8,128)(2,1)}, bf16[128,4096]{1,0:T(8,128)(2,1)S(1)}, u32[]{:S(2)}, u32[]{:S(2)}) collective-permute-start(bf16[128,4096]{1,0:T(8,128)(2,1)} %bitcast.29), channel_id=1, source_target_pairs={{0,4},{4,0},{1,5},{5,1},{2,6},{6,2},{3,7},{7,3},{8,12},{12,8},{9,1... | collective-permute-start | bytes 3145736 | tf_op jit(solution)/shard_map/ppermute | solution.py:200
  33.6 14.7 %collective-permute-start.6 = (bf16[512,512]{1,0:T(8,128)(2,1)S(1)}, bf16[512,512]{1,0:T(8,128)(2,1)S(1)}, u32[]{:S(2)}, u32[]{:S(2)}) collective-permute-start(bf16[512,512]{1,0:T(8,128)(2,1)S(1)} %collective-permute-done.3.refs_8_), channel_id=1, source_target_pairs={{0,16},{16,0},{1,17},{17,1},{2,18},{18,2},{3,19},{19,3},{4,20},{20... | collective-permute-start | bytes 1572872 | tf_op jit(solution)/shard_map/ppermute | solution.py:427
  34.9 13.5 %collective-permute-start.5 = (bf16[512,512]{1,0:T(8,128)(2,1)S(1)}, bf16[512,512]{1,0:T(8,128)(2,1)S(1)}, u32[]{:S(2)}, u32[]{:S(2)}) collective-permute-start(bf16[512,512]{1,0:T(8,128)(2,1)S(1)} %collective-permute-done.3.refs_8_), channel_id=1, source_target_pairs={{0,1},{1,2},{2,3},{3,0},{4,5},{5,6},{6,7},{7,4},{8,9},{9,10},{10,1... | collective-permute-start | bytes 1572872 | tf_op jit(solution)/shard_map/ppermute | solution.py:420
  35.1 18.1 %collective-permute-start.10 = (bf16[128,4096]{1,0:T(8,128)(2,1)}, bf16[128,4096]{1,0:T(8,128)(2,1)S(1)}, u32[]{:S(2)}, u32[]{:S(2)}) collective-permute-start(bf16[128,4096]{1,0:T(8,128)(2,1)} %collective-permute-done.1.refs_2_), channel_id=1, source_target_pairs={{0,4},{4,0},{1,5},{5,1},{2,6},{6,2},{3,7},{7,3},{8,12},{12,8},{9,1... | collective-permute-start | bytes 3145736 | tf_op jit(solution)/shard_map/ppermute | solution.py:200
  35.1 8.9 %collective-permute-start.7 = (bf16[4,128,256]{2,1,0:T(8,128)(2,1)}, bf16[4,128,256]{2,1,0:T(8,128)(2,1)S(1)}, u32[]{:S(2)}, u32[]{:S(2)}) collective-permute-start(bf16[4,128,256]{2,1,0:T(8,128)(2,1)} %copy-done.4), channel_id=1, source_target_pairs={{0,8},{8,0},{1,9},{9,1},{2,10},{10,2},{3,11},{11,3},{4,12},{12,4},... | collective-permute-start | bytes 786440 | tf_op jit(solution)/shard_map/ppermute | solution.py:200
  48.3 10.7 %collective-permute-start.8 = (bf16[512,512]{1,0:T(8,128)(2,1)S(1)}, bf16[512,512]{1,0:T(8,128)(2,1)S(1)}, u32[]{:S(2)}, u32[]{:S(2)}) collective-permute-start(bf16[512,512]{1,0:T(8,128)(2,1)S(1)} %collective-permute-done.5.refs_10_), channel_id=1, source_target_pairs={{0,16},{16,0},{1,17},{17,1},{2,18},{18,2},{3,19},{19,3},{4,20},{20... | collective-permute-start | bytes 1572872 | tf_op jit(solution)/shard_map/ppermute | solution.py:427
  49.3 11.1 %collective-permute-start.11 = (bf16[2,128,256]{2,1,0:T(8,128)(2,1)S(1)}, bf16[2,128,256]{2,1,0:T(8,128)(2,1)S(1)}, u32[]{:S(2)}, u32[]{:S(2)}) collective-permute-start(bf16[2,128,256]{2,1,0:T(8,128)(2,1)S(1)} %get-tuple-element.91), channel_id=1, source_target_pairs={{0,1},{1,2},{2,3},{3,0},{4,5},{5,6},{6,7},{7,4},{8,9},{9,10},{10,1... | collective-permute-start | bytes 393224 | tf_op jit(solution)/shard_map/ppermute | solution.py:420
  49.3 11.2 %collective-permute-start.12 = (bf16[2,128,256]{2,1,0:T(8,128)(2,1)S(1)}, bf16[2,128,256]{2,1,0:T(8,128)(2,1)S(1)}, u32[]{:S(2)}, u32[]{:S(2)}) collective-permute-start(bf16[2,128,256]{2,1,0:T(8,128)(2,1)S(1)} %get-tuple-element.92), channel_id=1, source_target_pairs={{0,2},{1,3},{2,0},{3,1},{4,6},{5,7},{6,4},{7,5},{8,10},{9,11},{10,... | collective-permute-start | bytes 393224 | tf_op jit(solution)/shard_map/ppermute | solution.py:420
  49.6 10.9 %collective-permute-start.13 = (bf16[2,128,256]{2,1,0:T(8,128)(2,1)S(1)}, bf16[2,128,256]{2,1,0:T(8,128)(2,1)S(1)}, u32[]{:S(2)}, u32[]{:S(2)}) collective-permute-start(bf16[2,128,256]{2,1,0:T(8,128)(2,1)S(1)} %get-tuple-element.93), channel_id=1, source_target_pairs={{0,3},{1,0},{2,1},{3,2},{4,7},{5,4},{6,5},{7,6},{8,11},{9,8},{10,9... | collective-permute-start | bytes 393224 | tf_op jit(solution)/shard_map/ppermute | solution.py:420
  60.5 7.4 %collective-permute-start.14 = (bf16[512,128]{1,0:T(8,128)(2,1)S(1)}, bf16[512,128]{1,0:T(8,128)(2,1)S(1)}, u32[]{:S(2)}, u32[]{:S(2)}) collective-permute-start(bf16[512,128]{1,0:T(8,128)(2,1)S(1)} %get-tuple-element.95), channel_id=1, source_target_pairs={{0,1},{1,2},{2,3},{3,0},{4,5},{5,6},{6,7},{7,4},{8,9},{9,10},{10,1... | collective-permute-start | bytes 393224 | tf_op jit(solution)/shard_map/ppermute | solution.py:420
  61.5 10.2 %collective-permute-start.15 = (bf16[512,128]{1,0:T(8,128)(2,1)S(1)}, bf16[512,128]{1,0:T(8,128)(2,1)S(1)}, u32[]{:S(2)}, u32[]{:S(2)}) collective-permute-start(bf16[512,128]{1,0:T(8,128)(2,1)S(1)} %get-tuple-element.96), channel_id=1, source_target_pairs={{0,2},{1,3},{2,0},{3,1},{4,6},{5,7},{6,4},{7,5},{8,10},{9,11},{10,... | collective-permute-start | bytes 393224 | tf_op jit(solution)/shard_map/ppermute | solution.py:420
  63.3 8.4 %collective-permute-start.16 = (bf16[512,128]{1,0:T(8,128)(2,1)S(1)}, bf16[512,128]{1,0:T(8,128)(2,1)S(1)}, u32[]{:S(2)}, u32[]{:S(2)}) collective-permute-start(bf16[512,128]{1,0:T(8,128)(2,1)S(1)} %get-tuple-element.97), channel_id=1, source_target_pairs={{0,3},{1,0},{2,1},{3,2},{4,7},{5,4},{6,5},{7,6},{8,11},{9,8},{10,9... | collective-permute-start | bytes 393224 | tf_op jit(solution)/shard_map/ppermute | solution.py:420
  64.4 7.8 %collective-permute-start.17 = (bf16[512,128]{1,0:T(8,128)(2,1)S(1)}, bf16[512,128]{1,0:T(8,128)(2,1)S(1)}, u32[]{:S(2)}, u32[]{:S(2)}) collective-permute-start(bf16[512,128]{1,0:T(8,128)(2,1)S(1)} %get-tuple-element.94.refs_0_), channel_id=1, source_target_pairs={{0,4},{4,0},{1,5},{5,1},{2,6},{6,2},{3,7},{7,3},{8,12},{12,8},{9,1... | collective-permute-start | bytes 393224 | tf_op jit(solution)/shard_map/ppermute | solution.py:200
  77.3 8.6 %collective-permute-start.24 = (bf16[4,128,256]{2,1,0:T(8,128)(2,1)S(1)}, bf16[4,128,256]{2,1,0:T(8,128)(2,1)S(1)}, u32[]{:S(2)}, u32[]{:S(2)}) collective-permute-start(bf16[4,128,256]{2,1,0:T(8,128)(2,1)S(1)} %get-tuple-element.106), channel_id=1, source_target_pairs={{0,8},{8,0},{1,9},{9,1},{2,10},{10,2},{3,11},{11,3},{4,12},{12,4},... | collective-permute-start | bytes 786440 | tf_op jit(solution)/shard_map/ppermute | solution.py:200
  78.1 11.5 %collective-permute-start.21 = (bf16[128,256]{1,0:T(8,128)(2,1)S(1)}, bf16[128,256]{1,0:T(8,128)(2,1)S(1)}, u32[]{:S(2)}, u32[]{:S(2)}) collective-permute-start(bf16[128,256]{1,0:T(8,128)(2,1)S(1)} %get-tuple-element.103), channel_id=1, source_target_pairs={{0,1},{1,2},{2,3},{3,0},{4,5},{5,6},{6,7},{7,4},{8,9},{9,10},{10,1... | collective-permute-start | bytes 196616 | tf_op jit(solution)/shard_map/ppermute | solution.py:420
  81.1 9.3 %collective-permute-start.22 = (bf16[128,256]{1,0:T(8,128)(2,1)S(1)}, bf16[128,256]{1,0:T(8,128)(2,1)S(1)}, u32[]{:S(2)}, u32[]{:S(2)}) collective-permute-start(bf16[128,256]{1,0:T(8,128)(2,1)S(1)} %get-tuple-element.104), channel_id=1, source_target_pairs={{0,2},{1,3},{2,0},{3,1},{4,6},{5,7},{6,4},{7,5},{8,10},{9,11},{10,... | collective-permute-start | bytes 196616 | tf_op jit(solution)/shard_map/ppermute | solution.py:420
  82.5 7.9 %collective-permute-start.23 = (bf16[128,256]{1,0:T(8,128)(2,1)S(1)}, bf16[128,256]{1,0:T(8,128)(2,1)S(1)}, u32[]{:S(2)}, u32[]{:S(2)}) collective-permute-start(bf16[128,256]{1,0:T(8,128)(2,1)S(1)} %get-tuple-element.105), channel_id=1, source_target_pairs={{0,3},{1,0},{2,1},{3,2},{4,7},{5,4},{6,5},{7,6},{8,11},{9,8},{10,9... | collective-permute-start | bytes 196616 | tf_op jit(solution)/shard_map/ppermute | solution.py:420
  86.0 6.6 %collective-permute-start.25 = (bf16[128,256]{1,0:T(8,128)(2,1)S(1)}, bf16[128,256]{1,0:T(8,128)(2,1)S(1)}, u32[]{:S(2)}, u32[]{:S(2)}) collective-permute-start(bf16[128,256]{1,0:T(8,128)(2,1)S(1)} %get-tuple-element.109), channel_id=1, source_target_pairs={{0,1},{1,2},{2,3},{3,0},{4,5},{5,6},{6,7},{7,4},{8,9},{9,10},{10,1... | collective-permute-start | bytes 196616 | tf_op jit(solution)/shard_map/ppermute | solution.py:420
  88.0 6.7 %collective-permute-start.26 = (bf16[128,256]{1,0:T(8,128)(2,1)S(1)}, bf16[128,256]{1,0:T(8,128)(2,1)S(1)}, u32[]{:S(2)}, u32[]{:S(2)}) collective-permute-start(bf16[128,256]{1,0:T(8,128)(2,1)S(1)} %get-tuple-element.108), channel_id=1, source_target_pairs={{0,2},{1,3},{2,0},{3,1},{4,6},{5,7},{6,4},{7,5},{8,10},{9,11},{10,... | collective-permute-start | bytes 196616 | tf_op jit(solution)/shard_map/ppermute | solution.py:420
  (12 other events, 78.1 us)

commit v6 on v5

--- a/solution.py
+++ b/solution.py
@@ -294,7 +294,7 @@
     for distance in range(blocks):
         block = lax.rem(block_here + blocks - distance, blocks)
         near, far = refs[distance], refs[blocks + distance]
-        for source, rows in ((chip, near[...]), (1 - chip, far[0] if distance == 0 else far[...])):
+        for source, rows in ((chip, near[...]), (1 - chip, far[...] if distance else far[far.shape[0] - 1])):
             pair = source * blocks + block
             out_ref[:, pl.ds(pl.multiple_of(pair * width, width), width)] = rows
 
@@ -304,7 +304,7 @@
     blocks = spans // 2
     mine_refs, theirs_refs = refs[:blocks], refs[blocks : 2 * blocks]
     near_query, far_query, *packed_queries = refs[2 * blocks : 3 * blocks + 1]
-    far_ref, *near_refs = refs[3 * blocks + 1 : -4]
+    first_far_ref, last_far_ref, *near_refs = refs[3 * blocks + 1 : -4]
     key_rows, value_rows, query_rows, out_rows = refs[-4:]
     token_rows = query_rows.shape[1]
     span_rows = 2 * token_rows
@@ -367,7 +367,11 @@
     for distance, near_ref in enumerate(near_refs):
         block = lax.rem(block_here + distance, blocks)
         near_ref[...] = out_rows[2 * block + chip]
-        far_ref[distance] = out_rows[2 * block + 1 - chip]
+    order = [*far_first(blocks), 0]
+    for index, distance in enumerate(order):
+        block = lax.rem(block_here + distance, blocks)
+        half, place_in_half = divmod(index, blocks // 2)
+        (first_far_ref, last_far_ref)[half][place_in_half] = out_rows[2 * block + 1 - chip]
 
 
 VMEM = pl.BlockSpec(memory_space=pltpu.VMEM)
@@ -503,11 +507,12 @@
     in_order = range(cycle_size)
 
     sequence_rows = cycle_size * block_rows
-    far, *near = pl.pallas_call(
+    half = jax.ShapeDtypeStruct((cycle_size // 2, *one.shape), one.dtype)
+    first_far, last_far, *near = pl.pallas_call(
         attention_kernel,
-        out_shape=[by_distance] + [one] * cycle_size,
+        out_shape=[half, half] + [one] * cycle_size,
         in_specs=[SMEM, SMEM] + [VMEM] * (3 * cycle_size + 1),
-        out_specs=[VMEM] * (cycle_size + 1),
+        out_specs=[VMEM] * (cycle_size + 2),
         scratch_shapes=[
             pltpu.VMEM((sequence_rows, HD), jnp.bfloat16),
             pltpu.VMEM((sequence_rows, HD), jnp.bfloat16),
@@ -525,9 +530,12 @@
         far_queries,
         *packed,
     )
-    far = exchange(far, "chip", 1)
+    halves = [exchange(half, "chip", 1) for half in (first_far, last_far)]
     arrived = [near[0], *along_blocks(near)]
-    crossed = [far, *along_blocks(far)]
+    crossed = {0: halves[1]}
+    for index, distance in enumerate(far_first(cycle_size)):
+        part, place_in_half = divmod(index, cycle_size // 2)
+        crossed[distance] = ahead(halves[part][place_in_half], distance)
     heads = pl.pallas_call(
         order_heads_kernel,
         out_shape=jax.ShapeDtypeStruct((token_rows, QH * HD), jnp.bfloat16),
@@ -535,7 +543,7 @@
         out_specs=VMEM,
         compiler_params=pltpu.CompilerParams(vmem_limit_bytes=8 * 1024 * 1024),
         name="order_heads",
-    )(place, *arrived, *crossed)
+    )(place, *arrived, *(crossed[distance] for distance in in_order))
     return heads[None]
 
 

time: 96.3 us -> 94.7 us (0.983)
  waiting for transfers between devices: 42.6 us -> 38.6 us
  starting transfers between devices: 31.5 us -> 33.9 us
    ppermute x9 -> x10, waiting for transfers between devices: 11 us -> 8.5 us  [exchange(): return lax.ppermute(block, axis, [(i, i ^ distance) for i in range(size)])]
    ppermute x15, waiting for transfers between devices: 30.2 us -> 28.2 us  [ahead(): lax.ppermute(block, 'blk', [(i, (i + distance) % cycle_size) for i in ran...]
    ppermute x9 -> x10, starting transfers between devices: 4.29 us -> 5.59 us  [exchange(): return lax.ppermute(block, axis, [(i, i ^ distance) for i in range(size)])]
  transfers between devices with their start and end apart: 28 -> 29, of which waited for: 12 -> 10; matrix products, arithmetic and copies ran while one was open for 6% -> 6% of each run, Pallas kernels for 7% -> 7%
where the time goes in v6:
time: 94.7 us; the launch traced here: 94.5 us
  waiting for transfers between devices  38.6 us (41%)
  starting transfers between devices  33.9 us (36%)
  Pallas kernels  12.2 us (13%)
  local copies, waits for them, and re-layouts  4.96 us (5%)
  other arithmetic  4.58 us (5%)
    ppermute x15, waiting for transfers between devices, ahead(): lax.ppermute(block, 'blk', [(i, (i + distance) % cycle_size) for i in ran...  28.2 us
    ppermute x15, starting transfers between devices, ahead(): lax.ppermute(block, 'blk', [(i, (i + distance) % cycle_size) for i in ran...  22.7 us
    ppermute x10, waiting for transfers between devices, exchange(): return lax.ppermute(block, axis, [(i, i ^ distance) for i in range(size)])  8.5 us
    ppermute x10, starting transfers between devices, exchange(): return lax.ppermute(block, axis, [(i, i ^ distance) for i in range(size)])  5.59 us
    ppermute x4, starting transfers between devices, across(): lax.ppermute(block, 'dp', [(i, dp_size - 1 - i) for i in range(dp_size)])  5.55 us
    pallas_call x1, Pallas kernels, whole_cycle_shards(): pl.pallas_call(functools.partial(terms_kernel, ulysses_size, len(received...  4.46 us
    pallas_call x1, Pallas kernels, whole_cycle_shards(): pl.pallas_call(attention_kernel, out_shape=[half, half] + [one] * cycle_s...  4.1 us
    unnamed x16, local copies, waits for them, and re-layouts  3.5 us
  transfers between devices with their start and end apart: 29, of which 10 were waited for; matrix products, arithmetic and copies ran while one was open for 6% of the time, Pallas kernels for 7%

profile of v6, /device:TPU:0, one launch (start us, length us, event | category | flops | bytes accessed | tf_op | source)
XLA Modules:
  0.0 94.5 jit_solution(2770728600255356606)
XLA Ops:
  0.0 1.6 %copy-done = bf16[512,2048]{1,0:T(8,128)(2,1)S(1)} copy-done((bf16[512,2048]{1,0:T(8,128)(2,1)S(1)}, bf16[512,2048]{1,0:T(8,128)(2,1)}, u32[]{:S(2)}) %copy-start) | copy-done | bytes 2097176
  1.6 3.1 %collective-permute-start = (bf16[512,512]{1,0:T(8,128)(2,1)S(1)}, bf16[512,512]{1,0:T(8,128)(2,1)S(1)}, u32[]{:S(2)}, u32[]{:S(2)}) collective-permute-start(bf16[512,512]{1,0:T(8,128)(2,1)S(1)} %constant_dynamic-slice_fusion.refs_4_), channel_id=1, source_target_pairs={{0,1},{1,2},{2,3},{3,0},{4,5},{5,6},{6,7},{7,4},{8,9},{9,10},{10,1... | collective-permute-start | bytes 1572872 | tf_op jit(solution)/shard_map/ppermute | solution.py:424
  4.7 1.5 %collective-permute-start.2 = (bf16[512,512]{1,0:T(8,128)(2,1)S(1)}, bf16[512,512]{1,0:T(8,128)(2,1)}, u32[]{:S(2)}, u32[]{:S(2)}) collective-permute-start(bf16[512,512]{1,0:T(8,128)(2,1)S(1)} %constant_dynamic-slice_fusion.refs_4_), channel_id=1, source_target_pairs={{0,16},{16,0},{1,17},{17,1},{2,18},{18,2},{3,19},{19,3},{4,20},{20... | collective-permute-start | bytes 1572872 | tf_op jit(solution)/shard_map/ppermute | solution.py:431
  6.2 1.5 %collective-permute-start.1 = (bf16[128,4096]{1,0:T(8,128)(2,1)}, bf16[128,4096]{1,0:T(8,128)(2,1)}, u32[]{:S(2)}, u32[]{:S(2)}) collective-permute-start(bf16[128,4096]{1,0:T(8,128)(2,1)} %bitcast.28), channel_id=1, source_target_pairs={{0,8},{8,0},{1,9},{9,1},{2,10},{10,2},{3,11},{11,3},{4,12},{12,4},... | collective-permute-start | bytes 3145736 | tf_op jit(solution)/shard_map/ppermute | solution.py:200
  16.5 2.1 %collective-permute-done.refs_6_ = bf16[512,512]{1,0:T(8,128)(2,1)S(1)} collective-permute-done((bf16[512,512]{1,0:T(8,128)(2,1)S(1)}, bf16[512,512]{1,0:T(8,128)(2,1)S(1)}, u32[]{:S(2)}, u32[]{:S(2)}) %collective-permute-start) | collective-permute-done | bytes 524320 | tf_op jit(solution)/shard_map/ppermute | solution.py:424
  19.8 1.5 %collective-permute-start.4 = (bf16[512,512]{1,0:T(8,128)(2,1)S(1)}, bf16[512,512]{1,0:T(8,128)(2,1)S(1)}, u32[]{:S(2)}, u32[]{:S(2)}) collective-permute-start(bf16[512,512]{1,0:T(8,128)(2,1)S(1)} %collective-permute-done.refs_6_), channel_id=1, source_target_pairs={{0,16},{16,0},{1,17},{17,1},{2,18},{18,2},{3,19},{19,3},{4,20},{20... | collective-permute-start | bytes 1572872 | tf_op jit(solution)/shard_map/ppermute | solution.py:431
  21.3 12.3 %collective-permute-done.3.refs_8_ = bf16[512,512]{1,0:T(8,128)(2,1)S(1)} collective-permute-done((bf16[512,512]{1,0:T(8,128)(2,1)S(1)}, bf16[512,512]{1,0:T(8,128)(2,1)S(1)}, u32[]{:S(2)}, u32[]{:S(2)}) %collective-permute-start.3) | collective-permute-done | bytes 524320 | tf_op jit(solution)/shard_map/ppermute | solution.py:424
  35.1 1.5 %collective-permute-start.7 = (bf16[4,128,256]{2,1,0:T(8,128)(2,1)}, bf16[4,128,256]{2,1,0:T(8,128)(2,1)S(1)}, u32[]{:S(2)}, u32[]{:S(2)}) collective-permute-start(bf16[4,128,256]{2,1,0:T(8,128)(2,1)} %copy-done.4), channel_id=1, source_target_pairs={{0,8},{8,0},{1,9},{9,1},{2,10},{10,2},{3,11},{11,3},{4,12},{12,4},... | collective-permute-start | bytes 786440 | tf_op jit(solution)/shard_map/ppermute | solution.py:200
  36.6 7.4 %collective-permute-done.7.far_ref.refs_9_ = bf16[4,128,256]{2,1,0:T(8,128)(2,1)S(1)} collective-permute-done((bf16[4,128,256]{2,1,0:T(8,128)(2,1)}, bf16[4,128,256]{2,1,0:T(8,128)(2,1)S(1)}, u32[]{:S(2)}, u32[]{:S(2)}) %collective-permute-start.7) | collective-permute-done | bytes 262176 | tf_op jit(solution)/shard_map/ppermute | solution.py:200
  44.0 3.5 %collective-permute-done.5.refs_10_ = bf16[512,512]{1,0:T(8,128)(2,1)S(1)} collective-permute-done((bf16[512,512]{1,0:T(8,128)(2,1)S(1)}, bf16[512,512]{1,0:T(8,128)(2,1)S(1)}, u32[]{:S(2)}, u32[]{:S(2)}) %collective-permute-start.5) | collective-permute-done | bytes 524320 | tf_op jit(solution)/shard_map/ppermute | solution.py:424
  48.6 2.3 %collective-permute-start.12 = (bf16[2,128,256]{2,1,0:T(8,128)(2,1)S(1)}, bf16[2,128,256]{2,1,0:T(8,128)(2,1)S(1)}, u32[]{:S(2)}, u32[]{:S(2)}) collective-permute-start(bf16[2,128,256]{2,1,0:T(8,128)(2,1)S(1)} %get-tuple-element.93), channel_id=1, source_target_pairs={{0,2},{1,3},{2,0},{3,1},{4,6},{5,7},{6,4},{7,5},{8,10},{9,11},{10,... | collective-permute-start | bytes 393224 | tf_op jit(solution)/shard_map/ppermute | solution.py:424
  50.9 1.5 %collective-permute-start.13 = (bf16[2,128,256]{2,1,0:T(8,128)(2,1)S(1)}, bf16[2,128,256]{2,1,0:T(8,128)(2,1)S(1)}, u32[]{:S(2)}, u32[]{:S(2)}) collective-permute-start(bf16[2,128,256]{2,1,0:T(8,128)(2,1)S(1)} %get-tuple-element.94), channel_id=1, source_target_pairs={{0,3},{1,0},{2,1},{3,2},{4,7},{5,4},{6,5},{7,6},{8,11},{9,8},{10,9... | collective-permute-start | bytes 393224 | tf_op jit(solution)/shard_map/ppermute | solution.py:424
  52.4 4.5 %terms.1 = (f32[512,512]{1,0:T(8,128)S(1)}, bf16[512,512]{1,0:T(8,128)(2,1)S(1)}) custom-call(s32[8]{0:T(128)S(1)} %stack.47.rows_ref, bf16[128,4096]{1,0:T(8,128)(2,1)S(1)} %bitcast.30, bf16[128,4096]{1,0:T(8,128)(2,1)S(1)} %collective-permute-done.9.refs_1_, bf16[128,4096]{1,0:T(8,128)(2,1)} %collective-permute-done.1.refs_2_, ...), custom_call_target="tpu_custom_call" | custom-call | tf_op jit(solution)/shard_map/terms/pallas_call | solution.py:475
  56.9 1.9 %collective-permute-done.8.piece_ref = bf16[512,512]{1,0:T(8,128)(2,1)S(1)} collective-permute-done((bf16[512,512]{1,0:T(8,128)(2,1)S(1)}, bf16[512,512]{1,0:T(8,128)(2,1)S(1)}, u32[]{:S(2)}, u32[]{:S(2)}) %collective-permute-start.8) | collective-permute-done | bytes 524320 | tf_op jit(solution)/shard_map/ppermute | solution.py:431
  60.9 2.5 %collective-permute-start.15 = (bf16[512,128]{1,0:T(8,128)(2,1)S(1)}, bf16[512,128]{1,0:T(8,128)(2,1)S(1)}, u32[]{:S(2)}, u32[]{:S(2)}) collective-permute-start(bf16[512,128]{1,0:T(8,128)(2,1)S(1)} %get-tuple-element.97), channel_id=1, source_target_pairs={{0,2},{1,3},{2,0},{3,1},{4,6},{5,7},{6,4},{7,5},{8,10},{9,11},{10,... | collective-permute-start | bytes 393224 | tf_op jit(solution)/shard_map/ppermute | solution.py:424
  64.2 3.1 %collective-permute-done.14.refs_1_ = bf16[512,128]{1,0:T(8,128)(2,1)S(1)} collective-permute-done((bf16[512,128]{1,0:T(8,128)(2,1)S(1)}, bf16[512,128]{1,0:T(8,128)(2,1)S(1)}, u32[]{:S(2)}, u32[]{:S(2)}) %collective-permute-start.14) | collective-permute-done | bytes 131104 | tf_op jit(solution)/shard_map/ppermute | solution.py:424
  67.3 3.8 %collective-permute-done.15.refs_2_ = bf16[512,128]{1,0:T(8,128)(2,1)S(1)} collective-permute-done((bf16[512,128]{1,0:T(8,128)(2,1)S(1)}, bf16[512,128]{1,0:T(8,128)(2,1)S(1)}, u32[]{:S(2)}, u32[]{:S(2)}) %collective-permute-start.15) | collective-permute-done | bytes 131104 | tf_op jit(solution)/shard_map/ppermute | solution.py:424
  72.6 4.1 %attention.1 = (bf16[2,128,256]{2,1,0:T(8,128)(2,1)S(1)}, bf16[2,128,256]{2,1,0:T(8,128)(2,1)S(1)}, bf16[128,256]{1,0:T(8,128)(2,1)S(1)}, bf16[128,256]{1,0:T(8,...) custom-call(s32[1,8]{1,0:T(1,128)S(1)} %copy-done.3, s32[2]{0:T(128)S(1)} %pad_add_fusion.place_ref, ...), custom_call_target="tpu_custom_call" | custom-call | tf_op jit(solution)/shard_map/attention/pallas_call | solution.py:511
  78.8 2.1 %collective-permute-start.21 = (bf16[128,256]{1,0:T(8,128)(2,1)S(1)}, bf16[128,256]{1,0:T(8,128)(2,1)S(1)}, u32[]{:S(2)}, u32[]{:S(2)}) collective-permute-start(bf16[128,256]{1,0:T(8,128)(2,1)S(1)} %get-tuple-element.104), channel_id=1, source_target_pairs={{0,1},{1,2},{2,3},{3,0},{4,5},{5,6},{6,7},{7,4},{8,9},{9,10},{10,1... | collective-permute-start | bytes 196616 | tf_op jit(solution)/shard_map/ppermute | solution.py:424
  80.9 1.6 %collective-permute-start.22 = (bf16[128,256]{1,0:T(8,128)(2,1)S(1)}, bf16[128,256]{1,0:T(8,128)(2,1)S(1)}, u32[]{:S(2)}, u32[]{:S(2)}) collective-permute-start(bf16[128,256]{1,0:T(8,128)(2,1)S(1)} %get-tuple-element.105), channel_id=1, source_target_pairs={{0,2},{1,3},{2,0},{3,1},{4,6},{5,7},{6,4},{7,5},{8,10},{9,11},{10,... | collective-permute-start | bytes 196616 | tf_op jit(solution)/shard_map/ppermute | solution.py:424
  83.3 2.0 %collective-permute-start.26 = (bf16[128,256]{1,0:T(8,128)(2,1)S(1)}, bf16[128,256]{1,0:T(8,128)(2,1)S(1)}, u32[]{:S(2)}, u32[]{:S(2)}) collective-permute-start(bf16[128,256]{1,0:T(8,128)(2,1)S(1)} %get-tuple-element.110), channel_id=1, source_target_pairs={{0,1},{1,2},{2,3},{3,0},{4,5},{5,6},{6,7},{7,4},{8,9},{9,10},{10,1... | collective-permute-start | bytes 196616 | tf_op jit(solution)/shard_map/ppermute | solution.py:424
  85.3 1.6 %collective-permute-start.27 = (bf16[128,256]{1,0:T(8,128)(2,1)S(1)}, bf16[128,256]{1,0:T(8,128)(2,1)S(1)}, u32[]{:S(2)}, u32[]{:S(2)}) collective-permute-start(bf16[128,256]{1,0:T(8,128)(2,1)S(1)} %get-tuple-element.109), channel_id=1, source_target_pairs={{0,2},{1,3},{2,0},{3,1},{4,6},{5,7},{6,4},{7,5},{8,10},{9,11},{10,... | collective-permute-start | bytes 196616 | tf_op jit(solution)/shard_map/ppermute | solution.py:424
  86.9 2.8 %collective-permute-start.28 = (bf16[128,256]{1,0:T(8,128)(2,1)S(1)}, bf16[128,256]{1,0:T(8,128)(2,1)S(1)}, u32[]{:S(2)}, u32[]{:S(2)}) collective-permute-start(bf16[128,256]{1,0:T(8,128)(2,1)S(1)} %slice_bitcast_fusion), channel_id=1, source_target_pairs={{0,3},{1,0},{2,1},{3,2},{4,7},{5,4},{6,5},{7,6},{8,11},{9,8},{10,9... | collective-permute-start | bytes 196616 | tf_op jit(solution)/shard_map/ppermute | solution.py:424
  89.7 3.4 %collective-permute-done.27.refs_6_ = bf16[128,256]{1,0:T(8,128)(2,1)S(1)} collective-permute-done((bf16[128,256]{1,0:T(8,128)(2,1)S(1)}, bf16[128,256]{1,0:T(8,128)(2,1)S(1)}, u32[]{:S(2)}, u32[]{:S(2)}) %collective-permute-start.27) | collective-permute-done | bytes 65568 | tf_op jit(solution)/shard_map/ppermute | solution.py:424
  (69 shorter events, 21.1 us)
Async XLA Ops:
  1.6 17.0 %collective-permute-start = (bf16[512,512]{1,0:T(8,128)(2,1)S(1)}, bf16[512,512]{1,0:T(8,128)(2,1)S(1)}, u32[]{:S(2)}, u32[]{:S(2)}) collective-permute-start(bf16[512,512]{1,0:T(8,128)(2,1)S(1)} %constant_dynamic-slice_fusion.refs_4_), channel_id=1, source_target_pairs={{0,1},{1,2},{2,3},{3,0},{4,5},{5,6},{6,7},{7,4},{8,9},{9,10},{10,1... | collective-permute-start | bytes 1572872 | tf_op jit(solution)/shard_map/ppermute | solution.py:424
  4.7 14.0 %collective-permute-start.2 = (bf16[512,512]{1,0:T(8,128)(2,1)S(1)}, bf16[512,512]{1,0:T(8,128)(2,1)}, u32[]{:S(2)}, u32[]{:S(2)}) collective-permute-start(bf16[512,512]{1,0:T(8,128)(2,1)S(1)} %constant_dynamic-slice_fusion.refs_4_), channel_id=1, source_target_pairs={{0,16},{16,0},{1,17},{17,1},{2,18},{18,2},{3,19},{19,3},{4,20},{20... | collective-permute-start | bytes 1572872 | tf_op jit(solution)/shard_map/ppermute | solution.py:431
  6.2 27.3 %collective-permute-start.1 = (bf16[128,4096]{1,0:T(8,128)(2,1)}, bf16[128,4096]{1,0:T(8,128)(2,1)}, u32[]{:S(2)}, u32[]{:S(2)}) collective-permute-start(bf16[128,4096]{1,0:T(8,128)(2,1)} %bitcast.28), channel_id=1, source_target_pairs={{0,8},{8,0},{1,9},{9,1},{2,10},{10,2},{3,11},{11,3},{4,12},{12,4},... | collective-permute-start | bytes 3145736 | tf_op jit(solution)/shard_map/ppermute | solution.py:200
  18.7 14.9 %collective-permute-start.3 = (bf16[512,512]{1,0:T(8,128)(2,1)S(1)}, bf16[512,512]{1,0:T(8,128)(2,1)S(1)}, u32[]{:S(2)}, u32[]{:S(2)}) collective-permute-start(bf16[512,512]{1,0:T(8,128)(2,1)S(1)} %collective-permute-done.refs_6_), channel_id=1, source_target_pairs={{0,1},{1,2},{2,3},{3,0},{4,5},{5,6},{6,7},{7,4},{8,9},{9,10},{10,1... | collective-permute-start | bytes 1572872 | tf_op jit(solution)/shard_map/ppermute | solution.py:424
  19.8 13.8 %collective-permute-start.4 = (bf16[512,512]{1,0:T(8,128)(2,1)S(1)}, bf16[512,512]{1,0:T(8,128)(2,1)S(1)}, u32[]{:S(2)}, u32[]{:S(2)}) collective-permute-start(bf16[512,512]{1,0:T(8,128)(2,1)S(1)} %collective-permute-done.refs_6_), channel_id=1, source_target_pairs={{0,16},{16,0},{1,17},{17,1},{2,18},{18,2},{3,19},{19,3},{4,20},{20... | collective-permute-start | bytes 1572872 | tf_op jit(solution)/shard_map/ppermute | solution.py:431
  21.3 29.6 %collective-permute-start.9 = (bf16[128,4096]{1,0:T(8,128)(2,1)}, bf16[128,4096]{1,0:T(8,128)(2,1)S(1)}, u32[]{:S(2)}, u32[]{:S(2)}) collective-permute-start(bf16[128,4096]{1,0:T(8,128)(2,1)} %bitcast.29), channel_id=1, source_target_pairs={{0,4},{4,0},{1,5},{5,1},{2,6},{6,2},{3,7},{7,3},{8,12},{12,8},{9,1... | collective-permute-start | bytes 3145736 | tf_op jit(solution)/shard_map/ppermute | solution.py:200
  33.6 14.0 %collective-permute-start.5 = (bf16[512,512]{1,0:T(8,128)(2,1)S(1)}, bf16[512,512]{1,0:T(8,128)(2,1)S(1)}, u32[]{:S(2)}, u32[]{:S(2)}) collective-permute-start(bf16[512,512]{1,0:T(8,128)(2,1)S(1)} %collective-permute-done.3.refs_8_), channel_id=1, source_target_pairs={{0,1},{1,2},{2,3},{3,0},{4,5},{5,6},{6,7},{7,4},{8,9},{9,10},{10,1... | collective-permute-start | bytes 1572872 | tf_op jit(solution)/shard_map/ppermute | solution.py:424
  33.6 14.0 %collective-permute-start.6 = (bf16[512,512]{1,0:T(8,128)(2,1)S(1)}, bf16[512,512]{1,0:T(8,128)(2,1)S(1)}, u32[]{:S(2)}, u32[]{:S(2)}) collective-permute-start(bf16[512,512]{1,0:T(8,128)(2,1)S(1)} %collective-permute-done.3.refs_8_), channel_id=1, source_target_pairs={{0,16},{16,0},{1,17},{17,1},{2,18},{18,2},{3,19},{19,3},{4,20},{20... | collective-permute-start | bytes 1572872 | tf_op jit(solution)/shard_map/ppermute | solution.py:431
  35.1 17.4 %collective-permute-start.10 = (bf16[128,4096]{1,0:T(8,128)(2,1)}, bf16[128,4096]{1,0:T(8,128)(2,1)S(1)}, u32[]{:S(2)}, u32[]{:S(2)}) collective-permute-start(bf16[128,4096]{1,0:T(8,128)(2,1)} %collective-permute-done.1.refs_2_), channel_id=1, source_target_pairs={{0,4},{4,0},{1,5},{5,1},{2,6},{6,2},{3,7},{7,3},{8,12},{12,8},{9,1... | collective-permute-start | bytes 3145736 | tf_op jit(solution)/shard_map/ppermute | solution.py:200
  35.1 8.9 %collective-permute-start.7 = (bf16[4,128,256]{2,1,0:T(8,128)(2,1)}, bf16[4,128,256]{2,1,0:T(8,128)(2,1)S(1)}, u32[]{:S(2)}, u32[]{:S(2)}) collective-permute-start(bf16[4,128,256]{2,1,0:T(8,128)(2,1)} %copy-done.4), channel_id=1, source_target_pairs={{0,8},{8,0},{1,9},{9,1},{2,10},{10,2},{3,11},{11,3},{4,12},{12,4},... | collective-permute-start | bytes 786440 | tf_op jit(solution)/shard_map/ppermute | solution.py:200
  47.6 11.3 %collective-permute-start.8 = (bf16[512,512]{1,0:T(8,128)(2,1)S(1)}, bf16[512,512]{1,0:T(8,128)(2,1)S(1)}, u32[]{:S(2)}, u32[]{:S(2)}) collective-permute-start(bf16[512,512]{1,0:T(8,128)(2,1)S(1)} %collective-permute-done.5.refs_10_), channel_id=1, source_target_pairs={{0,16},{16,0},{1,17},{17,1},{2,18},{18,2},{3,19},{19,3},{4,20},{20... | collective-permute-start | bytes 1572872 | tf_op jit(solution)/shard_map/ppermute | solution.py:431
  48.6 11.6 %collective-permute-start.11 = (bf16[2,128,256]{2,1,0:T(8,128)(2,1)S(1)}, bf16[2,128,256]{2,1,0:T(8,128)(2,1)S(1)}, u32[]{:S(2)}, u32[]{:S(2)}) collective-permute-start(bf16[2,128,256]{2,1,0:T(8,128)(2,1)S(1)} %get-tuple-element.92), channel_id=1, source_target_pairs={{0,1},{1,2},{2,3},{3,0},{4,5},{5,6},{6,7},{7,4},{8,9},{9,10},{10,1... | collective-permute-start | bytes 393224 | tf_op jit(solution)/shard_map/ppermute | solution.py:424
  48.6 11.7 %collective-permute-start.12 = (bf16[2,128,256]{2,1,0:T(8,128)(2,1)S(1)}, bf16[2,128,256]{2,1,0:T(8,128)(2,1)S(1)}, u32[]{:S(2)}, u32[]{:S(2)}) collective-permute-start(bf16[2,128,256]{2,1,0:T(8,128)(2,1)S(1)} %get-tuple-element.93), channel_id=1, source_target_pairs={{0,2},{1,3},{2,0},{3,1},{4,6},{5,7},{6,4},{7,5},{8,10},{9,11},{10,... | collective-permute-start | bytes 393224 | tf_op jit(solution)/shard_map/ppermute | solution.py:424
  50.9 9.4 %collective-permute-start.13 = (bf16[2,128,256]{2,1,0:T(8,128)(2,1)S(1)}, bf16[2,128,256]{2,1,0:T(8,128)(2,1)S(1)}, u32[]{:S(2)}, u32[]{:S(2)}) collective-permute-start(bf16[2,128,256]{2,1,0:T(8,128)(2,1)S(1)} %get-tuple-element.94), channel_id=1, source_target_pairs={{0,3},{1,0},{2,1},{3,2},{4,7},{5,4},{6,5},{7,6},{8,11},{9,8},{10,9... | collective-permute-start | bytes 393224 | tf_op jit(solution)/shard_map/ppermute | solution.py:424
  60.3 7.0 %collective-permute-start.14 = (bf16[512,128]{1,0:T(8,128)(2,1)S(1)}, bf16[512,128]{1,0:T(8,128)(2,1)S(1)}, u32[]{:S(2)}, u32[]{:S(2)}) collective-permute-start(bf16[512,128]{1,0:T(8,128)(2,1)S(1)} %get-tuple-element.96), channel_id=1, source_target_pairs={{0,1},{1,2},{2,3},{3,0},{4,5},{5,6},{6,7},{7,4},{8,9},{9,10},{10,1... | collective-permute-start | bytes 393224 | tf_op jit(solution)/shard_map/ppermute | solution.py:424
  60.9 10.2 %collective-permute-start.15 = (bf16[512,128]{1,0:T(8,128)(2,1)S(1)}, bf16[512,128]{1,0:T(8,128)(2,1)S(1)}, u32[]{:S(2)}, u32[]{:S(2)}) collective-permute-start(bf16[512,128]{1,0:T(8,128)(2,1)S(1)} %get-tuple-element.97), channel_id=1, source_target_pairs={{0,2},{1,3},{2,0},{3,1},{4,6},{5,7},{6,4},{7,5},{8,10},{9,11},{10,... | collective-permute-start | bytes 393224 | tf_op jit(solution)/shard_map/ppermute | solution.py:424
  63.3 7.7 %collective-permute-start.16 = (bf16[512,128]{1,0:T(8,128)(2,1)S(1)}, bf16[512,128]{1,0:T(8,128)(2,1)S(1)}, u32[]{:S(2)}, u32[]{:S(2)}) collective-permute-start(bf16[512,128]{1,0:T(8,128)(2,1)S(1)} %get-tuple-element.98), channel_id=1, source_target_pairs={{0,3},{1,0},{2,1},{3,2},{4,7},{5,4},{6,5},{7,6},{8,11},{9,8},{10,9... | collective-permute-start | bytes 393224 | tf_op jit(solution)/shard_map/ppermute | solution.py:424
  64.2 7.4 %collective-permute-start.17 = (bf16[512,128]{1,0:T(8,128)(2,1)S(1)}, bf16[512,128]{1,0:T(8,128)(2,1)S(1)}, u32[]{:S(2)}, u32[]{:S(2)}) collective-permute-start(bf16[512,128]{1,0:T(8,128)(2,1)S(1)} %get-tuple-element.95.refs_0_), channel_id=1, source_target_pairs={{0,4},{4,0},{1,5},{5,1},{2,6},{6,2},{3,7},{7,3},{8,12},{12,8},{9,1... | collective-permute-start | bytes 393224 | tf_op jit(solution)/shard_map/ppermute | solution.py:200
  76.7 6.6 %collective-permute-start.25 = (bf16[2,128,256]{2,1,0:T(8,128)(2,1)S(1)}, bf16[2,128,256]{2,1,0:T(8,128)(2,1)S(1)}, u32[]{:S(2)}, u32[]{:S(2)}) collective-permute-start(bf16[2,128,256]{2,1,0:T(8,128)(2,1)S(1)} %get-tuple-element.108), channel_id=1, source_target_pairs={{0,8},{8,0},{1,9},{9,1},{2,10},{10,2},{3,11},{11,3},{4,12},{12,4},... | collective-permute-start | bytes 393224 | tf_op jit(solution)/shard_map/ppermute | solution.py:200
  78.1 7.2 %collective-permute-start.24 = (bf16[2,128,256]{2,1,0:T(8,128)(2,1)S(1)}, bf16[2,128,256]{2,1,0:T(8,128)(2,1)S(1)}, u32[]{:S(2)}, u32[]{:S(2)}) collective-permute-start(bf16[2,128,256]{2,1,0:T(8,128)(2,1)S(1)} %get-tuple-element.107), channel_id=1, source_target_pairs={{0,8},{8,0},{1,9},{9,1},{2,10},{10,2},{3,11},{11,3},{4,12},{12,4},... | collective-permute-start | bytes 393224 | tf_op jit(solution)/shard_map/ppermute | solution.py:200
  78.8 8.1 %collective-permute-start.21 = (bf16[128,256]{1,0:T(8,128)(2,1)S(1)}, bf16[128,256]{1,0:T(8,128)(2,1)S(1)}, u32[]{:S(2)}, u32[]{:S(2)}) collective-permute-start(bf16[128,256]{1,0:T(8,128)(2,1)S(1)} %get-tuple-element.104), channel_id=1, source_target_pairs={{0,1},{1,2},{2,3},{3,0},{4,5},{5,6},{6,7},{7,4},{8,9},{9,10},{10,1... | collective-permute-start | bytes 196616 | tf_op jit(solution)/shard_map/ppermute | solution.py:424
  80.9 8.8 %collective-permute-start.22 = (bf16[128,256]{1,0:T(8,128)(2,1)S(1)}, bf16[128,256]{1,0:T(8,128)(2,1)S(1)}, u32[]{:S(2)}, u32[]{:S(2)}) collective-permute-start(bf16[128,256]{1,0:T(8,128)(2,1)S(1)} %get-tuple-element.105), channel_id=1, source_target_pairs={{0,2},{1,3},{2,0},{3,1},{4,6},{5,7},{6,4},{7,5},{8,10},{9,11},{10,... | collective-permute-start | bytes 196616 | tf_op jit(solution)/shard_map/ppermute | solution.py:424
  82.5 7.1 %collective-permute-start.23 = (bf16[128,256]{1,0:T(8,128)(2,1)S(1)}, bf16[128,256]{1,0:T(8,128)(2,1)S(1)}, u32[]{:S(2)}, u32[]{:S(2)}) collective-permute-start(bf16[128,256]{1,0:T(8,128)(2,1)S(1)} %get-tuple-element.106), channel_id=1, source_target_pairs={{0,3},{1,0},{2,1},{3,2},{4,7},{5,4},{6,5},{7,6},{8,11},{9,8},{10,9... | collective-permute-start | bytes 196616 | tf_op jit(solution)/shard_map/ppermute | solution.py:424
  85.3 7.7 %collective-permute-start.27 = (bf16[128,256]{1,0:T(8,128)(2,1)S(1)}, bf16[128,256]{1,0:T(8,128)(2,1)S(1)}, u32[]{:S(2)}, u32[]{:S(2)}) collective-permute-start(bf16[128,256]{1,0:T(8,128)(2,1)S(1)} %get-tuple-element.109), channel_id=1, source_target_pairs={{0,2},{1,3},{2,0},{3,1},{4,6},{5,7},{6,4},{7,5},{8,10},{9,11},{10,... | collective-permute-start | bytes 196616 | tf_op jit(solution)/shard_map/ppermute | solution.py:424
  (13 other events, 84.9 us)

commit v7 on v6

--- a/solution.py
+++ b/solution.py
@@ -299,22 +299,33 @@
             out_ref[:, pl.ds(pl.multiple_of(pair * width, width), width)] = rows
 
 
-def attention_kernel(order_ref, place_ref, *refs):
+def sort_queries_kernel(order_ref, place_ref, near_ref, far_ref, *refs):
+    packed_refs, out_ref = refs[:-1], refs[-1]
+    blocks = len(packed_refs) + 1
+    token_rows = near_ref.shape[0]
+    chip, block_here = place_ref[0] // 2, place_ref[1]
+    for distance in range(blocks):
+        block = lax.rem(block_here + blocks - distance, blocks)
+        near = packed_refs[distance - 1][0] if distance else near_ref[...]
+        far = packed_refs[distance - 1][1] if distance else far_ref[0]
+        for source, pair in ((chip, near), (1 - chip, far)):
+            position = order_ref[0, 2 * block + source]
+            out_ref[position, :token_rows] = pair[:, :HD]
+            out_ref[position, token_rows:] = pair[:, HD:]
+
+
+def attention_kernel(order_ref, place_ref, query_ref, *refs):
     spans = order_ref.shape[1]
     blocks = spans // 2
     mine_refs, theirs_refs = refs[:blocks], refs[blocks : 2 * blocks]
-    near_query, far_query, *packed_queries = refs[2 * blocks : 3 * blocks + 1]
-    first_far_ref, last_far_ref, *near_refs = refs[3 * blocks + 1 : -4]
-    key_rows, value_rows, query_rows, out_rows = refs[-4:]
-    token_rows = query_rows.shape[1]
+    first_far_ref, last_far_ref, *near_refs = refs[2 * blocks : -3]
+    key_rows, value_rows, out_rows = refs[-3:]
+    token_rows = query_ref.shape[1] // 2
     span_rows = 2 * token_rows
     place, block_here = place_ref[0], place_ref[1]
     chip, core = place // 2, place % 2
     for distance in range(blocks):
         block = lax.rem(block_here + blocks - distance, blocks)
-        packed = packed_queries[distance - 1] if distance else None
-        query_rows[2 * block + chip] = packed[0] if distance else near_query[...]
-        query_rows[2 * block + 1 - chip] = packed[1] if distance else far_query[0]
         for half in range(2):
             first = order_ref[0, 2 * block + half] * span_rows
             for part in range(2):
@@ -338,10 +349,8 @@
     allowed = lax.broadcasted_iota(jnp.int32, square, 1) <= row_index
 
     def scores(position):
-        pair = query_rows[stored[position]]
-        query = jnp.concatenate([pair[:, :HD], pair[:, HD:]], axis=0)
         score = lax.dot_general(
-            query,
+            query_ref[position],
             key_rows[: (position + 1) * span_rows, :],
             (((1,), (1,)), ((), ())),
             preferred_element_type=jnp.float32,
@@ -506,17 +515,26 @@
         theirs[distance] = exchange(mine[distance], "core", 1)
     in_order = range(cycle_size)
 
+    first = far_first(cycle_size)[0]
+    mine[first], packed = lax.optimization_barrier((mine[first], packed))
+    sorted_queries = pl.pallas_call(
+        sort_queries_kernel,
+        out_shape=jax.ShapeDtypeStruct((2 * cycle_size, 2 * token_rows, HD), jnp.bfloat16),
+        in_specs=[SMEM, SMEM] + [VMEM] * (1 + cycle_size),
+        out_specs=VMEM,
+        compiler_params=pltpu.CompilerParams(vmem_limit_bytes=8 * 1024 * 1024),
+        name="sort_queries",
+    )(span_order, place, near_queries[0], far_queries, *packed)
     sequence_rows = cycle_size * block_rows
     half = jax.ShapeDtypeStruct((cycle_size // 2, *one.shape), one.dtype)
     first_far, last_far, *near = pl.pallas_call(
         attention_kernel,
         out_shape=[half, half] + [one] * cycle_size,
-        in_specs=[SMEM, SMEM] + [VMEM] * (3 * cycle_size + 1),
+        in_specs=[SMEM, SMEM] + [VMEM] * (1 + 2 * cycle_size),
         out_specs=[VMEM] * (cycle_size + 2),
         scratch_shapes=[
             pltpu.VMEM((sequence_rows, HD), jnp.bfloat16),
             pltpu.VMEM((sequence_rows, HD), jnp.bfloat16),
-            pltpu.VMEM((2 * cycle_size, token_rows, 2 * HD), jnp.bfloat16),
             pltpu.VMEM((2 * cycle_size, token_rows, 2 * HD), jnp.bfloat16),
         ],
         compiler_params=pltpu.CompilerParams(vmem_limit_bytes=24 * 1024 * 1024),
@@ -524,11 +542,9 @@
     )(
         span_order,
         place,
+        sorted_queries,
         *(mine[d] for d in in_order),
         *(theirs[d] for d in in_order),
-        near_queries[0],
-        far_queries,
-        *packed,
     )
     halves = [exchange(half, "chip", 1) for half in (first_far, last_far)]
     arrived = [near[0], *along_blocks(near)]

time: 94.7 us -> 94.7 us (level)
  transfers between devices with their start and end apart: 29 -> 29, of which waited for: 10 -> 10; matrix products, arithmetic and copies ran while one was open for 6% -> 6% of each run, Pallas kernels for 7% -> 8%
where the time goes in v7:
time: 94.7 us; the launch traced here: 94.4 us
  waiting for transfers between devices  38 us (40%)
  starting transfers between devices  33.8 us (36%)
  Pallas kernels  12.8 us (14%)
  local copies, waits for them, and re-layouts  4.96 us (5%)
  other arithmetic  4.58 us (5%)
    ppermute x15, waiting for transfers between devices, ahead(): lax.ppermute(block, 'blk', [(i, (i + distance) % cycle_size) for i in ran...  28.2 us
    ppermute x15, starting transfers between devices, ahead(): lax.ppermute(block, 'blk', [(i, (i + distance) % cycle_size) for i in ran...  22.7 us
    ppermute x10, waiting for transfers between devices, exchange(): return lax.ppermute(block, axis, [(i, i ^ distance) for i in range(size)])  7.85 us
    ppermute x10, starting transfers between devices, exchange(): return lax.ppermute(block, axis, [(i, i ^ distance) for i in range(size)])  5.59 us
    ppermute x4, starting transfers between devices, across(): lax.ppermute(block, 'dp', [(i, dp_size - 1 - i) for i in range(dp_size)])  5.55 us
    pallas_call x1, Pallas kernels, whole_cycle_shards(): pl.pallas_call(functools.partial(terms_kernel, ulysses_size, len(received...  4.46 us
    pallas_call x1, Pallas kernels, whole_cycle_shards(): pl.pallas_call(attention_kernel, out_shape=[half, half] + [one] * cycle_s...  4.08 us
    unnamed x16, local copies, waits for them, and re-layouts  3.5 us
  transfers between devices with their start and end apart: 29, of which 10 were waited for; matrix products, arithmetic and copies ran while one was open for 6% of the time, Pallas kernels for 8%

profile of v7, /device:TPU:0, one launch (start us, length us, event | category | flops | bytes accessed | tf_op | source)
XLA Modules:
  0.0 94.4 jit_solution(9656743754275889178)
XLA Ops:
  0.0 1.6 %copy-done = bf16[512,2048]{1,0:T(8,128)(2,1)S(1)} copy-done((bf16[512,2048]{1,0:T(8,128)(2,1)S(1)}, bf16[512,2048]{1,0:T(8,128)(2,1)}, u32[]{:S(2)}) %copy-start) | copy-done | bytes 2097176
  1.6 3.1 %collective-permute-start = (bf16[512,512]{1,0:T(8,128)(2,1)S(1)}, bf16[512,512]{1,0:T(8,128)(2,1)S(1)}, u32[]{:S(2)}, u32[]{:S(2)}) collective-permute-start(bf16[512,512]{1,0:T(8,128)(2,1)S(1)} %constant_dynamic-slice_fusion.refs_4_), channel_id=1, source_target_pairs={{0,1},{1,2},{2,3},{3,0},{4,5},{5,6},{6,7},{7,4},{8,9},{9,10},{10,1... | collective-permute-start | bytes 1572872 | tf_op jit(solution)/shard_map/ppermute | solution.py:433
  4.7 1.5 %collective-permute-start.2 = (bf16[512,512]{1,0:T(8,128)(2,1)S(1)}, bf16[512,512]{1,0:T(8,128)(2,1)}, u32[]{:S(2)}, u32[]{:S(2)}) collective-permute-start(bf16[512,512]{1,0:T(8,128)(2,1)S(1)} %constant_dynamic-slice_fusion.refs_4_), channel_id=1, source_target_pairs={{0,16},{16,0},{1,17},{17,1},{2,18},{18,2},{3,19},{19,3},{4,20},{20... | collective-permute-start | bytes 1572872 | tf_op jit(solution)/shard_map/ppermute | solution.py:440
  6.2 1.5 %collective-permute-start.1 = (bf16[128,4096]{1,0:T(8,128)(2,1)}, bf16[128,4096]{1,0:T(8,128)(2,1)}, u32[]{:S(2)}, u32[]{:S(2)}) collective-permute-start(bf16[128,4096]{1,0:T(8,128)(2,1)} %bitcast.28), channel_id=1, source_target_pairs={{0,8},{8,0},{1,9},{9,1},{2,10},{10,2},{3,11},{11,3},{4,12},{12,4},... | collective-permute-start | bytes 3145736 | tf_op jit(solution)/shard_map/ppermute | solution.py:200
  16.5 2.1 %collective-permute-done.refs_6_ = bf16[512,512]{1,0:T(8,128)(2,1)S(1)} collective-permute-done((bf16[512,512]{1,0:T(8,128)(2,1)S(1)}, bf16[512,512]{1,0:T(8,128)(2,1)S(1)}, u32[]{:S(2)}, u32[]{:S(2)}) %collective-permute-start) | collective-permute-done | bytes 524320 | tf_op jit(solution)/shard_map/ppermute | solution.py:433
  19.8 1.5 %collective-permute-start.4 = (bf16[512,512]{1,0:T(8,128)(2,1)S(1)}, bf16[512,512]{1,0:T(8,128)(2,1)S(1)}, u32[]{:S(2)}, u32[]{:S(2)}) collective-permute-start(bf16[512,512]{1,0:T(8,128)(2,1)S(1)} %collective-permute-done.refs_6_), channel_id=1, source_target_pairs={{0,16},{16,0},{1,17},{17,1},{2,18},{18,2},{3,19},{19,3},{4,20},{20... | collective-permute-start | bytes 1572872 | tf_op jit(solution)/shard_map/ppermute | solution.py:440
  21.3 12.3 %collective-permute-done.3.refs_8_ = bf16[512,512]{1,0:T(8,128)(2,1)S(1)} collective-permute-done((bf16[512,512]{1,0:T(8,128)(2,1)S(1)}, bf16[512,512]{1,0:T(8,128)(2,1)S(1)}, u32[]{:S(2)}, u32[]{:S(2)}) %collective-permute-start.3) | collective-permute-done | bytes 524320 | tf_op jit(solution)/shard_map/ppermute | solution.py:433
  35.1 1.5 %collective-permute-start.5 = (bf16[4,128,256]{2,1,0:T(8,128)(2,1)}, bf16[4,128,256]{2,1,0:T(8,128)(2,1)S(1)}, u32[]{:S(2)}, u32[]{:S(2)}) collective-permute-start(bf16[4,128,256]{2,1,0:T(8,128)(2,1)} %copy-done.4), channel_id=1, source_target_pairs={{0,8},{8,0},{1,9},{9,1},{2,10},{10,2},{3,11},{11,3},{4,12},{12,4},... | collective-permute-start | bytes 786440 | tf_op jit(solution)/shard_map/ppermute | solution.py:200
  36.6 7.4 %collective-permute-done.5.far_ref = bf16[4,128,256]{2,1,0:T(8,128)(2,1)S(1)} collective-permute-done((bf16[4,128,256]{2,1,0:T(8,128)(2,1)}, bf16[4,128,256]{2,1,0:T(8,128)(2,1)S(1)}, u32[]{:S(2)}, u32[]{:S(2)}) %collective-permute-start.5) | collective-permute-done | bytes 262176 | tf_op jit(solution)/shard_map/ppermute | solution.py:200
  44.0 3.5 %collective-permute-done.6.refs_10_ = bf16[512,512]{1,0:T(8,128)(2,1)S(1)} collective-permute-done((bf16[512,512]{1,0:T(8,128)(2,1)S(1)}, bf16[512,512]{1,0:T(8,128)(2,1)S(1)}, u32[]{:S(2)}, u32[]{:S(2)}) %collective-permute-start.6) | collective-permute-done | bytes 524320 | tf_op jit(solution)/shard_map/ppermute | solution.py:433
  48.6 2.3 %collective-permute-start.12 = (bf16[2,128,256]{2,1,0:T(8,128)(2,1)S(1)}, bf16[2,128,256]{2,1,0:T(8,128)(2,1)S(1)}, u32[]{:S(2)}, u32[]{:S(2)}) collective-permute-start(bf16[2,128,256]{2,1,0:T(8,128)(2,1)S(1)} %get-tuple-element.98), channel_id=1, source_target_pairs={{0,2},{1,3},{2,0},{3,1},{4,6},{5,7},{6,4},{7,5},{8,10},{9,11},{10,... | collective-permute-start | bytes 393224 | tf_op jit(solution)/shard_map/ppermute | solution.py:433
  50.9 1.5 %collective-permute-start.13 = (bf16[2,128,256]{2,1,0:T(8,128)(2,1)S(1)}, bf16[2,128,256]{2,1,0:T(8,128)(2,1)S(1)}, u32[]{:S(2)}, u32[]{:S(2)}) collective-permute-start(bf16[2,128,256]{2,1,0:T(8,128)(2,1)S(1)} %get-tuple-element.99), channel_id=1, source_target_pairs={{0,3},{1,0},{2,1},{3,2},{4,7},{5,4},{6,5},{7,6},{8,11},{9,8},{10,9... | collective-permute-start | bytes 393224 | tf_op jit(solution)/shard_map/ppermute | solution.py:433
  52.4 4.5 %terms.1 = (f32[512,512]{1,0:T(8,128)S(1)}, bf16[512,512]{1,0:T(8,128)(2,1)S(1)}) custom-call(s32[8]{0:T(128)S(1)} %stack.47.rows_ref, bf16[128,4096]{1,0:T(8,128)(2,1)S(1)} %bitcast.30, bf16[128,4096]{1,0:T(8,128)(2,1)S(1)} %collective-permute-done.9.refs_1_, bf16[128,4096]{1,0:T(8,128)(2,1)} %collective-permute-done.1.refs_2_, ...), custom_call_target="tpu_custom_call" | custom-call | tf_op jit(solution)/shard_map/terms/pallas_call | solution.py:484
  56.9 1.9 %collective-permute-done.8.piece_ref = bf16[512,512]{1,0:T(8,128)(2,1)S(1)} collective-permute-done((bf16[512,512]{1,0:T(8,128)(2,1)S(1)}, bf16[512,512]{1,0:T(8,128)(2,1)S(1)}, u32[]{:S(2)}, u32[]{:S(2)}) %collective-permute-start.8) | collective-permute-done | bytes 524320 | tf_op jit(solution)/shard_map/ppermute | solution.py:440
  60.9 2.5 %collective-permute-start.14 = (bf16[512,128]{1,0:T(8,128)(2,1)S(1)}, bf16[512,128]{1,0:T(8,128)(2,1)S(1)}, u32[]{:S(2)}, u32[]{:S(2)}) collective-permute-start(bf16[512,128]{1,0:T(8,128)(2,1)S(1)} %get-tuple-element.100), channel_id=1, source_target_pairs={{0,2},{1,3},{2,0},{3,1},{4,6},{5,7},{6,4},{7,5},{8,10},{9,11},{10,... | collective-permute-start | bytes 393224 | tf_op jit(solution)/shard_map/ppermute | solution.py:433
  64.2 3.1 %collective-permute-done.15.refs_1_ = bf16[512,128]{1,0:T(8,128)(2,1)S(1)} collective-permute-done((bf16[512,128]{1,0:T(8,128)(2,1)S(1)}, bf16[512,128]{1,0:T(8,128)(2,1)S(1)}, u32[]{:S(2)}, u32[]{:S(2)}) %collective-permute-start.15) | collective-permute-done | bytes 131104 | tf_op jit(solution)/shard_map/ppermute | solution.py:433
  67.3 3.8 %collective-permute-done.14.refs_2_ = bf16[512,128]{1,0:T(8,128)(2,1)S(1)} collective-permute-done((bf16[512,128]{1,0:T(8,128)(2,1)S(1)}, bf16[512,128]{1,0:T(8,128)(2,1)S(1)}, u32[]{:S(2)}, u32[]{:S(2)}) %collective-permute-start.14) | collective-permute-done | bytes 131104 | tf_op jit(solution)/shard_map/ppermute | solution.py:433
  72.6 4.1 %attention.1 = (bf16[2,128,256]{2,1,0:T(8,128)(2,1)S(1)}, bf16[2,128,256]{2,1,0:T(8,128)(2,1)S(1)}, bf16[128,256]{1,0:T(8,128)(2,1)S(1)}, bf16[128,256]{1,0:T(8,...) custom-call(s32[1,8]{1,0:T(1,128)S(1)} %copy-done.3, s32[2]{0:T(128)S(1)} %pad_add_fusion.place_ref, ...), custom_call_target="tpu_custom_call" | custom-call | tf_op jit(solution)/shard_map/attention/pallas_call | solution.py:530
  78.8 2.1 %collective-permute-start.21 = (bf16[128,256]{1,0:T(8,128)(2,1)S(1)}, bf16[128,256]{1,0:T(8,128)(2,1)S(1)}, u32[]{:S(2)}, u32[]{:S(2)}) collective-permute-start(bf16[128,256]{1,0:T(8,128)(2,1)S(1)} %get-tuple-element.112), channel_id=1, source_target_pairs={{0,1},{1,2},{2,3},{3,0},{4,5},{5,6},{6,7},{7,4},{8,9},{9,10},{10,1... | collective-permute-start | bytes 196616 | tf_op jit(solution)/shard_map/ppermute | solution.py:433
  80.9 1.6 %collective-permute-start.22 = (bf16[128,256]{1,0:T(8,128)(2,1)S(1)}, bf16[128,256]{1,0:T(8,128)(2,1)S(1)}, u32[]{:S(2)}, u32[]{:S(2)}) collective-permute-start(bf16[128,256]{1,0:T(8,128)(2,1)S(1)} %get-tuple-element.113), channel_id=1, source_target_pairs={{0,2},{1,3},{2,0},{3,1},{4,6},{5,7},{6,4},{7,5},{8,10},{9,11},{10,... | collective-permute-start | bytes 196616 | tf_op jit(solution)/shard_map/ppermute | solution.py:433
  83.2 2.0 %collective-permute-start.26 = (bf16[128,256]{1,0:T(8,128)(2,1)S(1)}, bf16[128,256]{1,0:T(8,128)(2,1)S(1)}, u32[]{:S(2)}, u32[]{:S(2)}) collective-permute-start(bf16[128,256]{1,0:T(8,128)(2,1)S(1)} %get-tuple-element.118), channel_id=1, source_target_pairs={{0,1},{1,2},{2,3},{3,0},{4,5},{5,6},{6,7},{7,4},{8,9},{9,10},{10,1... | collective-permute-start | bytes 196616 | tf_op jit(solution)/shard_map/ppermute | solution.py:433
  85.3 1.6 %collective-permute-start.27 = (bf16[128,256]{1,0:T(8,128)(2,1)S(1)}, bf16[128,256]{1,0:T(8,128)(2,1)S(1)}, u32[]{:S(2)}, u32[]{:S(2)}) collective-permute-start(bf16[128,256]{1,0:T(8,128)(2,1)S(1)} %get-tuple-element.117), channel_id=1, source_target_pairs={{0,2},{1,3},{2,0},{3,1},{4,6},{5,7},{6,4},{7,5},{8,10},{9,11},{10,... | collective-permute-start | bytes 196616 | tf_op jit(solution)/shard_map/ppermute | solution.py:433
  86.9 2.8 %collective-permute-start.28 = (bf16[128,256]{1,0:T(8,128)(2,1)S(1)}, bf16[128,256]{1,0:T(8,128)(2,1)S(1)}, u32[]{:S(2)}, u32[]{:S(2)}) collective-permute-start(bf16[128,256]{1,0:T(8,128)(2,1)S(1)} %slice_bitcast_fusion), channel_id=1, source_target_pairs={{0,3},{1,0},{2,1},{3,2},{4,7},{5,4},{6,5},{7,6},{8,11},{9,8},{10,9... | collective-permute-start | bytes 196616 | tf_op jit(solution)/shard_map/ppermute | solution.py:433
  89.6 3.4 %collective-permute-done.27.refs_6_ = bf16[128,256]{1,0:T(8,128)(2,1)S(1)} collective-permute-done((bf16[128,256]{1,0:T(8,128)(2,1)S(1)}, bf16[128,256]{1,0:T(8,128)(2,1)S(1)}, u32[]{:S(2)}, u32[]{:S(2)}) %collective-permute-start.27) | collective-permute-done | bytes 65568 | tf_op jit(solution)/shard_map/ppermute | solution.py:433
  (70 shorter events, 21.1 us)
Async XLA Ops:
  1.6 17.0 %collective-permute-start = (bf16[512,512]{1,0:T(8,128)(2,1)S(1)}, bf16[512,512]{1,0:T(8,128)(2,1)S(1)}, u32[]{:S(2)}, u32[]{:S(2)}) collective-permute-start(bf16[512,512]{1,0:T(8,128)(2,1)S(1)} %constant_dynamic-slice_fusion.refs_4_), channel_id=1, source_target_pairs={{0,1},{1,2},{2,3},{3,0},{4,5},{5,6},{6,7},{7,4},{8,9},{9,10},{10,1... | collective-permute-start | bytes 1572872 | tf_op jit(solution)/shard_map/ppermute | solution.py:433
  4.7 14.0 %collective-permute-start.2 = (bf16[512,512]{1,0:T(8,128)(2,1)S(1)}, bf16[512,512]{1,0:T(8,128)(2,1)}, u32[]{:S(2)}, u32[]{:S(2)}) collective-permute-start(bf16[512,512]{1,0:T(8,128)(2,1)S(1)} %constant_dynamic-slice_fusion.refs_4_), channel_id=1, source_target_pairs={{0,16},{16,0},{1,17},{17,1},{2,18},{18,2},{3,19},{19,3},{4,20},{20... | collective-permute-start | bytes 1572872 | tf_op jit(solution)/shard_map/ppermute | solution.py:440
  6.2 27.3 %collective-permute-start.1 = (bf16[128,4096]{1,0:T(8,128)(2,1)}, bf16[128,4096]{1,0:T(8,128)(2,1)}, u32[]{:S(2)}, u32[]{:S(2)}) collective-permute-start(bf16[128,4096]{1,0:T(8,128)(2,1)} %bitcast.28), channel_id=1, source_target_pairs={{0,8},{8,0},{1,9},{9,1},{2,10},{10,2},{3,11},{11,3},{4,12},{12,4},... | collective-permute-start | bytes 3145736 | tf_op jit(solution)/shard_map/ppermute | solution.py:200
  18.7 14.9 %collective-permute-start.3 = (bf16[512,512]{1,0:T(8,128)(2,1)S(1)}, bf16[512,512]{1,0:T(8,128)(2,1)S(1)}, u32[]{:S(2)}, u32[]{:S(2)}) collective-permute-start(bf16[512,512]{1,0:T(8,128)(2,1)S(1)} %collective-permute-done.refs_6_), channel_id=1, source_target_pairs={{0,1},{1,2},{2,3},{3,0},{4,5},{5,6},{6,7},{7,4},{8,9},{9,10},{10,1... | collective-permute-start | bytes 1572872 | tf_op jit(solution)/shard_map/ppermute | solution.py:433
  19.8 13.8 %collective-permute-start.4 = (bf16[512,512]{1,0:T(8,128)(2,1)S(1)}, bf16[512,512]{1,0:T(8,128)(2,1)S(1)}, u32[]{:S(2)}, u32[]{:S(2)}) collective-permute-start(bf16[512,512]{1,0:T(8,128)(2,1)S(1)} %collective-permute-done.refs_6_), channel_id=1, source_target_pairs={{0,16},{16,0},{1,17},{17,1},{2,18},{18,2},{3,19},{19,3},{4,20},{20... | collective-permute-start | bytes 1572872 | tf_op jit(solution)/shard_map/ppermute | solution.py:440
  21.3 29.6 %collective-permute-start.9 = (bf16[128,4096]{1,0:T(8,128)(2,1)}, bf16[128,4096]{1,0:T(8,128)(2,1)S(1)}, u32[]{:S(2)}, u32[]{:S(2)}) collective-permute-start(bf16[128,4096]{1,0:T(8,128)(2,1)} %bitcast.29), channel_id=1, source_target_pairs={{0,4},{4,0},{1,5},{5,1},{2,6},{6,2},{3,7},{7,3},{8,12},{12,8},{9,1... | collective-permute-start | bytes 3145736 | tf_op jit(solution)/shard_map/ppermute | solution.py:200
  33.6 14.0 %collective-permute-start.6 = (bf16[512,512]{1,0:T(8,128)(2,1)S(1)}, bf16[512,512]{1,0:T(8,128)(2,1)S(1)}, u32[]{:S(2)}, u32[]{:S(2)}) collective-permute-start(bf16[512,512]{1,0:T(8,128)(2,1)S(1)} %collective-permute-done.3.refs_8_), channel_id=1, source_target_pairs={{0,1},{1,2},{2,3},{3,0},{4,5},{5,6},{6,7},{7,4},{8,9},{9,10},{10,1... | collective-permute-start | bytes 1572872 | tf_op jit(solution)/shard_map/ppermute | solution.py:433
  33.6 14.0 %collective-permute-start.7 = (bf16[512,512]{1,0:T(8,128)(2,1)S(1)}, bf16[512,512]{1,0:T(8,128)(2,1)S(1)}, u32[]{:S(2)}, u32[]{:S(2)}) collective-permute-start(bf16[512,512]{1,0:T(8,128)(2,1)S(1)} %collective-permute-done.3.refs_8_), channel_id=1, source_target_pairs={{0,16},{16,0},{1,17},{17,1},{2,18},{18,2},{3,19},{19,3},{4,20},{20... | collective-permute-start | bytes 1572872 | tf_op jit(solution)/shard_map/ppermute | solution.py:440
  35.1 17.4 %collective-permute-start.10 = (bf16[128,4096]{1,0:T(8,128)(2,1)}, bf16[128,4096]{1,0:T(8,128)(2,1)S(1)}, u32[]{:S(2)}, u32[]{:S(2)}) collective-permute-start(bf16[128,4096]{1,0:T(8,128)(2,1)} %collective-permute-done.1.refs_2_), channel_id=1, source_target_pairs={{0,4},{4,0},{1,5},{5,1},{2,6},{6,2},{3,7},{7,3},{8,12},{12,8},{9,1... | collective-permute-start | bytes 3145736 | tf_op jit(solution)/shard_map/ppermute | solution.py:200
  35.1 8.9 %collective-permute-start.5 = (bf16[4,128,256]{2,1,0:T(8,128)(2,1)}, bf16[4,128,256]{2,1,0:T(8,128)(2,1)S(1)}, u32[]{:S(2)}, u32[]{:S(2)}) collective-permute-start(bf16[4,128,256]{2,1,0:T(8,128)(2,1)} %copy-done.4), channel_id=1, source_target_pairs={{0,8},{8,0},{1,9},{9,1},{2,10},{10,2},{3,11},{11,3},{4,12},{12,4},... | collective-permute-start | bytes 786440 | tf_op jit(solution)/shard_map/ppermute | solution.py:200
  47.6 11.3 %collective-permute-start.8 = (bf16[512,512]{1,0:T(8,128)(2,1)S(1)}, bf16[512,512]{1,0:T(8,128)(2,1)S(1)}, u32[]{:S(2)}, u32[]{:S(2)}) collective-permute-start(bf16[512,512]{1,0:T(8,128)(2,1)S(1)} %collective-permute-done.6.refs_10_), channel_id=1, source_target_pairs={{0,16},{16,0},{1,17},{17,1},{2,18},{18,2},{3,19},{19,3},{4,20},{20... | collective-permute-start | bytes 1572872 | tf_op jit(solution)/shard_map/ppermute | solution.py:440
  48.6 11.6 %collective-permute-start.11 = (bf16[2,128,256]{2,1,0:T(8,128)(2,1)S(1)}, bf16[2,128,256]{2,1,0:T(8,128)(2,1)S(1)}, u32[]{:S(2)}, u32[]{:S(2)}) collective-permute-start(bf16[2,128,256]{2,1,0:T(8,128)(2,1)S(1)} %get-tuple-element.97), channel_id=1, source_target_pairs={{0,1},{1,2},{2,3},{3,0},{4,5},{5,6},{6,7},{7,4},{8,9},{9,10},{10,1... | collective-permute-start | bytes 393224 | tf_op jit(solution)/shard_map/ppermute | solution.py:433
  48.6 11.7 %collective-permute-start.12 = (bf16[2,128,256]{2,1,0:T(8,128)(2,1)S(1)}, bf16[2,128,256]{2,1,0:T(8,128)(2,1)S(1)}, u32[]{:S(2)}, u32[]{:S(2)}) collective-permute-start(bf16[2,128,256]{2,1,0:T(8,128)(2,1)S(1)} %get-tuple-element.98), channel_id=1, source_target_pairs={{0,2},{1,3},{2,0},{3,1},{4,6},{5,7},{6,4},{7,5},{8,10},{9,11},{10,... | collective-permute-start | bytes 393224 | tf_op jit(solution)/shard_map/ppermute | solution.py:433
  50.9 9.4 %collective-permute-start.13 = (bf16[2,128,256]{2,1,0:T(8,128)(2,1)S(1)}, bf16[2,128,256]{2,1,0:T(8,128)(2,1)S(1)}, u32[]{:S(2)}, u32[]{:S(2)}) collective-permute-start(bf16[2,128,256]{2,1,0:T(8,128)(2,1)S(1)} %get-tuple-element.99), channel_id=1, source_target_pairs={{0,3},{1,0},{2,1},{3,2},{4,7},{5,4},{6,5},{7,6},{8,11},{9,8},{10,9... | collective-permute-start | bytes 393224 | tf_op jit(solution)/shard_map/ppermute | solution.py:433
  60.3 7.0 %collective-permute-start.15 = (bf16[512,128]{1,0:T(8,128)(2,1)S(1)}, bf16[512,128]{1,0:T(8,128)(2,1)S(1)}, u32[]{:S(2)}, u32[]{:S(2)}) collective-permute-start(bf16[512,128]{1,0:T(8,128)(2,1)S(1)} %get-tuple-element.108), channel_id=1, source_target_pairs={{0,1},{1,2},{2,3},{3,0},{4,5},{5,6},{6,7},{7,4},{8,9},{9,10},{10,1... | collective-permute-start | bytes 393224 | tf_op jit(solution)/shard_map/ppermute | solution.py:433
  60.9 10.2 %collective-permute-start.14 = (bf16[512,128]{1,0:T(8,128)(2,1)S(1)}, bf16[512,128]{1,0:T(8,128)(2,1)S(1)}, u32[]{:S(2)}, u32[]{:S(2)}) collective-permute-start(bf16[512,128]{1,0:T(8,128)(2,1)S(1)} %get-tuple-element.100), channel_id=1, source_target_pairs={{0,2},{1,3},{2,0},{3,1},{4,6},{5,7},{6,4},{7,5},{8,10},{9,11},{10,... | collective-permute-start | bytes 393224 | tf_op jit(solution)/shard_map/ppermute | solution.py:433
  63.3 7.7 %collective-permute-start.16 = (bf16[512,128]{1,0:T(8,128)(2,1)S(1)}, bf16[512,128]{1,0:T(8,128)(2,1)S(1)}, u32[]{:S(2)}, u32[]{:S(2)}) collective-permute-start(bf16[512,128]{1,0:T(8,128)(2,1)S(1)} %get-tuple-element.110), channel_id=1, source_target_pairs={{0,3},{1,0},{2,1},{3,2},{4,7},{5,4},{6,5},{7,6},{8,11},{9,8},{10,9... | collective-permute-start | bytes 393224 | tf_op jit(solution)/shard_map/ppermute | solution.py:433
  64.2 8.0 %collective-permute-start.17 = (bf16[512,128]{1,0:T(8,128)(2,1)S(1)}, bf16[512,128]{1,0:T(8,128)(2,1)S(1)}, u32[]{:S(2)}, u32[]{:S(2)}) collective-permute-start(bf16[512,128]{1,0:T(8,128)(2,1)S(1)} %get-tuple-element.107.refs_0_), channel_id=1, source_target_pairs={{0,4},{4,0},{1,5},{5,1},{2,6},{6,2},{3,7},{7,3},{8,12},{12,8},{9,1... | collective-permute-start | bytes 393224 | tf_op jit(solution)/shard_map/ppermute | solution.py:200
  76.7 6.5 %collective-permute-start.25 = (bf16[2,128,256]{2,1,0:T(8,128)(2,1)S(1)}, bf16[2,128,256]{2,1,0:T(8,128)(2,1)S(1)}, u32[]{:S(2)}, u32[]{:S(2)}) collective-permute-start(bf16[2,128,256]{2,1,0:T(8,128)(2,1)S(1)} %get-tuple-element.116), channel_id=1, source_target_pairs={{0,8},{8,0},{1,9},{9,1},{2,10},{10,2},{3,11},{11,3},{4,12},{12,4},... | collective-permute-start | bytes 393224 | tf_op jit(solution)/shard_map/ppermute | solution.py:200
  78.0 7.2 %collective-permute-start.24 = (bf16[2,128,256]{2,1,0:T(8,128)(2,1)S(1)}, bf16[2,128,256]{2,1,0:T(8,128)(2,1)S(1)}, u32[]{:S(2)}, u32[]{:S(2)}) collective-permute-start(bf16[2,128,256]{2,1,0:T(8,128)(2,1)S(1)} %get-tuple-element.115), channel_id=1, source_target_pairs={{0,8},{8,0},{1,9},{9,1},{2,10},{10,2},{3,11},{11,3},{4,12},{12,4},... | collective-permute-start | bytes 393224 | tf_op jit(solution)/shard_map/ppermute | solution.py:200
  78.8 8.1 %collective-permute-start.21 = (bf16[128,256]{1,0:T(8,128)(2,1)S(1)}, bf16[128,256]{1,0:T(8,128)(2,1)S(1)}, u32[]{:S(2)}, u32[]{:S(2)}) collective-permute-start(bf16[128,256]{1,0:T(8,128)(2,1)S(1)} %get-tuple-element.112), channel_id=1, source_target_pairs={{0,1},{1,2},{2,3},{3,0},{4,5},{5,6},{6,7},{7,4},{8,9},{9,10},{10,1... | collective-permute-start | bytes 196616 | tf_op jit(solution)/shard_map/ppermute | solution.py:433
  80.9 8.8 %collective-permute-start.22 = (bf16[128,256]{1,0:T(8,128)(2,1)S(1)}, bf16[128,256]{1,0:T(8,128)(2,1)S(1)}, u32[]{:S(2)}, u32[]{:S(2)}) collective-permute-start(bf16[128,256]{1,0:T(8,128)(2,1)S(1)} %get-tuple-element.113), channel_id=1, source_target_pairs={{0,2},{1,3},{2,0},{3,1},{4,6},{5,7},{6,4},{7,5},{8,10},{9,11},{10,... | collective-permute-start | bytes 196616 | tf_op jit(solution)/shard_map/ppermute | solution.py:433
  82.5 7.1 %collective-permute-start.23 = (bf16[128,256]{1,0:T(8,128)(2,1)S(1)}, bf16[128,256]{1,0:T(8,128)(2,1)S(1)}, u32[]{:S(2)}, u32[]{:S(2)}) collective-permute-start(bf16[128,256]{1,0:T(8,128)(2,1)S(1)} %get-tuple-element.114), channel_id=1, source_target_pairs={{0,3},{1,0},{2,1},{3,2},{4,7},{5,4},{6,5},{7,6},{8,11},{9,8},{10,9... | collective-permute-start | bytes 196616 | tf_op jit(solution)/shard_map/ppermute | solution.py:433
  85.3 7.7 %collective-permute-start.27 = (bf16[128,256]{1,0:T(8,128)(2,1)S(1)}, bf16[128,256]{1,0:T(8,128)(2,1)S(1)}, u32[]{:S(2)}, u32[]{:S(2)}) collective-permute-start(bf16[128,256]{1,0:T(8,128)(2,1)S(1)} %get-tuple-element.117), channel_id=1, source_target_pairs={{0,2},{1,3},{2,0},{3,1},{4,6},{5,7},{6,4},{7,5},{8,10},{9,11},{10,... | collective-permute-start | bytes 196616 | tf_op jit(solution)/shard_map/ppermute | solution.py:433
  (13 other events, 84.6 us)

commit v8 on v6

--- a/solution.py
+++ b/solution.py
@@ -286,17 +286,20 @@
         out_ref[...] = rope_head(rows, cosine, sine).astype(jnp.bfloat16)
 
 
-def order_heads_kernel(place_ref, *refs):
-    out_ref = refs[-1]
-    blocks = (len(refs) - 1) // 2
-    chip, block_here = place_ref[0] // 2, place_ref[1]
-    width = refs[0].shape[1]
-    for distance in range(blocks):
+def place_heads_kernel(crossed, distances, place_ref, *refs):
+    out_ref, sems = refs[-2:]
+    blocks, chip, block_here = out_ref.shape[1] // (4 * HD), place_ref[0] // 2, place_ref[1]
+    width = 2 * HD
+    copies = []
+    for index, (distance, rows) in enumerate(zip(distances, refs)):
         block = lax.rem(block_here + blocks - distance, blocks)
-        near, far = refs[distance], refs[blocks + distance]
-        for source, rows in ((chip, near[...]), (1 - chip, far[...] if distance else far[far.shape[0] - 1])):
-            pair = source * blocks + block
-            out_ref[:, pl.ds(pl.multiple_of(pair * width, width), width)] = rows
+        source = 1 - chip if crossed[index] else chip
+        columns = pl.ds(pl.multiple_of((source * blocks + block) * width, width), width)
+        rows = rows.at[rows.shape[0] - 1] if len(rows.shape) == 3 else rows
+        copies.append(pltpu.make_async_copy(rows, out_ref.at[:, columns], sems.at[index]))
+        copies[-1].start()
+    for copy in copies:
+        copy.wait()
 
 
 def attention_kernel(order_ref, place_ref, *refs):
@@ -536,14 +539,25 @@
     for index, distance in enumerate(far_first(cycle_size)):
         part, place_in_half = divmod(index, cycle_size // 2)
         crossed[distance] = ahead(halves[part][place_in_half], distance)
-    heads = pl.pallas_call(
-        order_heads_kernel,
-        out_shape=jax.ShapeDtypeStruct((token_rows, QH * HD), jnp.bfloat16),
-        in_specs=[SMEM] + [VMEM] * (2 * cycle_size),
-        out_specs=VMEM,
-        compiler_params=pltpu.CompilerParams(vmem_limit_bytes=8 * 1024 * 1024),
-        name="order_heads",
-    )(place, *arrived, *(crossed[distance] for distance in in_order))
+    def place_heads(crossed, distances, parts, before):
+        extra = [] if before is None else [before]
+        return pl.pallas_call(
+            functools.partial(place_heads_kernel, crossed, distances),
+            out_shape=jax.ShapeDtypeStruct((token_rows, QH * HD), jnp.bfloat16),
+            in_specs=[SMEM] + [VMEM] * len(parts) + [ANY] * len(extra),
+            out_specs=ANY,
+            scratch_shapes=[pltpu.SemaphoreType.DMA((len(parts),))],
+            input_output_aliases={1 + len(parts): 0} if extra else {},
+            compiler_params=pltpu.CompilerParams(vmem_limit_bytes=8 * 1024 * 1024),
+            name="place_heads",
+        )(place, *parts, *extra)
+
+    early = [*in_order, 0]
+    heads = place_heads(
+        [False] * cycle_size + [True], early, [*(arrived[d] for d in in_order), crossed[0]], None
+    )
+    late = list(in_order)[1:]
+    heads = place_heads([True] * len(late), late, [crossed[d] for d in late], heads)
     return heads[None]
 
 

time: 94.7 us -> 94.6 us (level)
  waiting for transfers between devices: 38.6 us -> 37.3 us
  Pallas kernels: 12.2 us -> 13.4 us
    ppermute x15, waiting for transfers between devices: 28.2 us -> 26.9 us  [ahead(): lax.ppermute(block, 'blk', [(i, (i + distance) % cycle_size) for i in ran...]
    pallas_call x1 -> x2, Pallas kernels: 1.41 us -> 2.56 us  [place_heads(): pl.pallas_call(functools.partial(place_heads_kernel, crossed, distances),...]
  transfers between devices with their start and end apart: 29 -> 29, of which waited for: 10 -> 10; matrix products, arithmetic and copies ran while one was open for 6% -> 6% of each run, Pallas kernels for 7% -> 9%
where the time goes in v8:
time: 94.6 us; the launch traced here: 94.3 us
  waiting for transfers between devices  37.3 us (39%)
  starting transfers between devices  33.9 us (36%)
  Pallas kernels  13.4 us (14%)
  local copies, waits for them, and re-layouts  4.96 us (5%)
  other arithmetic  4.58 us (5%)
    ppermute x15, waiting for transfers between devices, ahead(): lax.ppermute(block, 'blk', [(i, (i + distance) % cycle_size) for i in ran...  26.9 us
    ppermute x15, starting transfers between devices, ahead(): lax.ppermute(block, 'blk', [(i, (i + distance) % cycle_size) for i in ran...  22.7 us
    ppermute x10, waiting for transfers between devices, exchange(): return lax.ppermute(block, axis, [(i, i ^ distance) for i in range(size)])  8.5 us
    ppermute x10, starting transfers between devices, exchange(): return lax.ppermute(block, axis, [(i, i ^ distance) for i in range(size)])  5.59 us
    ppermute x4, starting transfers between devices, across(): lax.ppermute(block, 'dp', [(i, dp_size - 1 - i) for i in range(dp_size)])  5.55 us
    pallas_call x1, Pallas kernels, whole_cycle_shards(): pl.pallas_call(functools.partial(terms_kernel, ulysses_size, len(received...  4.46 us
    pallas_call x1, Pallas kernels, whole_cycle_shards(): pl.pallas_call(attention_kernel, out_shape=[half, half] + [one] * cycle_s...  4.1 us
    unnamed x16, local copies, waits for them, and re-layouts  3.5 us
  transfers between devices with their start and end apart: 29, of which 10 were waited for; matrix products, arithmetic and copies ran while one was open for 6% of the time, Pallas kernels for 9%

profile of v8, /device:TPU:0, one launch (start us, length us, event | category | flops | bytes accessed | tf_op | source)
XLA Modules:
  0.0 94.3 jit_solution(1055789297174024615)
XLA Ops:
  0.0 1.6 %copy-done = bf16[512,2048]{1,0:T(8,128)(2,1)S(1)} copy-done((bf16[512,2048]{1,0:T(8,128)(2,1)S(1)}, bf16[512,2048]{1,0:T(8,128)(2,1)}, u32[]{:S(2)}) %copy-start) | copy-done | bytes 2097176
  1.6 3.1 %collective-permute-start = (bf16[512,512]{1,0:T(8,128)(2,1)S(1)}, bf16[512,512]{1,0:T(8,128)(2,1)S(1)}, u32[]{:S(2)}, u32[]{:S(2)}) collective-permute-start(bf16[512,512]{1,0:T(8,128)(2,1)S(1)} %constant_dynamic-slice_fusion.refs_4_), channel_id=1, source_target_pairs={{0,1},{1,2},{2,3},{3,0},{4,5},{5,6},{6,7},{7,4},{8,9},{9,10},{10,1... | collective-permute-start | bytes 1572872 | tf_op jit(solution)/shard_map/ppermute | solution.py:427
  4.7 1.5 %collective-permute-start.2 = (bf16[512,512]{1,0:T(8,128)(2,1)S(1)}, bf16[512,512]{1,0:T(8,128)(2,1)}, u32[]{:S(2)}, u32[]{:S(2)}) collective-permute-start(bf16[512,512]{1,0:T(8,128)(2,1)S(1)} %constant_dynamic-slice_fusion.refs_4_), channel_id=1, source_target_pairs={{0,16},{16,0},{1,17},{17,1},{2,18},{18,2},{3,19},{19,3},{4,20},{20... | collective-permute-start | bytes 1572872 | tf_op jit(solution)/shard_map/ppermute | solution.py:434
  6.2 1.5 %collective-permute-start.1 = (bf16[128,4096]{1,0:T(8,128)(2,1)}, bf16[128,4096]{1,0:T(8,128)(2,1)}, u32[]{:S(2)}, u32[]{:S(2)}) collective-permute-start(bf16[128,4096]{1,0:T(8,128)(2,1)} %bitcast.28), channel_id=1, source_target_pairs={{0,8},{8,0},{1,9},{9,1},{2,10},{10,2},{3,11},{11,3},{4,12},{12,4},... | collective-permute-start | bytes 3145736 | tf_op jit(solution)/shard_map/ppermute | solution.py:200
  16.5 2.1 %collective-permute-done.refs_6_ = bf16[512,512]{1,0:T(8,128)(2,1)S(1)} collective-permute-done((bf16[512,512]{1,0:T(8,128)(2,1)S(1)}, bf16[512,512]{1,0:T(8,128)(2,1)S(1)}, u32[]{:S(2)}, u32[]{:S(2)}) %collective-permute-start) | collective-permute-done | bytes 524320 | tf_op jit(solution)/shard_map/ppermute | solution.py:427
  19.8 1.5 %collective-permute-start.4 = (bf16[512,512]{1,0:T(8,128)(2,1)S(1)}, bf16[512,512]{1,0:T(8,128)(2,1)S(1)}, u32[]{:S(2)}, u32[]{:S(2)}) collective-permute-start(bf16[512,512]{1,0:T(8,128)(2,1)S(1)} %collective-permute-done.refs_6_), channel_id=1, source_target_pairs={{0,16},{16,0},{1,17},{17,1},{2,18},{18,2},{3,19},{19,3},{4,20},{20... | collective-permute-start | bytes 1572872 | tf_op jit(solution)/shard_map/ppermute | solution.py:434
  21.3 12.3 %collective-permute-done.3.refs_8_ = bf16[512,512]{1,0:T(8,128)(2,1)S(1)} collective-permute-done((bf16[512,512]{1,0:T(8,128)(2,1)S(1)}, bf16[512,512]{1,0:T(8,128)(2,1)S(1)}, u32[]{:S(2)}, u32[]{:S(2)}) %collective-permute-start.3) | collective-permute-done | bytes 524320 | tf_op jit(solution)/shard_map/ppermute | solution.py:427
  35.1 1.5 %collective-permute-start.7 = (bf16[4,128,256]{2,1,0:T(8,128)(2,1)}, bf16[4,128,256]{2,1,0:T(8,128)(2,1)S(1)}, u32[]{:S(2)}, u32[]{:S(2)}) collective-permute-start(bf16[4,128,256]{2,1,0:T(8,128)(2,1)} %copy-done.4), channel_id=1, source_target_pairs={{0,8},{8,0},{1,9},{9,1},{2,10},{10,2},{3,11},{11,3},{4,12},{12,4},... | collective-permute-start | bytes 786440 | tf_op jit(solution)/shard_map/ppermute | solution.py:200
  36.6 7.4 %collective-permute-done.7.far_ref.refs_9_ = bf16[4,128,256]{2,1,0:T(8,128)(2,1)S(1)} collective-permute-done((bf16[4,128,256]{2,1,0:T(8,128)(2,1)}, bf16[4,128,256]{2,1,0:T(8,128)(2,1)S(1)}, u32[]{:S(2)}, u32[]{:S(2)}) %collective-permute-start.7) | collective-permute-done | bytes 262176 | tf_op jit(solution)/shard_map/ppermute | solution.py:200
  44.0 3.5 %collective-permute-done.5.refs_10_ = bf16[512,512]{1,0:T(8,128)(2,1)S(1)} collective-permute-done((bf16[512,512]{1,0:T(8,128)(2,1)S(1)}, bf16[512,512]{1,0:T(8,128)(2,1)S(1)}, u32[]{:S(2)}, u32[]{:S(2)}) %collective-permute-start.5) | collective-permute-done | bytes 524320 | tf_op jit(solution)/shard_map/ppermute | solution.py:427
  48.6 2.3 %collective-permute-start.12 = (bf16[2,128,256]{2,1,0:T(8,128)(2,1)S(1)}, bf16[2,128,256]{2,1,0:T(8,128)(2,1)S(1)}, u32[]{:S(2)}, u32[]{:S(2)}) collective-permute-start(bf16[2,128,256]{2,1,0:T(8,128)(2,1)S(1)} %get-tuple-element.93), channel_id=1, source_target_pairs={{0,2},{1,3},{2,0},{3,1},{4,6},{5,7},{6,4},{7,5},{8,10},{9,11},{10,... | collective-permute-start | bytes 393224 | tf_op jit(solution)/shard_map/ppermute | solution.py:427
  50.9 1.5 %collective-permute-start.13 = (bf16[2,128,256]{2,1,0:T(8,128)(2,1)S(1)}, bf16[2,128,256]{2,1,0:T(8,128)(2,1)S(1)}, u32[]{:S(2)}, u32[]{:S(2)}) collective-permute-start(bf16[2,128,256]{2,1,0:T(8,128)(2,1)S(1)} %get-tuple-element.94), channel_id=1, source_target_pairs={{0,3},{1,0},{2,1},{3,2},{4,7},{5,4},{6,5},{7,6},{8,11},{9,8},{10,9... | collective-permute-start | bytes 393224 | tf_op jit(solution)/shard_map/ppermute | solution.py:427
  52.4 4.5 %terms.1 = (f32[512,512]{1,0:T(8,128)S(1)}, bf16[512,512]{1,0:T(8,128)(2,1)S(1)}) custom-call(s32[8]{0:T(128)S(1)} %stack.47.rows_ref, bf16[128,4096]{1,0:T(8,128)(2,1)S(1)} %bitcast.30, bf16[128,4096]{1,0:T(8,128)(2,1)S(1)} %collective-permute-done.9.refs_1_, bf16[128,4096]{1,0:T(8,128)(2,1)} %collective-permute-done.1.refs_2_, ...), custom_call_target="tpu_custom_call" | custom-call | tf_op jit(solution)/shard_map/terms/pallas_call | solution.py:478
  56.9 1.9 %collective-permute-done.8.piece_ref = bf16[512,512]{1,0:T(8,128)(2,1)S(1)} collective-permute-done((bf16[512,512]{1,0:T(8,128)(2,1)S(1)}, bf16[512,512]{1,0:T(8,128)(2,1)S(1)}, u32[]{:S(2)}, u32[]{:S(2)}) %collective-permute-start.8) | collective-permute-done | bytes 524320 | tf_op jit(solution)/shard_map/ppermute | solution.py:434
  60.9 2.5 %collective-permute-start.15 = (bf16[512,128]{1,0:T(8,128)(2,1)S(1)}, bf16[512,128]{1,0:T(8,128)(2,1)S(1)}, u32[]{:S(2)}, u32[]{:S(2)}) collective-permute-start(bf16[512,128]{1,0:T(8,128)(2,1)S(1)} %get-tuple-element.97), channel_id=1, source_target_pairs={{0,2},{1,3},{2,0},{3,1},{4,6},{5,7},{6,4},{7,5},{8,10},{9,11},{10,... | collective-permute-start | bytes 393224 | tf_op jit(solution)/shard_map/ppermute | solution.py:427
  64.2 3.1 %collective-permute-done.14.refs_1_ = bf16[512,128]{1,0:T(8,128)(2,1)S(1)} collective-permute-done((bf16[512,128]{1,0:T(8,128)(2,1)S(1)}, bf16[512,128]{1,0:T(8,128)(2,1)S(1)}, u32[]{:S(2)}, u32[]{:S(2)}) %collective-permute-start.14) | collective-permute-done | bytes 131104 | tf_op jit(solution)/shard_map/ppermute | solution.py:427
  67.3 3.8 %collective-permute-done.15.refs_2_ = bf16[512,128]{1,0:T(8,128)(2,1)S(1)} collective-permute-done((bf16[512,128]{1,0:T(8,128)(2,1)S(1)}, bf16[512,128]{1,0:T(8,128)(2,1)S(1)}, u32[]{:S(2)}, u32[]{:S(2)}) %collective-permute-start.15) | collective-permute-done | bytes 131104 | tf_op jit(solution)/shard_map/ppermute | solution.py:427
  72.6 4.1 %attention.1 = (bf16[2,128,256]{2,1,0:T(8,128)(2,1)S(1)}, bf16[2,128,256]{2,1,0:T(8,128)(2,1)S(1)}, bf16[128,256]{1,0:T(8,128)(2,1)S(1)}, bf16[128,256]{1,0:T(8,...) custom-call(s32[1,8]{1,0:T(1,128)S(1)} %copy-done.3, s32[2]{0:T(128)S(1)} %pad_add_fusion.place_ref, ...), custom_call_target="tpu_custom_call" | custom-call | tf_op jit(solution)/shard_map/attention/pallas_call | solution.py:514
  78.8 2.1 %collective-permute-start.26 = (bf16[128,256]{1,0:T(8,128)(2,1)S(1)}, bf16[128,256]{1,0:T(8,128)(2,1)S(1)}, u32[]{:S(2)}, u32[]{:S(2)}) collective-permute-start(bf16[128,256]{1,0:T(8,128)(2,1)S(1)} %get-tuple-element.106), channel_id=1, source_target_pairs={{0,1},{1,2},{2,3},{3,0},{4,5},{5,6},{6,7},{7,4},{8,9},{9,10},{10,1... | collective-permute-start | bytes 196616 | tf_op jit(solution)/shard_map/ppermute | solution.py:427
  80.9 1.6 %collective-permute-start.27 = (bf16[128,256]{1,0:T(8,128)(2,1)S(1)}, bf16[128,256]{1,0:T(8,128)(2,1)S(1)}, u32[]{:S(2)}, u32[]{:S(2)}) collective-permute-start(bf16[128,256]{1,0:T(8,128)(2,1)S(1)} %get-tuple-element.107), channel_id=1, source_target_pairs={{0,2},{1,3},{2,0},{3,1},{4,6},{5,7},{6,4},{7,5},{8,10},{9,11},{10,... | collective-permute-start | bytes 196616 | tf_op jit(solution)/shard_map/ppermute | solution.py:427
  83.3 2.0 %collective-permute-start.22 = (bf16[128,256]{1,0:T(8,128)(2,1)S(1)}, bf16[128,256]{1,0:T(8,128)(2,1)S(1)}, u32[]{:S(2)}, u32[]{:S(2)}) collective-permute-start(bf16[128,256]{1,0:T(8,128)(2,1)S(1)} %get-tuple-element.110), channel_id=1, source_target_pairs={{0,1},{1,2},{2,3},{3,0},{4,5},{5,6},{6,7},{7,4},{8,9},{9,10},{10,1... | collective-permute-start | bytes 196616 | tf_op jit(solution)/shard_map/ppermute | solution.py:427
  85.3 1.6 %collective-permute-start.23 = (bf16[128,256]{1,0:T(8,128)(2,1)S(1)}, bf16[128,256]{1,0:T(8,128)(2,1)S(1)}, u32[]{:S(2)}, u32[]{:S(2)}) collective-permute-start(bf16[128,256]{1,0:T(8,128)(2,1)S(1)} %get-tuple-element.109), channel_id=1, source_target_pairs={{0,2},{1,3},{2,0},{3,1},{4,6},{5,7},{6,4},{7,5},{8,10},{9,11},{10,... | collective-permute-start | bytes 196616 | tf_op jit(solution)/shard_map/ppermute | solution.py:427
  86.9 2.8 %collective-permute-start.25 = (bf16[128,256]{1,0:T(8,128)(2,1)S(1)}, bf16[128,256]{1,0:T(8,128)(2,1)S(1)}, u32[]{:S(2)}, u32[]{:S(2)}) collective-permute-start(bf16[128,256]{1,0:T(8,128)(2,1)S(1)} %slice_bitcast_fusion), channel_id=1, source_target_pairs={{0,3},{1,0},{2,1},{3,2},{4,7},{5,4},{6,5},{7,6},{8,11},{9,8},{10,9... | collective-permute-start | bytes 196616 | tf_op jit(solution)/shard_map/ppermute | solution.py:427
  91.0 2.1 %collective-permute-done.23.refs_1_ = bf16[128,256]{1,0:T(8,128)(2,1)S(1)} collective-permute-done((bf16[128,256]{1,0:T(8,128)(2,1)S(1)}, bf16[128,256]{1,0:T(8,128)(2,1)S(1)}, u32[]{:S(2)}, u32[]{:S(2)}) %collective-permute-start.23) | collective-permute-done | bytes 65568 | tf_op jit(solution)/shard_map/ppermute | solution.py:427
  (70 shorter events, 22.3 us)
Async XLA Ops:
  1.6 17.0 %collective-permute-start = (bf16[512,512]{1,0:T(8,128)(2,1)S(1)}, bf16[512,512]{1,0:T(8,128)(2,1)S(1)}, u32[]{:S(2)}, u32[]{:S(2)}) collective-permute-start(bf16[512,512]{1,0:T(8,128)(2,1)S(1)} %constant_dynamic-slice_fusion.refs_4_), channel_id=1, source_target_pairs={{0,1},{1,2},{2,3},{3,0},{4,5},{5,6},{6,7},{7,4},{8,9},{9,10},{10,1... | collective-permute-start | bytes 1572872 | tf_op jit(solution)/shard_map/ppermute | solution.py:427
  4.7 14.0 %collective-permute-start.2 = (bf16[512,512]{1,0:T(8,128)(2,1)S(1)}, bf16[512,512]{1,0:T(8,128)(2,1)}, u32[]{:S(2)}, u32[]{:S(2)}) collective-permute-start(bf16[512,512]{1,0:T(8,128)(2,1)S(1)} %constant_dynamic-slice_fusion.refs_4_), channel_id=1, source_target_pairs={{0,16},{16,0},{1,17},{17,1},{2,18},{18,2},{3,19},{19,3},{4,20},{20... | collective-permute-start | bytes 1572872 | tf_op jit(solution)/shard_map/ppermute | solution.py:434
  6.2 27.3 %collective-permute-start.1 = (bf16[128,4096]{1,0:T(8,128)(2,1)}, bf16[128,4096]{1,0:T(8,128)(2,1)}, u32[]{:S(2)}, u32[]{:S(2)}) collective-permute-start(bf16[128,4096]{1,0:T(8,128)(2,1)} %bitcast.28), channel_id=1, source_target_pairs={{0,8},{8,0},{1,9},{9,1},{2,10},{10,2},{3,11},{11,3},{4,12},{12,4},... | collective-permute-start | bytes 3145736 | tf_op jit(solution)/shard_map/ppermute | solution.py:200
  18.7 14.9 %collective-permute-start.3 = (bf16[512,512]{1,0:T(8,128)(2,1)S(1)}, bf16[512,512]{1,0:T(8,128)(2,1)S(1)}, u32[]{:S(2)}, u32[]{:S(2)}) collective-permute-start(bf16[512,512]{1,0:T(8,128)(2,1)S(1)} %collective-permute-done.refs_6_), channel_id=1, source_target_pairs={{0,1},{1,2},{2,3},{3,0},{4,5},{5,6},{6,7},{7,4},{8,9},{9,10},{10,1... | collective-permute-start | bytes 1572872 | tf_op jit(solution)/shard_map/ppermute | solution.py:427
  19.8 13.8 %collective-permute-start.4 = (bf16[512,512]{1,0:T(8,128)(2,1)S(1)}, bf16[512,512]{1,0:T(8,128)(2,1)S(1)}, u32[]{:S(2)}, u32[]{:S(2)}) collective-permute-start(bf16[512,512]{1,0:T(8,128)(2,1)S(1)} %collective-permute-done.refs_6_), channel_id=1, source_target_pairs={{0,16},{16,0},{1,17},{17,1},{2,18},{18,2},{3,19},{19,3},{4,20},{20... | collective-permute-start | bytes 1572872 | tf_op jit(solution)/shard_map/ppermute | solution.py:434
  21.3 29.6 %collective-permute-start.9 = (bf16[128,4096]{1,0:T(8,128)(2,1)}, bf16[128,4096]{1,0:T(8,128)(2,1)S(1)}, u32[]{:S(2)}, u32[]{:S(2)}) collective-permute-start(bf16[128,4096]{1,0:T(8,128)(2,1)} %bitcast.29), channel_id=1, source_target_pairs={{0,4},{4,0},{1,5},{5,1},{2,6},{6,2},{3,7},{7,3},{8,12},{12,8},{9,1... | collective-permute-start | bytes 3145736 | tf_op jit(solution)/shard_map/ppermute | solution.py:200
  33.6 14.0 %collective-permute-start.5 = (bf16[512,512]{1,0:T(8,128)(2,1)S(1)}, bf16[512,512]{1,0:T(8,128)(2,1)S(1)}, u32[]{:S(2)}, u32[]{:S(2)}) collective-permute-start(bf16[512,512]{1,0:T(8,128)(2,1)S(1)} %collective-permute-done.3.refs_8_), channel_id=1, source_target_pairs={{0,1},{1,2},{2,3},{3,0},{4,5},{5,6},{6,7},{7,4},{8,9},{9,10},{10,1... | collective-permute-start | bytes 1572872 | tf_op jit(solution)/shard_map/ppermute | solution.py:427
  33.6 14.0 %collective-permute-start.6 = (bf16[512,512]{1,0:T(8,128)(2,1)S(1)}, bf16[512,512]{1,0:T(8,128)(2,1)S(1)}, u32[]{:S(2)}, u32[]{:S(2)}) collective-permute-start(bf16[512,512]{1,0:T(8,128)(2,1)S(1)} %collective-permute-done.3.refs_8_), channel_id=1, source_target_pairs={{0,16},{16,0},{1,17},{17,1},{2,18},{18,2},{3,19},{19,3},{4,20},{20... | collective-permute-start | bytes 1572872 | tf_op jit(solution)/shard_map/ppermute | solution.py:434
  35.1 17.4 %collective-permute-start.10 = (bf16[128,4096]{1,0:T(8,128)(2,1)}, bf16[128,4096]{1,0:T(8,128)(2,1)S(1)}, u32[]{:S(2)}, u32[]{:S(2)}) collective-permute-start(bf16[128,4096]{1,0:T(8,128)(2,1)} %collective-permute-done.1.refs_2_), channel_id=1, source_target_pairs={{0,4},{4,0},{1,5},{5,1},{2,6},{6,2},{3,7},{7,3},{8,12},{12,8},{9,1... | collective-permute-start | bytes 3145736 | tf_op jit(solution)/shard_map/ppermute | solution.py:200
  35.1 8.9 %collective-permute-start.7 = (bf16[4,128,256]{2,1,0:T(8,128)(2,1)}, bf16[4,128,256]{2,1,0:T(8,128)(2,1)S(1)}, u32[]{:S(2)}, u32[]{:S(2)}) collective-permute-start(bf16[4,128,256]{2,1,0:T(8,128)(2,1)} %copy-done.4), channel_id=1, source_target_pairs={{0,8},{8,0},{1,9},{9,1},{2,10},{10,2},{3,11},{11,3},{4,12},{12,4},... | collective-permute-start | bytes 786440 | tf_op jit(solution)/shard_map/ppermute | solution.py:200
  47.6 11.3 %collective-permute-start.8 = (bf16[512,512]{1,0:T(8,128)(2,1)S(1)}, bf16[512,512]{1,0:T(8,128)(2,1)S(1)}, u32[]{:S(2)}, u32[]{:S(2)}) collective-permute-start(bf16[512,512]{1,0:T(8,128)(2,1)S(1)} %collective-permute-done.5.refs_10_), channel_id=1, source_target_pairs={{0,16},{16,0},{1,17},{17,1},{2,18},{18,2},{3,19},{19,3},{4,20},{20... | collective-permute-start | bytes 1572872 | tf_op jit(solution)/shard_map/ppermute | solution.py:434
  48.6 11.6 %collective-permute-start.11 = (bf16[2,128,256]{2,1,0:T(8,128)(2,1)S(1)}, bf16[2,128,256]{2,1,0:T(8,128)(2,1)S(1)}, u32[]{:S(2)}, u32[]{:S(2)}) collective-permute-start(bf16[2,128,256]{2,1,0:T(8,128)(2,1)S(1)} %get-tuple-element.92), channel_id=1, source_target_pairs={{0,1},{1,2},{2,3},{3,0},{4,5},{5,6},{6,7},{7,4},{8,9},{9,10},{10,1... | collective-permute-start | bytes 393224 | tf_op jit(solution)/shard_map/ppermute | solution.py:427
  48.6 11.7 %collective-permute-start.12 = (bf16[2,128,256]{2,1,0:T(8,128)(2,1)S(1)}, bf16[2,128,256]{2,1,0:T(8,128)(2,1)S(1)}, u32[]{:S(2)}, u32[]{:S(2)}) collective-permute-start(bf16[2,128,256]{2,1,0:T(8,128)(2,1)S(1)} %get-tuple-element.93), channel_id=1, source_target_pairs={{0,2},{1,3},{2,0},{3,1},{4,6},{5,7},{6,4},{7,5},{8,10},{9,11},{10,... | collective-permute-start | bytes 393224 | tf_op jit(solution)/shard_map/ppermute | solution.py:427
  50.9 9.4 %collective-permute-start.13 = (bf16[2,128,256]{2,1,0:T(8,128)(2,1)S(1)}, bf16[2,128,256]{2,1,0:T(8,128)(2,1)S(1)}, u32[]{:S(2)}, u32[]{:S(2)}) collective-permute-start(bf16[2,128,256]{2,1,0:T(8,128)(2,1)S(1)} %get-tuple-element.94), channel_id=1, source_target_pairs={{0,3},{1,0},{2,1},{3,2},{4,7},{5,4},{6,5},{7,6},{8,11},{9,8},{10,9... | collective-permute-start | bytes 393224 | tf_op jit(solution)/shard_map/ppermute | solution.py:427
  60.3 7.0 %collective-permute-start.14 = (bf16[512,128]{1,0:T(8,128)(2,1)S(1)}, bf16[512,128]{1,0:T(8,128)(2,1)S(1)}, u32[]{:S(2)}, u32[]{:S(2)}) collective-permute-start(bf16[512,128]{1,0:T(8,128)(2,1)S(1)} %get-tuple-element.96), channel_id=1, source_target_pairs={{0,1},{1,2},{2,3},{3,0},{4,5},{5,6},{6,7},{7,4},{8,9},{9,10},{10,1... | collective-permute-start | bytes 393224 | tf_op jit(solution)/shard_map/ppermute | solution.py:427
  60.9 10.2 %collective-permute-start.15 = (bf16[512,128]{1,0:T(8,128)(2,1)S(1)}, bf16[512,128]{1,0:T(8,128)(2,1)S(1)}, u32[]{:S(2)}, u32[]{:S(2)}) collective-permute-start(bf16[512,128]{1,0:T(8,128)(2,1)S(1)} %get-tuple-element.97), channel_id=1, source_target_pairs={{0,2},{1,3},{2,0},{3,1},{4,6},{5,7},{6,4},{7,5},{8,10},{9,11},{10,... | collective-permute-start | bytes 393224 | tf_op jit(solution)/shard_map/ppermute | solution.py:427
  63.3 7.7 %collective-permute-start.16 = (bf16[512,128]{1,0:T(8,128)(2,1)S(1)}, bf16[512,128]{1,0:T(8,128)(2,1)S(1)}, u32[]{:S(2)}, u32[]{:S(2)}) collective-permute-start(bf16[512,128]{1,0:T(8,128)(2,1)S(1)} %get-tuple-element.98), channel_id=1, source_target_pairs={{0,3},{1,0},{2,1},{3,2},{4,7},{5,4},{6,5},{7,6},{8,11},{9,8},{10,9... | collective-permute-start | bytes 393224 | tf_op jit(solution)/shard_map/ppermute | solution.py:427
  64.2 7.4 %collective-permute-start.17 = (bf16[512,128]{1,0:T(8,128)(2,1)S(1)}, bf16[512,128]{1,0:T(8,128)(2,1)S(1)}, u32[]{:S(2)}, u32[]{:S(2)}) collective-permute-start(bf16[512,128]{1,0:T(8,128)(2,1)S(1)} %get-tuple-element.95.refs_0_), channel_id=1, source_target_pairs={{0,4},{4,0},{1,5},{5,1},{2,6},{6,2},{3,7},{7,3},{8,12},{12,8},{9,1... | collective-permute-start | bytes 393224 | tf_op jit(solution)/shard_map/ppermute | solution.py:200
  78.1 7.2 %collective-permute-start.24 = (bf16[2,128,256]{2,1,0:T(8,128)(2,1)S(1)}, bf16[2,128,256]{2,1,0:T(8,128)(2,1)S(1)}, u32[]{:S(2)}, u32[]{:S(2)}) collective-permute-start(bf16[2,128,256]{2,1,0:T(8,128)(2,1)S(1)} %get-tuple-element.104), channel_id=1, source_target_pairs={{0,8},{8,0},{1,9},{9,1},{2,10},{10,2},{3,11},{11,3},{4,12},{12,4},... | collective-permute-start | bytes 393224 | tf_op jit(solution)/shard_map/ppermute | solution.py:200
  78.8 8.1 %collective-permute-start.26 = (bf16[128,256]{1,0:T(8,128)(2,1)S(1)}, bf16[128,256]{1,0:T(8,128)(2,1)S(1)}, u32[]{:S(2)}, u32[]{:S(2)}) collective-permute-start(bf16[128,256]{1,0:T(8,128)(2,1)S(1)} %get-tuple-element.106), channel_id=1, source_target_pairs={{0,1},{1,2},{2,3},{3,0},{4,5},{5,6},{6,7},{7,4},{8,9},{9,10},{10,1... | collective-permute-start | bytes 196616 | tf_op jit(solution)/shard_map/ppermute | solution.py:427
  80.9 8.8 %collective-permute-start.27 = (bf16[128,256]{1,0:T(8,128)(2,1)S(1)}, bf16[128,256]{1,0:T(8,128)(2,1)S(1)}, u32[]{:S(2)}, u32[]{:S(2)}) collective-permute-start(bf16[128,256]{1,0:T(8,128)(2,1)S(1)} %get-tuple-element.107), channel_id=1, source_target_pairs={{0,2},{1,3},{2,0},{3,1},{4,6},{5,7},{6,4},{7,5},{8,10},{9,11},{10,... | collective-permute-start | bytes 196616 | tf_op jit(solution)/shard_map/ppermute | solution.py:427
  82.5 7.1 %collective-permute-start.28 = (bf16[128,256]{1,0:T(8,128)(2,1)S(1)}, bf16[128,256]{1,0:T(8,128)(2,1)S(1)}, u32[]{:S(2)}, u32[]{:S(2)}) collective-permute-start(bf16[128,256]{1,0:T(8,128)(2,1)S(1)} %get-tuple-element.108), channel_id=1, source_target_pairs={{0,3},{1,0},{2,1},{3,2},{4,7},{5,4},{6,5},{7,6},{8,11},{9,8},{10,9... | collective-permute-start | bytes 196616 | tf_op jit(solution)/shard_map/ppermute | solution.py:427
  83.3 7.7 %collective-permute-start.22 = (bf16[128,256]{1,0:T(8,128)(2,1)S(1)}, bf16[128,256]{1,0:T(8,128)(2,1)S(1)}, u32[]{:S(2)}, u32[]{:S(2)}) collective-permute-start(bf16[128,256]{1,0:T(8,128)(2,1)S(1)} %get-tuple-element.110), channel_id=1, source_target_pairs={{0,1},{1,2},{2,3},{3,0},{4,5},{5,6},{6,7},{7,4},{8,9},{9,10},{10,1... | collective-permute-start | bytes 196616 | tf_op jit(solution)/shard_map/ppermute | solution.py:427
  85.3 7.7 %collective-permute-start.23 = (bf16[128,256]{1,0:T(8,128)(2,1)S(1)}, bf16[128,256]{1,0:T(8,128)(2,1)S(1)}, u32[]{:S(2)}, u32[]{:S(2)}) collective-permute-start(bf16[128,256]{1,0:T(8,128)(2,1)S(1)} %get-tuple-element.109), channel_id=1, source_target_pairs={{0,2},{1,3},{2,0},{3,1},{4,6},{5,7},{6,4},{7,5},{8,10},{9,11},{10,... | collective-permute-start | bytes 196616 | tf_op jit(solution)/shard_map/ppermute | solution.py:427
  (13 other events, 85.1 us)
